TPU v7x, 32 devices: a whole 2x2x4 slice. The times are simulated.
32 devices in a mesh: grp: 2 (over y), ep: 8 (over z, x), seq: 1, rep: 2 (over core).
Axes of the slice: x: 2, y: 2, z: 4, core: 2. Of those that a mesh axis runs over, the one named last changes fastest.
Arguments:
- hidden_in: bfloat16 [1024, 2048], P(('grp', 'ep', 'rep'), 'seq'), parts along dimension 0, may hold values from -64 to 64
- row_counts: int32 [32], P(('grp', 'ep', 'rep')), parts along dimension 0, may hold values from 24 to 32, as said below
- qkv_new: bfloat16 [1024, 3, 2048], P(('grp', 'ep', 'rep')), parts along dimension 0, may hold values from -6 to 6
- cache_len: int32 [16, 64], P('grp', ('rep', 'seq')), parts along dimension 0, may hold values from 1 to 128, as said below
- kv_cache: bfloat16 [2, 16, 64, 128, 2048], P(None, 'grp', ('rep', 'seq'), None, 'ep'), parts along dimension 1, may hold values from -128 to 128
- w_out: bfloat16 [2048, 2048], P('ep', 'seq'), may hold values from -0.125 to 0.125
- moe_gain: float32 [2048], replicated, may hold values from 0.1 to 1.9
- w_in: bfloat16 [16, 2048, 2, 1408], P(('ep', 'rep'), None, None, 'seq'), may hold values from -0.125 to 0.125
- w_down: bfloat16 [16, 1408, 2048], P(('ep', 'rep'), 'seq'), may hold values from -0.15625 to 0.15625
- route_ids: int32 [1024, 6], P(('grp', 'ep', 'rep')), parts along dimension 0, may hold values from 0 to 15, all different within a row; in each aligned block of 32 rows (0 to 31, 32 to 63, ...) at most 24 rows name the same one
- route_weight: bfloat16 [1024, 6], P(('grp', 'ep', 'rep')), parts along dimension 0, may hold values from 0.049804688 to 0.44921875
Outputs:
- mixed: bfloat16 [1024, 2048], P(('grp', 'ep', 'rep'), 'seq'), parts along dimension 0
There are 2 independent parts, one for each index of `grp`. A program takes and returns all parts, laid end to end along the dimension named above; an argument that names none is the same for every part. Nothing has to cross between parts.
Inputs may be any that keep to these rules, and one draw needn't show every extreme that they name: The first row_counts[b] slots of block b are live; some block is full. `cache_len`: some row has 128 cached positions. `route_ids`: a row's 6 experts differ; among the 32 rows of one block no expert is named by more than 24 rows, and in some block one is named by exactly 24.
All inputs are finite; a program needn't handle non-finite values.
Results may differ from a plain program's by a relative error of at most 0.0053.
Values may be sent and summed in bfloat16 or wider, within the bound.
No kernel may reach another device: no remote copies, remote signals or barrier semaphores. Data moves between devices by JAX's collectives and lax.ppermute only.
A program may use at most 192 MiB of HBM per device.

v0:
```python
import math

import jax
import jax.numpy as jnp
from jax import lax
from jax.sharding import PartitionSpec as P

D = 2048
HEAD_DIM = 128
TOPK = 6


epsilon = 1e-06
masked_score = -1e30


def local(
    hidden_in,
    row_counts,
    qkv_new,
    cache_len,
    kv_cache,
    w_out,
    moe_gain,
    w_in,
    w_down,
    route_ids,
    route_weight,
):
    tok_rows, feat_local = hidden_in.shape
    owners = lax.axis_size("ep")
    parts_seq = lax.axis_size("seq")
    width_local = kv_cache.shape[-1]
    heads_local = width_local // HEAD_DIM
    positions = kv_cache.shape[3]
    share_rows = tok_rows // parts_seq
    attend_rows = owners * share_rows
    moved_block = lax.all_to_all(qkv_new, "ep", split_axis=2, concat_axis=0, tiled=True)
    moved_block = moved_block.reshape(owners, tok_rows, 3, width_local)
    heads_block = lax.dynamic_slice_in_dim(
        moved_block, lax.axis_index("seq") * share_rows, share_rows, 1
    )
    heads_block = heads_block.reshape(attend_rows, 3, heads_local, HEAD_DIM)
    queries = heads_block[:, 0]
    key_new = heads_block[:, 1].astype(jnp.float32)
    value_new = heads_block[:, 2].astype(jnp.float32)
    lengths = cache_len.reshape(attend_rows)
    cache_keys = kv_cache[0].reshape(attend_rows, positions, heads_local, HEAD_DIM)
    cache_values = kv_cache[1].reshape(attend_rows, positions, heads_local, HEAD_DIM)
    score_scale = 1.0 / math.sqrt(HEAD_DIM)
    position = jnp.arange(positions, dtype=jnp.int32)
    in_cache = position[None, None, :] < lengths[:, None, None]
    scores = (
        jnp.einsum("nhd,nphd->nhp", queries, cache_keys, preferred_element_type=jnp.float32)
        * score_scale
    )
    scores = jnp.where(in_cache, scores, masked_score)
    own_score = jnp.sum(queries.astype(jnp.float32) * key_new, axis=2) * score_scale
    highest = jnp.maximum(jnp.max(scores, axis=2), own_score)
    weights = jnp.where(in_cache, jnp.exp(scores - highest[..., None]), 0.0)
    partial_sum = jnp.einsum(
        "nhp,nphd->nhd",
        weights.astype(jnp.bfloat16),
        cache_values,
        preferred_element_type=jnp.float32,
    )
    own_weight = jnp.exp(own_score - highest)
    attended = (partial_sum + own_weight[..., None] * value_new) / (
        jnp.sum(weights, axis=2) + own_weight
    )[..., None]
    attended = attended.astype(jnp.bfloat16).reshape(owners, share_rows, width_local)
    attended = lax.all_gather(attended, "seq", axis=1, tiled=True).reshape(
        owners * tok_rows, width_local
    )
    attn_out = lax.psum_scatter(
        jnp.dot(attended, w_out, preferred_element_type=jnp.float32),
        "ep",
        scatter_dimension=0,
        tiled=True,
    )
    residual = (hidden_in.astype(jnp.float32) + attn_out).astype(jnp.bfloat16)
    residual_wide = lax.optimization_barrier(residual).astype(jnp.float32)
    is_live = jnp.arange(tok_rows, dtype=jnp.int32) < row_counts[0]
    expert_total = lax.axis_size(("ep", "rep")) * w_in.shape[0]
    capacity = min(tok_rows, max(2, 2 * tok_rows * TOPK // expert_total))
    pair_count = tok_rows * TOPK
    flat_ids = route_ids.reshape(pair_count)
    pair_hits = (
        flat_ids[:, None] == jnp.arange(expert_total, dtype=jnp.int32)[None, :]
    ) & jnp.repeat(is_live, TOPK)[:, None]
    hit_counts = pair_hits.astype(jnp.int32)
    earlier_hits = jnp.cumsum(hit_counts, axis=0) - hit_counts
    slot_index = jnp.sum(earlier_hits * hit_counts, axis=1)
    target_cell = jnp.where(
        jnp.any(pair_hits, axis=1), flat_ids * capacity + slot_index, -1
    ).reshape(tok_rows, TOPK)
    cell_index = jnp.arange(expert_total * capacity, dtype=jnp.int32)
    cell_hits = target_cell[None, :, :] == cell_index[:, None, None]
    dispatch_rows = jnp.any(cell_hits, axis=2).astype(jnp.bfloat16)
    combine_rows = jnp.sum(
        jnp.where(cell_hits, route_weight.astype(jnp.float32)[None], 0.0), axis=2
    ).astype(jnp.bfloat16)
    full_rows = lax.all_gather(residual, "seq", axis=1, tiled=True)
    rows_wide = full_rows.astype(jnp.float32)
    inverse_rms = lax.rsqrt(jnp.mean(rows_wide * rows_wide, axis=1) + epsilon)
    normed = (rows_wide * inverse_rms[:, None] * moe_gain).astype(jnp.bfloat16)
    outgoing = jnp.dot(dispatch_rows, normed, preferred_element_type=jnp.float32).astype(
        jnp.bfloat16
    )
    outgoing = outgoing.reshape(expert_total, capacity, D)
    arrived = lax.all_to_all(outgoing, ("ep", "rep"), split_axis=0, concat_axis=0, tiled=True)
    sources, slot_count, feature_count = arrived.shape
    flat_rows = arrived.reshape(sources * slot_count, D)
    gate_up = jnp.dot(flat_rows, w_in.reshape(D, -1), preferred_element_type=jnp.float32).reshape(
        sources * slot_count, 2, -1
    )
    hidden_units = (jax.nn.silu(gate_up[:, 0]) * gate_up[:, 1]).astype(jnp.bfloat16)
    down_part = jnp.dot(
        hidden_units, w_down.reshape(-1, D), preferred_element_type=jnp.float32
    ).reshape(sources, slot_count, D)
    summed = lax.psum_scatter(down_part, "seq", scatter_dimension=2, tiled=True).astype(
        jnp.bfloat16
    )
    returned = lax.all_to_all(summed, ("ep", "rep"), split_axis=0, concat_axis=0, tiled=True)
    returned = returned.reshape(expert_total * capacity, feat_local)
    moe_out = lax.dot_general(
        combine_rows, returned, (((0,), (0,)), ((), ())), preferred_element_type=jnp.float32
    )
    mixed = jnp.where(is_live[:, None], residual_wide + moe_out, 0.0).astype(jnp.bfloat16)
    return mixed


def solution(mesh):
    placed = (
        P(("grp", "ep", "rep"), "seq"),
        P(("grp", "ep", "rep")),
        P(("grp", "ep", "rep"), None, None),
        P("grp", ("rep", "seq")),
        P(None, "grp", ("rep", "seq"), None, "ep"),
        P("ep", "seq"),
        P(),
        P(("ep", "rep"), None, None, "seq"),
        P(("ep", "rep"), "seq", None),
        P(("grp", "ep", "rep"), None),
        P(("grp", "ep", "rep"), None),
    )
    return jax.shard_map(
        local, mesh=mesh, in_specs=placed, out_specs=P(("grp", "ep", "rep"), "seq"), check_vma=False
    )
```

profile of v0, /device:TPU:0, one launch (start us, length us, event | category | flops | bytes accessed | tf_op | source)
XLA Modules:
  0.0 283.7 jit_solution(12234026153400670893)
XLA Ops:
  6.5 2.9 %copy.41 = bf16[32,3,2048]{0,1,2:T(4,128)(2,1)S(1)} copy(bf16[32,3,2048]{2,0,1:T(8,128)(2,1)} %param.13) | data formatting | bytes 786432 | tf_op args[2]
  9.4 2.5 reshape.133
  11.9 7.3 %all-to-all-start = ((bf16[8,2,12288]{2,1,0:T(2,128)(2,1)}), bf16[8,2,12288]{2,1,0:T(2,128)(2,1)S(1)}, u32[]{:S(2)}, u32[]{:S(2)}) async-start(bf16[8,2,12288]{2,1,0:T(2,128)(2,1)} %reshape.133), calls=%async_computation | async-start | bytes 786432 | tf_op jit(solution)/shard_map/all_to_all | solution.py:38
  19.2 23.1 %fusion.39 = (bf16[1,8,32,128,256]{4,3,2,1,0:T(8,128)(2,1)}, bf16[1,8,32,128,256]{4,3,2,1,0:T(8,128)(2,1)}) fusion(bf16[2,8,32,128,256]{4,3,2,1,0:T(8,128)(2,1)} %param.15), kind=kLoop, calls=%fused_computation.65 | loop fusion | bytes 67108864 | tf_op jit(solution)/shard_map/slice | solution.py:48
  42.3 23.7 %reshape_squeeze.7 = bf16[256,128,2,128]{3,2,1,0:T(2,128)(2,1)} reshape(bf16[1,8,32,128,256]{4,3,2,1,0:T(8,128)(2,1)} %get-tuple-element.10) | data formatting | bytes 33554432 | tf_op jit(solution)/shard_map/reshape;squeeze | solution.py:49
  66.0 21.2 %copy.58 = bf16[1,8,32,128,256]{3,4,2,1,0:T(8,128)(2,1)} copy(bf16[1,8,32,128,256]{4,3,2,1,0:T(8,128)(2,1)} %get-tuple-element.9) | data formatting | bytes 33554432 | tf_op jit(solution)/shard_map/reshape;squeeze | solution.py:48
  87.3 0.7 iota_compare_fusion.1
  88.0 1.3 reshape.134
  89.4 1.0 copy.42
  90.6 0.3 fusion.16
  91.0 8.1 %fusion.19 = f32[256,2,1,128]{3,2,1,0:T(1,128)S(1)} fusion(bf16[256,128,2,128]{1,3,2,0:T(8,128)(2,1)} %bitcast.85, bf16[256,2,128,1]{2,1,0,3:T(2,128)(2,1)S(1)} %slice_bitcast_fusion.2), kind=kOutput, calls=%fused_computation.27 | convolution fusion | flops 16777216 | bytes 17170432 | tf_op jit(solution)/shard_map/nhd,nphd->nhp/dot_general | solution.py:54
  99.1 0.2 fusion.24
  99.3 0.3 fusion.22
  99.6 0.1 copy.45
  99.8 9.0 %fusion = f32[256,2,1,128]{3,2,1,0:T(1,128)S(1)} fusion(bf16[256,128,2,128]{3,2,1,0:T(2,128)(2,1)} %reshape_squeeze.7, bf16[256,2,128,1]{2,0,1,3:T(8,128)(2,1)S(1)} %get-tuple-element.12), kind=kOutput, calls=%fused_computation | convolution fusion | flops 16777216 | bytes 17170432 | tf_op jit(solution)/shard_map/nhp,nphd->nhd/dot_general | solution.py:61
  108.8 0.7 fusion.21
  109.6 1.8 fusion.27
  112.6 0.6 reduce-window.6
  113.2 0.2 slice_reduce_fusion
  113.9 67.2 %reduce-scatter.2.cloned.1.call-done = f32[32,2048]{1,0:T(8,128)} async-done(((f32[256,2048]{1,0:T(8,128)}), f32[32,2048]{1,0:T(8,128)}) %reduce-scatter.2.cloned.1.call-update) | async-done | bytes 262160 | tf_op jit(solution)/shard_map/reduce_scatter | solution.py:75
  181.0 1.1 fusion.11
  182.2 1.8 convolution_convert_fusion
  183.9 3.9 %all-to-all-start.1 = ((bf16[16,24,2048]{2,1,0:T(8,128)(2,1)}), bf16[16,24,2048]{2,1,0:T(8,128)(2,1)S(1)}, u32[]{:S(2)}, u32[]{:S(2)}) async-start(bf16[16,24,2048]{2,1,0:T(8,128)(2,1)} %bitcast.13), calls=%async_computation.2 | async-start | bytes 3145728 | tf_op jit(solution)/shard_map/all_to_all | solution.py:111
  187.8 11.3 %copy.62 = bf16[256,8,2,1408]{3,1,2,0:T(8,128)(2,1)} copy(bf16[256,8,2,1408]{3,2,1,0:T(2,128)(2,1)} %bitcast.87) | data formatting | bytes 23068672
  199.1 15.1 %copy.51 = bf16[2816,2048]{1,0:T(8,128)(2,1)} copy(bf16[2816,2048]{0,1:T(8,128)(2,1)} %bitcast.86) | data formatting | bytes 23068672 | tf_op jit(solution)/shard_map/dot_general | solution.py:114
  214.2 5.4 %all-to-all-done.1 = bf16[16,24,2048]{2,1,0:T(8,128)(2,1)S(1)} async-done(((bf16[16,24,2048]{2,1,0:T(8,128)(2,1)}), bf16[16,24,2048]{2,1,0:T(8,128)(2,1)S(1)}, u32[]{:S(2)}, u32[]{:S(2)}) %all-to-all-start.1) | async-done | bytes 1572896 | tf_op jit(solution)/shard_map/all_to_all | solution.py:111
  219.6 7.9 %fusion.40 = f32[384,2,1408]{2,0,1:T(8,128)S(1)} fusion(bf16[384,2048,1]{1,0,2:T(8,128)(2,1)S(1)} %bitcast.92, bf16[2,1408,2048]{2,1,0:T(8,128)(2,1)} %bitcast.88), kind=kOutput, calls=%fused_computation.66 | convolution fusion | flops 4429185024 | bytes 17432576 | tf_op jit(solution)/shard_map/dot_general | solution.py:114
  227.6 0.6 fusion.9
  228.2 6.4 %fusion.4 = bf16[16,24,2048]{2,1,0:T(8,128)(2,1)} fusion(bf16[16,24,1408]{2,1,0:T(8,128)(2,1)S(1)} %bitcast.94, bf16[1,1408,2048]{2,1,0:T(8,128)(2,1)} %param.19), kind=kOutput, calls=%fused_computation.4 | convolution fusion | flops 2215378944 | bytes 8421376 | tf_op jit(solution)/shard_map/dot_general | solution.py:118
  234.6 9.2 %all-to-all-start.2 = ((bf16[16,24,2048]{2,1,0:T(8,128)(2,1)}), bf16[16,24,2048]{2,1,0:T(8,128)(2,1)S(1)}, u32[]{:S(2)}, u32[]{:S(2)}) async-start(bf16[16,24,2048]{2,1,0:T(8,128)(2,1)} %fusion.4), calls=%async_computation.3 | async-start | bytes 3145728 | tf_op jit(solution)/shard_map/all_to_all | solution.py:124
  244.0 31.8 %all-to-all-done.2 = bf16[16,24,2048]{2,1,0:T(8,128)(2,1)S(1)} async-done(((bf16[16,24,2048]{2,1,0:T(8,128)(2,1)}), bf16[16,24,2048]{2,1,0:T(8,128)(2,1)S(1)}, u32[]{:S(2)}, u32[]{:S(2)}) %all-to-all-start.2) | async-done | bytes 1572896 | tf_op jit(solution)/shard_map/all_to_all | solution.py:124
  275.8 1.0 fusion.8
  (44 shorter events, 1.7 us)
Async XLA Ops:
  6.5 103.0 %copy-start = (bf16[256,2048]{1,0:T(8,128)(2,1)S(1)}, bf16[256,2048]{1,0:T(8,128)(2,1)}, u32[]{:S(2)}) copy-start(bf16[256,2048]{1,0:T(8,128)(2,1)} %param.16) | copy-start | bytes 3145732
  11.9 76.2 %all-to-all-start = ((bf16[8,2,12288]{2,1,0:T(2,128)(2,1)}), bf16[8,2,12288]{2,1,0:T(2,128)(2,1)S(1)}, u32[]{:S(2)}, u32[]{:S(2)}) async-start(bf16[8,2,12288]{2,1,0:T(2,128)(2,1)} %reshape.133), calls=%async_computation | async-start | bytes 786432 | tf_op jit(solution)/shard_map/all_to_all | solution.py:38
  19.1 161.9 %reduce-scatter.2.cloned.1.call-start = ((), (), s32[]{:S(2)}) async-start(), calls=%async_computation.4 | async-start | bytes 2359296 | tf_op jit(solution)/shard_map/reduce_scatter | solution.py:75
  66.0 21.2 %copy-start.5 = (s32[8,32]{1,0:T(8,128)S(1)}, s32[8,32]{1,0:T(8,128)}, u32[]{:S(2)}) copy-start(s32[8,32]{1,0:T(8,128)} %param.14) | copy-start | bytes 3076
  91.0 8.1 %copy-start.1 = (pred[256,128]{1,0:T(8,128)(4,1)S(1)}, pred[256,128]{1,0:T(8,128)(4,1)}, u32[]{:S(2)}) copy-start(pred[256,128]{1,0:T(8,128)(4,1)} %iota_compare_fusion.1) | copy-start | bytes 98308
  108.8 2.6 copy-start.4
  108.8 72.2 %copy-start.2 = (bf16[32,2048]{1,0:T(8,128)(2,1)S(1)}, bf16[32,2048]{1,0:T(8,128)(2,1)}, u32[]{:S(2)}) copy-start(bf16[32,2048]{1,0:T(8,128)(2,1)} %param.11) | copy-start | bytes 393220
  109.5 72.6 %copy-start.3 = (f32[2048]{0:T(1024)S(1)}, f32[2048]{0:T(1024)}, u32[]{:S(2)}) copy-start(f32[2048]{0:T(1024)} %param.17) | copy-start | bytes 24580
  183.9 35.7 %all-to-all-start.1 = ((bf16[16,24,2048]{2,1,0:T(8,128)(2,1)}), bf16[16,24,2048]{2,1,0:T(8,128)(2,1)S(1)}, u32[]{:S(2)}, u32[]{:S(2)}) async-start(bf16[16,24,2048]{2,1,0:T(8,128)(2,1)} %bitcast.13), calls=%async_computation.2 | async-start | bytes 3145728 | tf_op jit(solution)/shard_map/all_to_all | solution.py:111
  234.6 9.2 %copy-start.6 = (bf16[32,6]{0,1:T(8,128)(2,1)S(1)}, bf16[32,6]{0,1:T(8,128)(2,1)}, u32[]{:S(2)}) copy-start(bf16[32,6]{0,1:T(8,128)(2,1)} %param.21) | copy-start | bytes 1156
  234.6 41.2 %all-to-all-start.2 = ((bf16[16,24,2048]{2,1,0:T(8,128)(2,1)}), bf16[16,24,2048]{2,1,0:T(8,128)(2,1)S(1)}, u32[]{:S(2)}, u32[]{:S(2)}) async-start(bf16[16,24,2048]{2,1,0:T(8,128)(2,1)} %fusion.4), calls=%async_computation.3 | async-start | bytes 3145728 | tf_op jit(solution)/shard_map/all_to_all | solution.py:124
Sparse Core Ops, SparseCore 0:
  111.5 69.4 reduce-scatter.1
where the time goes:
time: 289 us; the launch traced here: 284 us
  local copies, waits for them, and re-layouts  104 us (36%)
  waiting for transfers between devices  104 us (36%)
  matrix products  35.9 us (12%)
  starting transfers between devices  20.4 us (7%)
  between operations  14.3 us (5%)
  other arithmetic  4.97 us (2%)
    reduce_scatter x1, waiting for transfers between devices, local(): lax.psum_scatter(jnp.dot(attended, w_out, preferred_element_type=jnp.floa...  67.2 us
    all_to_all x1, waiting for transfers between devices, local(): lax.all_to_all(summed, ('ep', 'rep'), split_axis=0, concat_axis=0, tiled=...  31.8 us
    another operation x1, local copies, waits for them, and re-layouts, local(): kv_cache[1].reshape(attend_rows, positions, heads_local, HEAD_DIM)  23.7 us
    slice x1, local copies, waits for them, and re-layouts, local(): kv_cache[0].reshape(attend_rows, positions, heads_local, HEAD_DIM)  23.1 us
    another operation x1, local copies, waits for them, and re-layouts, local(): kv_cache[0].reshape(attend_rows, positions, heads_local, HEAD_DIM)  21.2 us
    unnamed x19, local copies, waits for them, and re-layouts  18 us
    dot_general x1, local copies, waits for them, and re-layouts, local(): jnp.dot(flat_rows, w_in.reshape(D, -1), preferred_element_type=jnp.float32)  15.1 us
    all_to_all x1, starting transfers between devices, local(): lax.all_to_all(summed, ('ep', 'rep'), split_axis=0, concat_axis=0, tiled=...  9.24 us
  transfers between devices with their start and end apart: 4, of which 3 were waited for; matrix products, arithmetic and copies ran while one was open for 34% of the time, Pallas kernels for 0%

commit v1 on v0

v1 whole, which is shorter than its diff:
```python
import functools
import math

import jax
import jax.numpy as jnp
from jax import lax
from jax.experimental import pallas as pl
from jax.experimental.pallas import tpu as pltpu
from jax.sharding import PartitionSpec as P

HEAD_DIM = 128
LANES = 128
PART = 8
ROWS = 32
epsilon = 1e-06
masked_score = -1e30


def attend_kernel(q_ref, len_ref, k_ref, v_ref, o_ref, m_ref, l_ref):
    rows, positions, width = k_ref.shape[1:]
    heads = width // HEAD_DIM
    part = math.gcd(rows, PART)
    parts = rows // part
    group = heads * part
    q = q_ref[...].astype(jnp.float32)
    head_of = lax.broadcasted_iota(jnp.int32, (part, width), 1) // HEAD_DIM
    which = lax.broadcasted_iota(jnp.int32, (group, positions), 0) % part
    pieces = []
    for g in range(parts):
        mine = q[g * part : (g + 1) * part]
        spread = jnp.concatenate(
            [jnp.where(head_of == h, mine, 0.0) for h in range(heads)], axis=0
        ).astype(jnp.bfloat16)
        keys = k_ref[0, g * part : (g + 1) * part].reshape(part * positions, width)
        every = lax.dot_general(
            spread, keys, (((1,), (1,)), ((), ())), preferred_element_type=jnp.float32
        )
        scores = every[:, :positions]
        for row in range(1, part):
            scores = jnp.where(
                which == row, every[:, row * positions : (row + 1) * positions], scores
            )
        pieces.append(scores)
    scores = jnp.concatenate(pieces, axis=0) * (1.0 / math.sqrt(HEAD_DIM))
    lengths = len_ref[...]
    lengths = jnp.concatenate(
        [lengths[g * part : (g + 1) * part] for g in range(parts) for h in range(heads)], axis=0
    )
    in_cache = lax.broadcasted_iota(jnp.int32, scores.shape, 1) < lengths
    scores = jnp.where(in_cache, scores, masked_score)
    highest = jnp.max(scores, axis=1, keepdims=True)
    weights = jnp.where(in_cache, jnp.exp(scores - highest), 0.0)
    total = jnp.sum(weights, axis=1, keepdims=True)
    for g in range(parts):
        mine = weights[g * group : (g + 1) * group]
        blocks = jnp.concatenate(
            [jnp.where(which == row, mine, 0.0).astype(jnp.bfloat16) for row in range(part)],
            axis=1,
        )
        values = v_ref[0, g * part : (g + 1) * part].reshape(part * positions, width)
        summed = lax.dot_general(
            blocks, values, (((1,), (0,)), ((), ())), preferred_element_type=jnp.float32
        )
        for h in range(heads):
            at = g * group + h * part
            place = (pl.ds(g * part, part), pl.ds(h * HEAD_DIM, HEAD_DIM))
            o_ref[place] = summed[
                h * part : (h + 1) * part, h * HEAD_DIM : (h + 1) * HEAD_DIM
            ]
            m_ref[place] = jnp.broadcast_to(highest[at : at + part], (part, HEAD_DIM))
            l_ref[place] = jnp.broadcast_to(total[at : at + part], (part, HEAD_DIM))


def attend(q, lengths, kv):
    _, n, positions, width = kv.shape
    rows = math.gcd(n, ROWS)
    wide = jax.ShapeDtypeStruct((n, width), jnp.float32)
    return pl.pallas_call(
        attend_kernel,
        grid=(n // rows,),
        in_specs=[
            pl.BlockSpec((rows, width), lambda i: (i, 0)),
            pl.BlockSpec((rows, 1), lambda i: (i, 0)),
            pl.BlockSpec((1, rows, positions, width), lambda i: (0, i, 0, 0)),
            pl.BlockSpec((1, rows, positions, width), lambda i: (1, i, 0, 0)),
        ],
        out_specs=[pl.BlockSpec((rows, width), lambda i: (i, 0))] * 3,
        out_shape=[wide] * 3,
        compiler_params=pltpu.CompilerParams(vmem_limit_bytes=28 << 20),
        cost_estimate=pl.CostEstimate(
            flops=4 * n * positions * width,
            bytes_accessed=4 * n * positions * width,
            transcendentals=0,
        ),
    )(q, lengths, kv, kv)


def expert_kernel(first, x_ref, c_ref, w_ref, d_ref, y_ref, h_ref):
    step = pl.program_id(0)
    tile = w_ref.shape[2]

    @pl.when(step < first)
    def _():
        both = jnp.concatenate([w_ref[0], w_ref[1]], axis=1)
        gate_up = jnp.dot(x_ref[...], both, preferred_element_type=jnp.float32)
        gate, up = gate_up[:, :tile], gate_up[:, tile:]
        h_ref[step] = (gate / (1.0 + jnp.exp(-gate)) * up).astype(jnp.bfloat16)

    @pl.when(step >= first)
    def _():
        units = jnp.concatenate([h_ref[i] for i in range(first)], axis=1)
        y = jnp.dot(units, d_ref[...], preferred_element_type=jnp.float32)
        y = y.astype(jnp.bfloat16).astype(jnp.float32) * c_ref[...]
        y_ref[...] = y.astype(jnp.bfloat16)


def expert(x, coeffs, w_both, w_down):
    rows = x.shape[0]
    _, depth, units = w_both.shape
    width = w_down.shape[1]
    tile = LANES if units % LANES == 0 else units
    out_tile = math.gcd(width, 256)
    first, second = units // tile, width // out_tile
    return pl.pallas_call(
        functools.partial(expert_kernel, first),
        grid=(first + second,),
        in_specs=[
            pl.BlockSpec((rows, depth), lambda i: (0, 0)),
            pl.BlockSpec((rows, 1), lambda i: (0, 0)),
            pl.BlockSpec((2, depth, tile), lambda i: (0, 0, jnp.minimum(i, first - 1))),
            pl.BlockSpec((units, out_tile), lambda i: (0, jnp.maximum(i - first, 0))),
        ],
        out_specs=pl.BlockSpec((rows, out_tile), lambda i: (0, jnp.maximum(i - first, 0))),
        out_shape=jax.ShapeDtypeStruct((rows, width), jnp.bfloat16),
        scratch_shapes=[pltpu.VMEM((first, rows, tile), jnp.bfloat16)],
        compiler_params=pltpu.CompilerParams(vmem_limit_bytes=28 << 20),
        cost_estimate=pl.CostEstimate(
            flops=6 * rows * depth * units,
            bytes_accessed=2 * (3 * depth * units + 2 * rows * depth),
            transcendentals=rows * units,
        ),
    )(x, coeffs, w_both, w_down)


def split_three(v):
    parts = []
    for _ in range(3):
        part = lax.reduce_precision(v, 8, 7)
        parts.append(part.astype(jnp.bfloat16))
        v = v - part
    return jnp.stack(parts, axis=-1)


def local(
    hidden_in,
    row_counts,
    qkv_new,
    cache_len,
    kv_cache,
    w_out,
    moe_gain,
    w_in,
    w_down,
    route_ids,
    route_weight,
):
    wide = jnp.float32
    narrow = jnp.bfloat16
    tok_rows, feat_local = hidden_in.shape
    owners = lax.axis_size("ep")
    reps = lax.axis_size("rep")
    parts_seq = lax.axis_size("seq")
    width_local = kv_cache.shape[-1]
    heads_local = width_local // HEAD_DIM
    positions = kv_cache.shape[3]
    share_rows = tok_rows // parts_seq
    attend_rows = owners * share_rows
    inner = 2 if owners % 2 == 0 else 1
    outer = owners // inner
    me = lax.axis_index("ep")
    outer_me, inner_me = me // inner, me % inner

    def across(v):
        return lax.ppermute(v, "ep", [(i, i ^ 1) for i in range(owners)])

    def along(v, k):
        pairs = [
            (i, (i // inner + k) % outer * inner + i % inner) for i in range(owners)
        ]
        return lax.ppermute(v, "ep", pairs)

    def other(v):
        return lax.ppermute(v, "rep", [(i, (i + 1) % reps) for i in range(reps)])

    def rows_of_seq(v, axis):
        return lax.dynamic_slice_in_dim(v, lax.axis_index("seq") * share_rows, share_rows, axis)

    fresh = qkv_new.reshape(tok_rows, 3, owners, width_local)
    sent_q = fresh[:, 0].transpose(1, 0, 2)
    queries = lax.all_to_all(sent_q, "ep", split_axis=0, concat_axis=0, tiled=True)
    queries = rows_of_seq(queries, 1).reshape(attend_rows, width_local)

    heads = qkv_new.reshape(tok_rows, 3, owners, heads_local, HEAD_DIM).astype(wide)
    own = jnp.sum(heads[:, 0] * heads[:, 1], axis=-1) * (1.0 / math.sqrt(HEAD_DIM))
    own = split_three(own).reshape(tok_rows, owners, heads_local * 3)
    own = jnp.pad(own, ((0, 0), (0, 0), (0, LANES - heads_local * 3)))
    sent_v = jnp.concatenate([fresh[:, 2], own], axis=2).transpose(1, 0, 2)
    sent_v, queries = lax.optimization_barrier((sent_v, queries))
    values = lax.all_to_all(sent_v, "ep", split_axis=0, concat_axis=0, tiled=True)
    values = rows_of_seq(values, 1).reshape(attend_rows, width_local + LANES)

    kv = kv_cache.reshape(2, attend_rows, positions, width_local)
    summed, highest, total = attend(queries, cache_len.reshape(attend_rows, 1), kv)
    shape = (attend_rows, heads_local, HEAD_DIM)
    own = jnp.sum(
        values[:, width_local : width_local + heads_local * 3]
        .reshape(attend_rows, heads_local, 3)
        .astype(wide),
        axis=2,
    )[:, :, None]
    highest = highest.reshape(shape)
    top = jnp.maximum(highest, own)
    scale = jnp.exp(highest - top)
    own_weight = jnp.exp(own - top)
    value_new = values[:, :width_local].reshape(shape).astype(wide)
    attended = (summed.reshape(shape) * scale + own_weight * value_new) / (
        total.reshape(shape) * scale + own_weight
    )
    attended = attended.astype(narrow).reshape(owners, share_rows, width_local)
    attended = lax.all_gather(attended, "seq", axis=1, tiled=True)

    attended = attended.reshape(outer, inner, tok_rows, width_local)
    if inner == 2:
        first = inner_me == 0
        kept = jnp.where(first, attended[:, 0], attended[:, 1])
        given = jnp.where(first, attended[:, 1], attended[:, 0])
        joined = jnp.concatenate([kept, across(given)], axis=2)
        if reps == 2:
            half = w_out.shape[0] // 2
            rep_first = lax.axis_index("rep") == 0
            mine = across(jnp.where(rep_first, w_out[:half], w_out[half:]))
            theirs = other(mine)
            both = jnp.concatenate(
                [jnp.where(rep_first, mine, theirs), jnp.where(rep_first, theirs, mine)], axis=0
            )
        else:
            both = across(w_out)
        w_pair = jnp.concatenate([w_out, both], axis=0)
    else:
        joined, w_pair = attended[:, 0], w_out
    turned = lax.dynamic_slice_in_dim(
        jnp.concatenate([joined, joined], axis=0), outer_me, outer, 0
    )
    partial_out = jnp.dot(
        turned.reshape(outer * tok_rows, -1), w_pair, preferred_element_type=wide
    ).reshape(outer, tok_rows, feat_local)
    attn_out = partial_out[0]
    for k in range(1, outer):
        attn_out = attn_out + along(partial_out[k].astype(narrow), k).astype(wide)
    residual = (hidden_in.astype(wide) + attn_out).astype(narrow)
    residual_wide = residual.astype(wide)

    is_live = jnp.arange(tok_rows, dtype=jnp.int32) < row_counts[0]
    experts_local = w_in.shape[0]
    expert_total = owners * reps * experts_local
    hits = route_ids[:, :, None] == jnp.arange(expert_total, dtype=jnp.int32)[None, None, :]
    hits = hits & is_live[:, None, None]
    coeffs = jnp.sum(jnp.where(hits, route_weight.astype(wide)[:, :, None], 0.0), axis=1)
    lanes = -(-expert_total // LANES) * LANES
    coeffs = jnp.pad(coeffs, ((0, 0), (0, lanes - expert_total))).astype(narrow)
    full_rows = lax.all_gather(residual, "seq", axis=1, tiled=True).astype(wide)
    width = full_rows.shape[1]
    inverse_rms = lax.rsqrt(jnp.mean(full_rows * full_rows, axis=1) + epsilon)
    normed = (full_rows * inverse_rms[:, None] * moe_gain).astype(narrow)
    packed = jnp.concatenate([normed, coeffs], axis=1)
    slots = [packed] + [along(packed, k) for k in range(1, outer)]
    if inner == 2:
        slots = slots + [across(s) for s in slots]
    if reps == 2:
        slots = slots + [other(s) for s in slots]
    arrived = jnp.concatenate(slots, axis=0)
    rows_in = arrived[:, :width]
    gates = arrived[:, width:].astype(wide)
    first_expert = (me * reps + lax.axis_index("rep")) * experts_local
    produced = None
    for j in range(experts_local):
        mine = jnp.arange(lanes, dtype=jnp.int32)[None, :] == first_expert + j
        factor = jnp.sum(jnp.where(mine, gates, 0.0), axis=1, keepdims=True)
        w_both = w_in[j].transpose(1, 0, 2)
        part = expert(rows_in, factor, w_both, w_down[j])
        produced = part if produced is None else produced + part
    if parts_seq > 1:
        produced = lax.psum_scatter(
            produced.astype(wide), "seq", scatter_dimension=1, tiled=True
        ).astype(narrow)

    produced = produced.reshape(reps, inner, outer, tok_rows, feat_local)
    if reps == 2:
        merged = produced[0].astype(wide) + other(produced[1]).astype(wide)
    else:
        merged = produced[0].astype(wide)
    cut = feat_local // 2

    def inner_sum(v):
        if inner == 1:
            return v[0]
        return v[0] + across(v[1].astype(narrow)).astype(wide)

    def outer_sum(v):
        result = v[:, 0]
        for k in range(1, outer):
            result = result + along(v[:, k].astype(narrow), -k).astype(wide)
        return result

    left = outer_sum(inner_sum(merged[..., :cut])[None])[0]
    right = inner_sum(outer_sum(merged[..., cut:]))
    moe_out = jnp.concatenate([left, right], axis=1)
    return jnp.where(is_live[:, None], residual_wide + moe_out, 0.0).astype(narrow)


def solution(mesh):
    placed = (
        P(("grp", "ep", "rep"), "seq"),
        P(("grp", "ep", "rep")),
        P(("grp", "ep", "rep"), None, None),
        P("grp", ("rep", "seq")),
        P(None, "grp", ("rep", "seq"), None, "ep"),
        P("ep", "seq"),
        P(),
        P(("ep", "rep"), None, None, "seq"),
        P(("ep", "rep"), "seq", None),
        P(("grp", "ep", "rep"), None),
        P(("grp", "ep", "rep"), None),
    )
    return jax.shard_map(
        local, mesh=mesh, in_specs=placed, out_specs=P(("grp", "ep", "rep"), "seq"), check_vma=False
    )
```

time: 289 us -> 155 us (0.54); the launches traced: 284 us -> 155 us
  local copies, waits for them, and re-layouts: 104 us -> 35.1 us
  waiting for transfers between devices: 104 us -> 44.3 us
  matrix products: 35.9 us -> 0.68 us
  Pallas kernels: 0 us -> 30.8 us
  starting transfers between devices: 20.4 us -> 36.9 us
  between operations: 14.3 us -> 1.07 us
    reduce_scatter x1 -> x0, waiting for transfers between devices: 67.2 us -> none  [local(): lax.psum_scatter(jnp.dot(attended, w_out, preferred_element_type=jnp.floa...]
    another operation x3 -> x1, local copies, waits for them, and re-layouts: 44.9 us -> 0.09 us  [the longest x1 23.7 us: local(): kv_cache[1].reshape(attend_rows, positions, heads_local, HEAD_DIM)]
    ppermute x0 -> x30, waiting for transfers between devices: none -> 41.2 us  [the longest x12 29.2 us: along(): return lax.ppermute(v, 'ep', pairs)]
    dot_general x7 -> x1, matrix products: 35.9 us -> 0.68 us  [local(): jnp.dot(turned.reshape(outer * tok_rows, -1), w_pair, preferred_element_t...]
    all_to_all x3 -> x2, waiting for transfers between devices: 37.2 us -> 3.1 us  [the longest x1 3.1 us: local(): lax.all_to_all(sent_q, 'ep', split_axis=0, concat_axis=0, tiled=True)]
    pallas_call x0 -> x2, Pallas kernels: none -> 30.8 us  [the longest x1 16.2 us: expert(): pl.pallas_call(functools.partial(expert_kernel, first), grid=(first + sec...]
    ppermute x0 -> x30, starting transfers between devices: none -> 26.3 us  [the longest x12 13.1 us: along(): return lax.ppermute(v, 'ep', pairs)]
    slice x2 -> x5, local copies, waits for them, and re-layouts: 23.3 us -> 1.91 us  [the longest x1 1.73 us: local(): rows_in = arrived[:, :width]]
  transfers between devices with their start and end apart: 4 -> 32, of which waited for: 3 -> 15; matrix products, arithmetic and copies ran while one was open for 34% -> 16% of each run, Pallas kernels for 0% -> 9%
where the time goes in v1:
time: 155 us
  waiting for transfers between devices  44.3 us (29%)
  starting transfers between devices  36.9 us (24%)
  local copies, waits for them, and re-layouts  35.1 us (23%)
  Pallas kernels  30.8 us (20%)
  other arithmetic  6.04 us (4%)
    ppermute x12, waiting for transfers between devices, along(): return lax.ppermute(v, 'ep', pairs)  29.2 us
    unnamed x35, local copies, waits for them, and re-layouts  28.8 us
    pallas_call x1, Pallas kernels, expert(): pl.pallas_call(functools.partial(expert_kernel, first), grid=(first + sec...  16.2 us
    pallas_call x1, Pallas kernels, attend(): pl.pallas_call(attend_kernel, grid=(n // rows,), in_specs=[pl.BlockSpec((...  14.6 us
    ppermute x12, starting transfers between devices, along(): return lax.ppermute(v, 'ep', pairs)  13.1 us
    ppermute x8, starting transfers between devices, across(): return lax.ppermute(v, 'ep', [(i, i ^ 1) for i in range(owners)])  11.1 us
    ppermute x8, waiting for transfers between devices, across(): return lax.ppermute(v, 'ep', [(i, i ^ 1) for i in range(owners)])  9.67 us
    all_to_all x1, starting transfers between devices, local(): lax.all_to_all(sent_q, 'ep', split_axis=0, concat_axis=0, tiled=True)  7.25 us
  transfers between devices with their start and end apart: 32, of which 15 were waited for; matrix products, arithmetic and copies ran while one was open for 16% of the time, Pallas kernels for 9%

profile of v1, /device:TPU:0, one launch (start us, length us, event | category | flops | bytes accessed | tf_op | source)
XLA Modules:
  0.0 154.8 jit_solution(18152971538006554033)
XLA Ops:
  0.0 1.2 copy.106
  1.9 7.3 %all-to-all-start = ((bf16[8,32,256]{2,1,0:T(8,128)(2,1)}), bf16[8,32,256]{2,1,0:T(8,128)(2,1)S(1)}, u32[]{:S(2)}, u32[]{:S(2)}) async-start(bf16[8,32,256]{2,1,0:T(8,128)(2,1)} %copy.88), calls=%async_computation | async-start | bytes 262144 | tf_op jit(solution)/shard_map/all_to_all | solution.py:200
  10.0 2.0 %collective-permute-start.1 = (bf16[128,2048]{1,0:T(8,128)(2,1)}, bf16[128,2048]{1,0:T(8,128)(2,1)S(1)}, u32[]{:S(2)}, u32[]{:S(2)}) collective-permute-start(bf16[128,2048]{1,0:T(8,128)(2,1)} %slice_select_fusion), channel_id=1, source_target_pairs={{0,2},{2,0},{4,6},{6,4},{8,10},{10,8},{12,14},{14,12},{1,3},{3,1},... | collective-permute-start | bytes 1572872 | tf_op jit(solution)/shard_map/ppermute | solution.py:184
  13.5 3.1 %all-to-all-done = bf16[8,32,256]{2,1,0:T(8,128)(2,1)S(1)} async-done(((bf16[8,32,256]{2,1,0:T(8,128)(2,1)}), bf16[8,32,256]{2,1,0:T(8,128)(2,1)S(1)}, u32[]{:S(2)}, u32[]{:S(2)}) %all-to-all-start) | async-done | bytes 131104 | tf_op jit(solution)/shard_map/all_to_all | solution.py:200
  17.3 3.4 %all-to-all-start.1 = ((bf16[8,32,384]{2,1,0:T(8,128)(2,1)}), bf16[8,32,384]{2,1,0:T(8,128)(2,1)S(1)}, u32[]{:S(2)}, u32[]{:S(2)}) async-start(bf16[8,32,384]{2,1,0:T(8,128)(2,1)} %copy.90), calls=%async_computation.1 | async-start | bytes 393216 | tf_op jit(solution)/shard_map/all_to_all | solution.py:209
  21.5 14.6 %shard_map.109 = (f32[256,256]{1,0:T(8,128)S(1)}, f32[256,256]{1,0:T(8,128)S(1)}, f32[256,256]{1,0:T(8,128)S(1)}) custom-call(bf16[256,256]{1,0:T(8,128)(2,1)S(1)} %bitcast.117, s32[256,1]{1,0:T(8,128)S(1)} %reshape.195.len_ref, bf16[2,256,128,256]{3,2,1,0:T(8,128)(2,1)} %bitcast.122, bf16[2,256,128,256]{3,2,1,0:T(8,128)(2,1)} %bitcast.123), custom_call_target="tpu_custom_call" | custom-call | flops 33554432 | bytes 33554432 | tf_op jit(solution)/shard_map/pallas_call | solution.py:78
  37.3 2.0 %collective-permute-start = (bf16[4,32,256]{2,1,0:T(8,128)(2,1)S(1)}, bf16[4,32,256]{2,1,0:T(8,128)(2,1)S(1)}, u32[]{:S(2)}, u32[]{:S(2)}) collective-permute-start(bf16[4,32,256]{2,1,0:T(8,128)(2,1)S(1)} %fusion.39), channel_id=1, source_target_pairs={{0,2},{2,0},{4,6},{6,4},{8,10},{10,8},{12,14},{14,12},{1,3},{3,1},... | collective-permute-start | bytes 196616 | tf_op jit(solution)/shard_map/ppermute | solution.py:184
  39.2 2.7 %collective-permute-done = bf16[4,32,256]{2,1,0:T(8,128)(2,1)S(1)} collective-permute-done((bf16[4,32,256]{2,1,0:T(8,128)(2,1)S(1)}, bf16[4,32,256]{2,1,0:T(8,128)(2,1)S(1)}, u32[]{:S(2)}, u32[]{:S(2)}) %collective-permute-start) | collective-permute-done | bytes 65568 | tf_op jit(solution)/shard_map/ppermute | solution.py:184
  42.1 1.1 broadcast_select_fusion.1
  44.0 1.8 %collective-permute-start.3 = (bf16[32,2048]{1,0:T(8,128)(2,1)S(1)}, bf16[32,2048]{1,0:T(8,128)(2,1)S(1)}, u32[]{:S(2)}, u32[]{:S(2)}) collective-permute-start(bf16[32,2048]{1,0:T(8,128)(2,1)S(1)} %get-tuple-element.28), channel_id=1, source_target_pairs={{0,4},{2,6},{4,8},{6,10},{8,12},{10,14},{12,0},{14,2},{1,5},{3,7},... | collective-permute-start | bytes 393224 | tf_op jit(solution)/shard_map/ppermute | solution.py:190
  45.8 2.1 %collective-permute-start.5 = (bf16[32,2048]{1,0:T(8,128)(2,1)S(1)}, bf16[32,2048]{1,0:T(8,128)(2,1)S(1)}, u32[]{:S(2)}, u32[]{:S(2)}) collective-permute-start(bf16[32,2048]{1,0:T(8,128)(2,1)S(1)} %get-tuple-element.29), channel_id=1, source_target_pairs={{0,12},{2,14},{4,0},{6,2},{8,4},{10,6},{12,8},{14,10},{1,13},{3,15... | collective-permute-start | bytes 393224 | tf_op jit(solution)/shard_map/ppermute | solution.py:190
  48.8 3.4 %collective-permute-done.3 = bf16[32,2048]{1,0:T(8,128)(2,1)S(1)} collective-permute-done((bf16[32,2048]{1,0:T(8,128)(2,1)S(1)}, bf16[32,2048]{1,0:T(8,128)(2,1)S(1)}, u32[]{:S(2)}, u32[]{:S(2)}) %collective-permute-start.3) | collective-permute-done | bytes 131104 | tf_op jit(solution)/shard_map/ppermute | solution.py:190
  52.2 1.2 collective-permute-done.5
  53.4 6.0 %collective-permute-done.4 = bf16[32,2048]{1,0:T(8,128)(2,1)S(1)} collective-permute-done((bf16[32,2048]{1,0:T(8,128)(2,1)S(1)}, bf16[32,2048]{1,0:T(8,128)(2,1)S(1)}, u32[]{:S(2)}, u32[]{:S(2)}) %collective-permute-start.4) | collective-permute-done | bytes 131104 | tf_op jit(solution)/shard_map/ppermute | solution.py:190
  60.4 1.7 %collective-permute-start.8 = (bf16[32,2176]{1,0:T(8,128)(2,1)S(1)}, bf16[32,2176]{1,0:T(8,128)(2,1)S(1)}, u32[]{:S(2)}, u32[]{:S(2)}) collective-permute-start(bf16[32,2176]{1,0:T(8,128)(2,1)S(1)} %get-tuple-element.36), channel_id=1, source_target_pairs={{0,12},{2,14},{4,0},{6,2},{8,4},{10,6},{12,8},{14,10},{1,13},{3,15... | collective-permute-start | bytes 417800 | tf_op jit(solution)/shard_map/ppermute | solution.py:190
  62.5 11.2 %copy.110 = bf16[1,2048,2,1408]{3,1,2,0:T(8,128)(2,1)} copy(bf16[1,2048,2,1408]{3,2,1,0:T(2,128)(2,1)} %param.18) | data formatting | bytes 23068672 | tf_op args[7]
  73.7 1.7 %collective-permute-start.9 = (bf16[32,2176]{1,0:T(8,128)(2,1)S(1)}, bf16[32,2176]{1,0:T(8,128)(2,1)S(1)}, u32[]{:S(2)}, u32[]{:S(2)}) collective-permute-start(bf16[32,2176]{1,0:T(8,128)(2,1)S(1)} %get-tuple-element.36), channel_id=1, source_target_pairs={{0,2},{2,0},{4,6},{6,4},{8,10},{10,8},{12,14},{14,12},{1,3},{3,1},... | collective-permute-start | bytes 417800 | tf_op jit(solution)/shard_map/ppermute | solution.py:184
  77.1 2.1 %collective-permute-done.9 = bf16[32,2176]{1,0:T(8,128)(2,1)S(1)} collective-permute-done((bf16[32,2176]{1,0:T(8,128)(2,1)S(1)}, bf16[32,2176]{1,0:T(8,128)(2,1)S(1)}, u32[]{:S(2)}, u32[]{:S(2)}) %collective-permute-start.9) | collective-permute-done | bytes 139296 | tf_op jit(solution)/shard_map/ppermute | solution.py:184
  79.2 2.5 %collective-permute-start.10 = (bf16[32,2176]{1,0:T(8,128)(2,1)S(1)}, bf16[32,2176]{1,0:T(8,128)(2,1)S(1)}, u32[]{:S(2)}, u32[]{:S(2)}) collective-permute-start(bf16[32,2176]{1,0:T(8,128)(2,1)S(1)} %collective-permute-done.6), channel_id=1, source_target_pairs={{0,2},{2,0},{4,6},{6,4},{8,10},{10,8},{12,14},{14,12},{1,3},{3,1},... | collective-permute-start | bytes 417800 | tf_op jit(solution)/shard_map/ppermute | solution.py:184
  81.7 2.2 %collective-permute-done.7 = bf16[32,2176]{1,0:T(8,128)(2,1)S(1)} collective-permute-done((bf16[32,2176]{1,0:T(8,128)(2,1)S(1)}, bf16[32,2176]{1,0:T(8,128)(2,1)S(1)}, u32[]{:S(2)}, u32[]{:S(2)}) %collective-permute-start.7) | collective-permute-done | bytes 139296 | tf_op jit(solution)/shard_map/ppermute | solution.py:190
  87.4 4.6 %collective-permute-done.11 = bf16[32,2176]{1,0:T(8,128)(2,1)S(1)} collective-permute-done((bf16[32,2176]{1,0:T(8,128)(2,1)S(1)}, bf16[32,2176]{1,0:T(8,128)(2,1)S(1)}, u32[]{:S(2)}, u32[]{:S(2)}) %collective-permute-start.11) | collective-permute-done | bytes 139296 | tf_op jit(solution)/shard_map/ppermute | solution.py:184
  99.7 1.7 %slice.159.x_ref = bf16[512,2048]{1,0:T(8,128)(2,1)S(1)} slice(bf16[512,2176]{1,0:T(8,128)(2,1)} %constant_dynamic-update-slice_fusion), slice={[0:512], [0:2048]} | slice | bytes 4194304 | tf_op jit(solution)/shard_map/slice | solution.py:282
  102.7 4.3 %copy-done = bf16[1,2048,2,1408]{3,1,2,0:T(8,128)(2,1)S(1)} copy-done((bf16[1,2048,2,1408]{3,1,2,0:T(8,128)(2,1)S(1)}, bf16[1,2048,2,1408]{3,1,2,0:T(8,128)(2,1)}, u32[]{:S(2)}) %copy-start) | copy-done | bytes 11534360
  106.9 2.6 %copy-done.1 = bf16[1,1408,2048]{2,1,0:T(8,128)(2,1)S(1)} copy-done((bf16[1,1408,2048]{2,1,0:T(8,128)(2,1)S(1)}, bf16[1,1408,2048]{2,1,0:T(8,128)(2,1)}, u32[]{:S(2)}) %copy-start.1) | copy-done | bytes 5767192
  109.6 16.2 %shard_map.110 = bf16[512,2048]{1,0:T(8,128)(2,1)S(1)} custom-call(bf16[512,2048]{1,0:T(8,128)(2,1)S(1)} %slice.159.x_ref, f32[512,1]{1,0:T(8,128)S(1)} %copy.99.c_ref, bf16[2,2048,1408]{2,1,0:T(8,128)(2,1)S(1)} %bitcast.116, bf16[1408,2048]{1,0:T(8,128)(2,1)S(1)} %bitcast.121), custom_call_target="tpu_custom_call" | custom-call | flops 8858370048 | bytes 21495808 | tf_op jit(solution)/shard_map/pallas_call | solution.py:124
  126.6 2.3 %collective-permute-done.21 = bf16[2,4,32,2048]{3,2,0,1:T(8,128)(2,1)S(1)} collective-permute-done((bf16[2,4,32,2048]{3,2,0,1:T(8,128)(2,1)S(1)}, bf16[2,4,32,2048]{3,2,0,1:T(8,128)(2,1)S(1)}, u32[]{:S(2)}, u32[]{:S(2)}) %collective-permute-start.21) | collective-permute-done | bytes 1048608 | tf_op jit(solution)/shard_map/ppermute | solution.py:193
  129.4 1.4 collective-permute-start.26
  133.3 1.9 %collective-permute-done.26 = bf16[2,32,1024]{2,1,0:T(8,128)(2,1)S(1)} collective-permute-done((bf16[2,32,1024]{2,1,0:T(8,128)(2,1)S(1)}, bf16[2,32,1024]{2,1,0:T(8,128)(2,1)S(1)}, u32[]{:S(2)}, u32[]{:S(2)}) %collective-permute-start.26) | collective-permute-done | bytes 131104 | tf_op jit(solution)/shard_map/ppermute | solution.py:190
  135.2 3.8 %collective-permute-done.28 = bf16[2,32,1024]{2,1,0:T(8,128)(2,1)S(1)} collective-permute-done((bf16[2,32,1024]{2,1,0:T(8,128)(2,1)S(1)}, bf16[2,32,1024]{2,1,0:T(8,128)(2,1)S(1)}, u32[]{:S(2)}, u32[]{:S(2)}) %collective-permute-start.28) | collective-permute-done | bytes 131104 | tf_op jit(solution)/shard_map/ppermute | solution.py:190
  139.0 5.5 %collective-permute-done.27 = bf16[2,32,1024]{2,1,0:T(8,128)(2,1)S(1)} collective-permute-done((bf16[2,32,1024]{2,1,0:T(8,128)(2,1)S(1)}, bf16[2,32,1024]{2,1,0:T(8,128)(2,1)S(1)}, u32[]{:S(2)}, u32[]{:S(2)}) %collective-permute-start.27) | collective-permute-done | bytes 131104 | tf_op jit(solution)/shard_map/ppermute | solution.py:190
  145.3 2.7 %collective-permute-start.23 = (bf16[1,32,1024]{2,1,0:T(8,128)(2,1)S(1)}, bf16[1,32,1024]{2,1,0:T(8,128)(2,1)S(1)}, u32[]{:S(2)}, u32[]{:S(2)}) collective-permute-start(bf16[1,32,1024]{2,1,0:T(8,128)(2,1)S(1)} %get-tuple-element.33), channel_id=1, source_target_pairs={{0,12},{2,14},{4,0},{6,2},{8,4},{10,6},{12,8},{14,10},{1,13},{3,15... | collective-permute-start | bytes 196616 | tf_op jit(solution)/shard_map/ppermute | solution.py:190
  150.0 4.0 %collective-permute-done.25 = bf16[1,32,1024]{2,1,0:T(8,128)(2,1)S(1)} collective-permute-done((bf16[1,32,1024]{2,1,0:T(8,128)(2,1)S(1)}, bf16[1,32,1024]{2,1,0:T(8,128)(2,1)S(1)}, u32[]{:S(2)}, u32[]{:S(2)}) %collective-permute-start.25) | collective-permute-done | bytes 65568 | tf_op jit(solution)/shard_map/ppermute | solution.py:190
  (120 shorter events, 29.6 us)
Async XLA Ops:
  1.9 14.7 %all-to-all-start = ((bf16[8,32,256]{2,1,0:T(8,128)(2,1)}), bf16[8,32,256]{2,1,0:T(8,128)(2,1)S(1)}, u32[]{:S(2)}, u32[]{:S(2)}) async-start(bf16[8,32,256]{2,1,0:T(8,128)(2,1)} %copy.88), calls=%async_computation | async-start | bytes 262144 | tf_op jit(solution)/shard_map/all_to_all | solution.py:200
  10.0 26.1 %collective-permute-start.1 = (bf16[128,2048]{1,0:T(8,128)(2,1)}, bf16[128,2048]{1,0:T(8,128)(2,1)S(1)}, u32[]{:S(2)}, u32[]{:S(2)}) collective-permute-start(bf16[128,2048]{1,0:T(8,128)(2,1)} %slice_select_fusion), channel_id=1, source_target_pairs={{0,2},{2,0},{4,6},{6,4},{8,10},{10,8},{12,14},{14,12},{1,3},{3,1},... | collective-permute-start | bytes 1572872 | tf_op jit(solution)/shard_map/ppermute | solution.py:184
  17.3 18.9 %all-to-all-start.1 = ((bf16[8,32,384]{2,1,0:T(8,128)(2,1)}), bf16[8,32,384]{2,1,0:T(8,128)(2,1)S(1)}, u32[]{:S(2)}, u32[]{:S(2)}) async-start(bf16[8,32,384]{2,1,0:T(8,128)(2,1)} %copy.90), calls=%async_computation.1 | async-start | bytes 393216 | tf_op jit(solution)/shard_map/all_to_all | solution.py:209
  36.1 5.9 %collective-permute-start.2 = (bf16[128,2048]{1,0:T(8,128)(2,1)S(1)}, bf16[128,2048]{1,0:T(8,128)(2,1)}, u32[]{:S(2)}, u32[]{:S(2)}) collective-permute-start(bf16[128,2048]{1,0:T(8,128)(2,1)S(1)} %collective-permute-done.1), channel_id=1, source_target_pairs={{0,1},{1,0},{2,3},{3,2},{4,5},{5,4},{6,7},{7,6},{8,9},{9,8},{10,11... | collective-permute-start | bytes 1572872 | tf_op jit(solution)/shard_map/ppermute | solution.py:193
  37.3 4.7 %collective-permute-start = (bf16[4,32,256]{2,1,0:T(8,128)(2,1)S(1)}, bf16[4,32,256]{2,1,0:T(8,128)(2,1)S(1)}, u32[]{:S(2)}, u32[]{:S(2)}) collective-permute-start(bf16[4,32,256]{2,1,0:T(8,128)(2,1)S(1)} %fusion.39), channel_id=1, source_target_pairs={{0,2},{2,0},{4,6},{6,4},{8,10},{10,8},{12,14},{14,12},{1,3},{3,1},... | collective-permute-start | bytes 196616 | tf_op jit(solution)/shard_map/ppermute | solution.py:184
  44.0 8.2 %collective-permute-start.3 = (bf16[32,2048]{1,0:T(8,128)(2,1)S(1)}, bf16[32,2048]{1,0:T(8,128)(2,1)S(1)}, u32[]{:S(2)}, u32[]{:S(2)}) collective-permute-start(bf16[32,2048]{1,0:T(8,128)(2,1)S(1)} %get-tuple-element.28), channel_id=1, source_target_pairs={{0,4},{2,6},{4,8},{6,10},{8,12},{10,14},{12,0},{14,2},{1,5},{3,7},... | collective-permute-start | bytes 393224 | tf_op jit(solution)/shard_map/ppermute | solution.py:190
  45.8 7.6 %collective-permute-start.5 = (bf16[32,2048]{1,0:T(8,128)(2,1)S(1)}, bf16[32,2048]{1,0:T(8,128)(2,1)S(1)}, u32[]{:S(2)}, u32[]{:S(2)}) collective-permute-start(bf16[32,2048]{1,0:T(8,128)(2,1)S(1)} %get-tuple-element.29), channel_id=1, source_target_pairs={{0,12},{2,14},{4,0},{6,2},{8,4},{10,6},{12,8},{14,10},{1,13},{3,15... | collective-permute-start | bytes 393224 | tf_op jit(solution)/shard_map/ppermute | solution.py:190
  47.9 11.6 %collective-permute-start.4 = (bf16[32,2048]{1,0:T(8,128)(2,1)S(1)}, bf16[32,2048]{1,0:T(8,128)(2,1)S(1)}, u32[]{:S(2)}, u32[]{:S(2)}) collective-permute-start(bf16[32,2048]{1,0:T(8,128)(2,1)S(1)} %get-tuple-element.30), channel_id=1, source_target_pairs={{0,8},{2,10},{4,12},{6,14},{8,0},{10,2},{12,4},{14,6},{1,9},{3,11}... | collective-permute-start | bytes 393224 | tf_op jit(solution)/shard_map/ppermute | solution.py:190
  60.4 15.0 %collective-permute-start.8 = (bf16[32,2176]{1,0:T(8,128)(2,1)S(1)}, bf16[32,2176]{1,0:T(8,128)(2,1)S(1)}, u32[]{:S(2)}, u32[]{:S(2)}) collective-permute-start(bf16[32,2176]{1,0:T(8,128)(2,1)S(1)} %get-tuple-element.36), channel_id=1, source_target_pairs={{0,12},{2,14},{4,0},{6,2},{8,4},{10,6},{12,8},{14,10},{1,13},{3,15... | collective-permute-start | bytes 417800 | tf_op jit(solution)/shard_map/ppermute | solution.py:190
  62.1 13.8 %collective-permute-start.6 = (bf16[32,2176]{1,0:T(8,128)(2,1)S(1)}, bf16[32,2176]{1,0:T(8,128)(2,1)S(1)}, u32[]{:S(2)}, u32[]{:S(2)}) collective-permute-start(bf16[32,2176]{1,0:T(8,128)(2,1)S(1)} %get-tuple-element.36), channel_id=1, source_target_pairs={{0,4},{2,6},{4,8},{6,10},{8,12},{10,14},{12,0},{14,2},{1,5},{3,7},... | collective-permute-start | bytes 417800 | tf_op jit(solution)/shard_map/ppermute | solution.py:190
  73.7 5.5 %collective-permute-start.9 = (bf16[32,2176]{1,0:T(8,128)(2,1)S(1)}, bf16[32,2176]{1,0:T(8,128)(2,1)S(1)}, u32[]{:S(2)}, u32[]{:S(2)}) collective-permute-start(bf16[32,2176]{1,0:T(8,128)(2,1)S(1)} %get-tuple-element.36), channel_id=1, source_target_pairs={{0,2},{2,0},{4,6},{6,4},{8,10},{10,8},{12,14},{14,12},{1,3},{3,1},... | collective-permute-start | bytes 417800 | tf_op jit(solution)/shard_map/ppermute | solution.py:184
  75.4 8.6 %collective-permute-start.7 = (bf16[32,2176]{1,0:T(8,128)(2,1)S(1)}, bf16[32,2176]{1,0:T(8,128)(2,1)S(1)}, u32[]{:S(2)}, u32[]{:S(2)}) collective-permute-start(bf16[32,2176]{1,0:T(8,128)(2,1)S(1)} %get-tuple-element.36), channel_id=1, source_target_pairs={{0,8},{2,10},{4,12},{6,14},{8,0},{10,2},{12,4},{14,6},{1,9},{3,11}... | collective-permute-start | bytes 417800 | tf_op jit(solution)/shard_map/ppermute | solution.py:190
  75.4 18.5 %collective-permute-start.13 = (bf16[32,2176]{1,0:T(8,128)(2,1)S(1)}, bf16[32,2176]{1,0:T(8,128)(2,1)S(1)}, u32[]{:S(2)}, u32[]{:S(2)}) collective-permute-start(bf16[32,2176]{1,0:T(8,128)(2,1)S(1)} %get-tuple-element.36), channel_id=1, source_target_pairs={{0,1},{1,0},{2,3},{3,2},{4,5},{5,4},{6,7},{7,6},{8,9},{9,8},{10,11... | collective-permute-start | bytes 417800 | tf_op jit(solution)/shard_map/ppermute | solution.py:193
  75.4 21.0 %collective-permute-start.16 = (bf16[32,2176]{1,0:T(8,128)(2,1)S(1)}, bf16[32,2176]{1,0:T(8,128)(2,1)S(1)}, u32[]{:S(2)}, u32[]{:S(2)}) collective-permute-start(bf16[32,2176]{1,0:T(8,128)(2,1)S(1)} %collective-permute-done.8), channel_id=1, source_target_pairs={{0,1},{1,0},{2,3},{3,2},{4,5},{5,4},{6,7},{7,6},{8,9},{9,8},{10,11... | collective-permute-start | bytes 417800 | tf_op jit(solution)/shard_map/ppermute | solution.py:193
  75.9 16.8 %collective-permute-start.12 = (bf16[32,2176]{1,0:T(8,128)(2,1)S(1)}, bf16[32,2176]{1,0:T(8,128)(2,1)S(1)}, u32[]{:S(2)}, u32[]{:S(2)}) collective-permute-start(bf16[32,2176]{1,0:T(8,128)(2,1)S(1)} %collective-permute-done.8), channel_id=1, source_target_pairs={{0,2},{2,0},{4,6},{6,4},{8,10},{10,8},{12,14},{14,12},{1,3},{3,1},... | collective-permute-start | bytes 417800 | tf_op jit(solution)/shard_map/ppermute | solution.py:184
  79.2 6.7 %collective-permute-start.10 = (bf16[32,2176]{1,0:T(8,128)(2,1)S(1)}, bf16[32,2176]{1,0:T(8,128)(2,1)S(1)}, u32[]{:S(2)}, u32[]{:S(2)}) collective-permute-start(bf16[32,2176]{1,0:T(8,128)(2,1)S(1)} %collective-permute-done.6), channel_id=1, source_target_pairs={{0,2},{2,0},{4,6},{6,4},{8,10},{10,8},{12,14},{14,12},{1,3},{3,1},... | collective-permute-start | bytes 417800 | tf_op jit(solution)/shard_map/ppermute | solution.py:184
  83.9 13.2 %collective-permute-start.17 = (bf16[32,2176]{1,0:T(8,128)(2,1)S(1)}, bf16[32,2176]{1,0:T(8,128)(2,1)S(1)}, u32[]{:S(2)}, u32[]{:S(2)}) collective-permute-start(bf16[32,2176]{1,0:T(8,128)(2,1)S(1)} %collective-permute-done.9), channel_id=1, source_target_pairs={{0,1},{1,0},{2,3},{3,2},{4,5},{5,4},{6,7},{7,6},{8,9},{9,8},{10,11... | collective-permute-start | bytes 417800 | tf_op jit(solution)/shard_map/ppermute | solution.py:193
  85.9 6.1 %collective-permute-start.11 = (bf16[32,2176]{1,0:T(8,128)(2,1)S(1)}, bf16[32,2176]{1,0:T(8,128)(2,1)S(1)}, u32[]{:S(2)}, u32[]{:S(2)}) collective-permute-start(bf16[32,2176]{1,0:T(8,128)(2,1)S(1)} %collective-permute-done.7), channel_id=1, source_target_pairs={{0,2},{2,0},{4,6},{6,4},{8,10},{10,8},{12,14},{14,12},{1,3},{3,1},... | collective-permute-start | bytes 417800 | tf_op jit(solution)/shard_map/ppermute | solution.py:184
  92.0 3.7 %collective-permute-start.15 = (bf16[32,2176]{1,0:T(8,128)(2,1)S(1)}, bf16[32,2176]{1,0:T(8,128)(2,1)S(1)}, u32[]{:S(2)}, u32[]{:S(2)}) collective-permute-start(bf16[32,2176]{1,0:T(8,128)(2,1)S(1)} %collective-permute-done.7), channel_id=1, source_target_pairs={{0,1},{1,0},{2,3},{3,2},{4,5},{5,4},{6,7},{7,6},{8,9},{9,8},{10,11... | collective-permute-start | bytes 417800 | tf_op jit(solution)/shard_map/ppermute | solution.py:193
  92.7 1.9 %collective-permute-start.14 = (bf16[32,2176]{1,0:T(8,128)(2,1)S(1)}, bf16[32,2176]{1,0:T(8,128)(2,1)S(1)}, u32[]{:S(2)}, u32[]{:S(2)}) collective-permute-start(bf16[32,2176]{1,0:T(8,128)(2,1)S(1)} %collective-permute-done.6), channel_id=1, source_target_pairs={{0,1},{1,0},{2,3},{3,2},{4,5},{5,4},{6,7},{7,6},{8,9},{9,8},{10,11... | collective-permute-start | bytes 417800 | tf_op jit(solution)/shard_map/ppermute | solution.py:193
  93.9 5.2 %collective-permute-start.20 = (bf16[32,2176]{1,0:T(8,128)(2,1)S(1)}, bf16[32,2176]{1,0:T(8,128)(2,1)S(1)}, u32[]{:S(2)}, u32[]{:S(2)}) collective-permute-start(bf16[32,2176]{1,0:T(8,128)(2,1)S(1)} %collective-permute-done.12), channel_id=1, source_target_pairs={{0,1},{1,0},{2,3},{3,2},{4,5},{5,4},{6,7},{7,6},{8,9},{9,8},{10,11... | collective-permute-start | bytes 417800 | tf_op jit(solution)/shard_map/ppermute | solution.py:193
  94.6 3.8 %collective-permute-start.19 = (bf16[32,2176]{1,0:T(8,128)(2,1)S(1)}, bf16[32,2176]{1,0:T(8,128)(2,1)S(1)}, u32[]{:S(2)}, u32[]{:S(2)}) collective-permute-start(bf16[32,2176]{1,0:T(8,128)(2,1)S(1)} %collective-permute-done.11), channel_id=1, source_target_pairs={{0,1},{1,0},{2,3},{3,2},{4,5},{5,4},{6,7},{7,6},{8,9},{9,8},{10,11... | collective-permute-start | bytes 417800 | tf_op jit(solution)/shard_map/ppermute | solution.py:193
  95.8 2.0 %collective-permute-start.18 = (bf16[32,2176]{1,0:T(8,128)(2,1)S(1)}, bf16[32,2176]{1,0:T(8,128)(2,1)S(1)}, u32[]{:S(2)}, u32[]{:S(2)}) collective-permute-start(bf16[32,2176]{1,0:T(8,128)(2,1)S(1)} %collective-permute-done.10), channel_id=1, source_target_pairs={{0,1},{1,0},{2,3},{3,2},{4,5},{5,4},{6,7},{7,6},{8,9},{9,8},{10,11... | collective-permute-start | bytes 417800 | tf_op jit(solution)/shard_map/ppermute | solution.py:193
  126.0 2.9 %collective-permute-start.21 = (bf16[2,4,32,2048]{3,2,0,1:T(8,128)(2,1)S(1)}, bf16[2,4,32,2048]{3,2,0,1:T(8,128)(2,1)S(1)}, u32[]{:S(2)}, u32[]{:S(2)}) collective-permute-start(bf16[2,4,32,2048]{3,2,0,1:T(8,128)(2,1)S(1)} %copy.100), channel_id=1, source_target_pairs={{0,1},{1,0},{2,3},{3,2},{4,5},{5,4},{6,7},{7,6},{8,9},{9,8},{10,11... | collective-permute-start | bytes 3145736 | tf_op jit(solution)/shard_map/ppermute | solution.py:193
  129.4 5.8 %collective-permute-start.26 = (bf16[2,32,1024]{2,1,0:T(8,128)(2,1)S(1)}, bf16[2,32,1024]{2,1,0:T(8,128)(2,1)S(1)}, u32[]{:S(2)}, u32[]{:S(2)}) collective-permute-start(bf16[2,32,1024]{2,1,0:T(8,128)(2,1)S(1)} %get-tuple-element.23), channel_id=1, source_target_pairs={{0,12},{2,14},{4,0},{6,2},{8,4},{10,6},{12,8},{14,10},{1,13},{3,15... | collective-permute-start | bytes 393224 | tf_op jit(solution)/shard_map/ppermute | solution.py:190
  130.7 8.3 %collective-permute-start.28 = (bf16[2,32,1024]{2,1,0:T(8,128)(2,1)S(1)}, bf16[2,32,1024]{2,1,0:T(8,128)(2,1)S(1)}, u32[]{:S(2)}, u32[]{:S(2)}) collective-permute-start(bf16[2,32,1024]{2,1,0:T(8,128)(2,1)S(1)} %get-tuple-element.24), channel_id=1, source_target_pairs={{0,4},{2,6},{4,8},{6,10},{8,12},{10,14},{12,0},{14,2},{1,5},{3,7},... | collective-permute-start | bytes 393224 | tf_op jit(solution)/shard_map/ppermute | solution.py:190
  131.5 13.0 %collective-permute-start.27 = (bf16[2,32,1024]{2,1,0:T(8,128)(2,1)S(1)}, bf16[2,32,1024]{2,1,0:T(8,128)(2,1)S(1)}, u32[]{:S(2)}, u32[]{:S(2)}) collective-permute-start(bf16[2,32,1024]{2,1,0:T(8,128)(2,1)S(1)} %get-tuple-element.25), channel_id=1, source_target_pairs={{0,8},{2,10},{4,12},{6,14},{8,0},{10,2},{12,4},{14,6},{1,9},{3,11}... | collective-permute-start | bytes 393224 | tf_op jit(solution)/shard_map/ppermute | solution.py:190
  132.3 12.9 %collective-permute-start.22 = (bf16[4,32,1024]{2,1,0:T(8,128)(2,1)S(1)}, bf16[4,32,1024]{2,1,0:T(8,128)(2,1)S(1)}, u32[]{:S(2)}, u32[]{:S(2)}) collective-permute-start(bf16[4,32,1024]{2,1,0:T(8,128)(2,1)S(1)} %slice_bitcast_fusion.2), channel_id=1, source_target_pairs={{0,2},{2,0},{4,6},{6,4},{8,10},{10,8},{12,14},{14,12},{1,3},{3,1},... | collective-permute-start | bytes 786440 | tf_op jit(solution)/shard_map/ppermute | solution.py:184
  144.5 4.3 %collective-permute-start.29 = (bf16[32,1024]{1,0:T(8,128)(2,1)S(1)}, bf16[32,1024]{1,0:T(8,128)(2,1)S(1)}, u32[]{:S(2)}, u32[]{:S(2)}) collective-permute-start(bf16[32,1024]{1,0:T(8,128)(2,1)S(1)} %fusion.40), channel_id=1, source_target_pairs={{0,2},{2,0},{4,6},{6,4},{8,10},{10,8},{12,14},{14,12},{1,3},{3,1},... | collective-permute-start | bytes 196616 | tf_op jit(solution)/shard_map/ppermute | solution.py:184
  145.3 4.7 %collective-permute-start.23 = (bf16[1,32,1024]{2,1,0:T(8,128)(2,1)S(1)}, bf16[1,32,1024]{2,1,0:T(8,128)(2,1)S(1)}, u32[]{:S(2)}, u32[]{:S(2)}) collective-permute-start(bf16[1,32,1024]{2,1,0:T(8,128)(2,1)S(1)} %get-tuple-element.33), channel_id=1, source_target_pairs={{0,12},{2,14},{4,0},{6,2},{8,4},{10,6},{12,8},{14,10},{1,13},{3,15... | collective-permute-start | bytes 196616 | tf_op jit(solution)/shard_map/ppermute | solution.py:190
  148.0 6.1 %collective-permute-start.25 = (bf16[1,32,1024]{2,1,0:T(8,128)(2,1)S(1)}, bf16[1,32,1024]{2,1,0:T(8,128)(2,1)S(1)}, u32[]{:S(2)}, u32[]{:S(2)}) collective-permute-start(bf16[1,32,1024]{2,1,0:T(8,128)(2,1)S(1)} %get-tuple-element.34), channel_id=1, source_target_pairs={{0,4},{2,6},{4,8},{6,10},{8,12},{10,14},{12,0},{14,2},{1,5},{3,7},... | collective-permute-start | bytes 196616 | tf_op jit(solution)/shard_map/ppermute | solution.py:190
  148.0 6.1 %collective-permute-start.24 = (bf16[1,32,1024]{2,1,0:T(8,128)(2,1)S(1)}, bf16[1,32,1024]{2,1,0:T(8,128)(2,1)S(1)}, u32[]{:S(2)}, u32[]{:S(2)}) collective-permute-start(bf16[1,32,1024]{2,1,0:T(8,128)(2,1)S(1)} %get-tuple-element.35), channel_id=1, source_target_pairs={{0,8},{2,10},{4,12},{6,14},{8,0},{10,2},{12,4},{14,6},{1,9},{3,11}... | collective-permute-start | bytes 196616 | tf_op jit(solution)/shard_map/ppermute | solution.py:190
  (9 other events, 84.0 us)

commit v2 on v1

v2 whole, which is shorter than its diff:
```python
import functools
import math

import jax
import jax.numpy as jnp
from jax import lax
from jax.experimental import pallas as pl
from jax.experimental.pallas import tpu as pltpu
from jax.sharding import PartitionSpec as P

HEAD_DIM = 128
LANES = 128
PART = 8
ROWS = 32
VMEM_LIMIT = 50 << 20
epsilon = 1e-06
masked_score = -1e30


def attend_kernel(fresh_ref, len_ref, k_ref, v_ref, o_ref):
    rows, positions, width = k_ref.shape[1:]
    heads = width // HEAD_DIM
    part = math.gcd(rows, PART)
    parts = rows // part
    group = heads * part
    q, key_new, value_new = (fresh_ref[0, n].astype(jnp.float32) for n in range(3))
    score_scale = 1.0 / math.sqrt(HEAD_DIM)
    head_of = lax.broadcasted_iota(jnp.int32, (part, width), 1) // HEAD_DIM
    which = lax.broadcasted_iota(jnp.int32, (group, positions), 0) % part
    order = [(g, h) for g in range(parts) for h in range(heads)]

    def stacked(v):
        return jnp.concatenate(
            [
                v[g * part : (g + 1) * part, h * HEAD_DIM : (h + 1) * HEAD_DIM]
                for g, h in order
            ],
            axis=0,
        )

    own = jnp.sum(stacked(q * key_new), axis=1, keepdims=True) * score_scale
    pieces = []
    for g in range(parts):
        mine = q[g * part : (g + 1) * part]
        spread = jnp.concatenate(
            [jnp.where(head_of == h, mine, 0.0) for h in range(heads)], axis=0
        ).astype(jnp.bfloat16)
        keys = k_ref[0, g * part : (g + 1) * part].reshape(part * positions, width)
        every = lax.dot_general(
            spread, keys, (((1,), (1,)), ((), ())), preferred_element_type=jnp.float32
        )
        scores = every[:, :positions]
        for row in range(1, part):
            scores = jnp.where(
                which == row, every[:, row * positions : (row + 1) * positions], scores
            )
        pieces.append(scores)
    scores = jnp.concatenate(pieces, axis=0) * score_scale
    lengths = len_ref[...]
    lengths = jnp.concatenate([lengths[g * part : (g + 1) * part] for g, h in order], axis=0)
    in_cache = lax.broadcasted_iota(jnp.int32, scores.shape, 1) < lengths
    scores = jnp.where(in_cache, scores, masked_score)
    top = jnp.maximum(jnp.max(scores, axis=1, keepdims=True), own)
    weights = jnp.where(in_cache, jnp.exp(scores - top), 0.0)
    own_weight = jnp.exp(own - top)
    total = jnp.sum(weights, axis=1, keepdims=True) + own_weight
    added = own_weight * stacked(value_new)
    pieces = []
    for g in range(parts):
        mine = weights[g * group : (g + 1) * group]
        blocks = jnp.concatenate(
            [jnp.where(which == row, mine, 0.0).astype(jnp.bfloat16) for row in range(part)],
            axis=1,
        )
        values = v_ref[0, g * part : (g + 1) * part].reshape(part * positions, width)
        summed = lax.dot_general(
            blocks, values, (((1,), (0,)), ((), ())), preferred_element_type=jnp.float32
        )
        pieces += [
            summed[h * part : (h + 1) * part, h * HEAD_DIM : (h + 1) * HEAD_DIM]
            for h in range(heads)
        ]
    attended = (jnp.concatenate(pieces, axis=0) + added) / total
    attended = jnp.concatenate(
        [
            jnp.concatenate(
                [
                    attended[(g * heads + h) * part : (g * heads + h + 1) * part]
                    for h in range(heads)
                ],
                axis=1,
            )
            for g in range(parts)
        ],
        axis=0,
    )
    o_ref[...] = attended.astype(jnp.bfloat16)


def attend(fresh, lengths, kv):
    _, n, positions, width = kv.shape
    rows = fresh.shape[2]
    return pl.pallas_call(
        attend_kernel,
        grid=(n // rows,),
        in_specs=[
            pl.BlockSpec((1, 3, rows, width), lambda i: (i, 0, 0, 0)),
            pl.BlockSpec((rows, 1), lambda i: (i, 0)),
            pl.BlockSpec((1, rows, positions, width), lambda i: (0, i, 0, 0)),
            pl.BlockSpec((1, rows, positions, width), lambda i: (1, i, 0, 0)),
        ],
        out_specs=pl.BlockSpec((rows, width), lambda i: (i, 0)),
        out_shape=jax.ShapeDtypeStruct((n, width), jnp.bfloat16),
        compiler_params=pltpu.CompilerParams(vmem_limit_bytes=28 << 20),
        cost_estimate=pl.CostEstimate(
            flops=4 * n * positions * width,
            bytes_accessed=4 * n * positions * width,
            transcendentals=0,
        ),
    )(fresh, lengths, kv, kv)


def pieces_of(size, most):
    if size % LANES:
        return [(0, size)]
    return [(at, min(most, size - at)) for at in range(0, size, most)]


def expert_kernel(count, outs, mine_ref, *refs):
    slots, (w_ref, d_ref), y_refs = refs[:count], refs[count : count + 2], refs[count + 2 :][:outs]
    x_ref, c_ref, h_ref, in_ref, down_ref, in_sem, down_sem = refs[count + 2 + outs :]
    each = slots[0].shape[0]
    _, width, units = w_ref.shape
    in_cuts, down_cuts = pieces_of(units, 256), pieces_of(width, 512)
    in_copies, down_copies = [], []
    for n, (at, size) in enumerate(in_cuts):
        for half in range(2):
            src, dst = w_ref.at[half], in_ref.at[half]
            if size < units:
                src, dst = src.at[:, pl.ds(at, size)], dst.at[:, pl.ds(at, size)]
            in_copies.append(pltpu.make_async_copy(src, dst, in_sem.at[n, half]))
    for n, (at, size) in enumerate(down_cuts):
        down_copies.append(
            pltpu.make_async_copy(
                d_ref.at[:, pl.ds(at, size)], down_ref.at[:, pl.ds(at, size)], down_sem.at[n]
            )
        )
    for copy in in_copies + down_copies:
        copy.start()
    for n, slot in enumerate(slots):
        place = pl.ds(n * each, each)
        x_ref[place, :] = slot[:, :width]
        gates = slot[:, width:].astype(jnp.float32)
        lane = lax.broadcasted_iota(jnp.int32, gates.shape, 1)
        chosen = jnp.where(lane == mine_ref[0], gates, 0.0)
        c_ref[place, :] = jnp.sum(chosen, axis=1, keepdims=True)

    def keep(n, gate, up):
        at, size = in_cuts[n]
        h_ref[:, at : at + size] = (gate / (1.0 + jnp.exp(-gate)) * up).astype(jnp.bfloat16)

    def give(n, y):
        at, size = down_cuts[n]
        y = (y.astype(jnp.bfloat16).astype(jnp.float32) * c_ref[...]).astype(jnp.bfloat16)
        rows = y.shape[0] // outs
        for m, out in enumerate(y_refs):
            out[:, at : at + size] = y[m * rows : (m + 1) * rows]

    held = None
    for n, (at, size) in enumerate(in_cuts):
        in_copies[2 * n].wait()
        in_copies[2 * n + 1].wait()
        place = slice(at, at + size)
        gate = jnp.dot(x_ref[...], in_ref[0, :, place], preferred_element_type=jnp.float32)
        up = jnp.dot(x_ref[...], in_ref[1, :, place], preferred_element_type=jnp.float32)
        if held is not None:
            keep(*held)
        held = (n, gate, up)
    keep(*held)
    held = None
    for n, (at, size) in enumerate(down_cuts):
        down_copies[n].wait()
        place = slice(at, at + size)
        y = jnp.dot(h_ref[...], down_ref[:, place], preferred_element_type=jnp.float32)
        if held is not None:
            give(*held)
        held = (n, y)
    give(*held)


def expert(slots, outs, mine, w_both, w_down):
    each, packed = slots[0].shape
    rows = each * len(slots)
    _, depth, units = w_both.shape
    width = w_down.shape[1]
    inside = pl.BlockSpec(memory_space=pltpu.VMEM)
    return pl.pallas_call(
        functools.partial(expert_kernel, len(slots), outs),
        in_specs=[pl.BlockSpec(memory_space=pltpu.SMEM)]
        + [inside] * len(slots)
        + [pl.BlockSpec(memory_space=pl.ANY)] * 2,
        out_specs=[inside] * outs,
        scratch_shapes=[
            pltpu.VMEM((rows, depth), jnp.bfloat16),
            pltpu.VMEM((rows, 1), jnp.float32),
            pltpu.VMEM((rows, units), jnp.bfloat16),
            pltpu.VMEM((2, depth, units), jnp.bfloat16),
            pltpu.VMEM((units, width), jnp.bfloat16),
            pltpu.SemaphoreType.DMA((len(pieces_of(units, 256)), 2)),
            pltpu.SemaphoreType.DMA((len(pieces_of(width, 512)),)),
        ],
        out_shape=[jax.ShapeDtypeStruct((rows // outs, width), jnp.bfloat16)] * outs,
        compiler_params=pltpu.CompilerParams(vmem_limit_bytes=VMEM_LIMIT),
        cost_estimate=pl.CostEstimate(
            flops=6 * rows * depth * units,
            bytes_accessed=2 * (3 * depth * units + 2 * rows * depth),
            transcendentals=rows * units,
        ),
    )(mine, *slots, w_both, w_down)


def local(
    hidden_in,
    row_counts,
    qkv_new,
    cache_len,
    kv_cache,
    w_out,
    moe_gain,
    w_in,
    w_down,
    route_ids,
    route_weight,
):
    wide = jnp.float32
    narrow = jnp.bfloat16
    tok_rows, feat_local = hidden_in.shape
    owners = lax.axis_size("ep")
    reps = lax.axis_size("rep")
    parts_seq = lax.axis_size("seq")
    width_local = kv_cache.shape[-1]
    positions = kv_cache.shape[3]
    share_rows = tok_rows // parts_seq
    attend_rows = owners * share_rows
    inner = 2 if owners % 2 == 0 else 1
    outer = owners // inner
    me = lax.axis_index("ep")
    outer_me, inner_me = me // inner, me % inner

    def across(v):
        return lax.ppermute(v, "ep", [(i, i ^ 1) for i in range(owners)])

    def along(v, k):
        pairs = [
            (i, (i // inner + k) % outer * inner + i % inner) for i in range(owners)
        ]
        return lax.ppermute(v, "ep", pairs)

    def other(v):
        return lax.ppermute(v, "rep", [(i, (i + 1) % reps) for i in range(reps)])

    def rows_of_seq(v, axis):
        return lax.dynamic_slice_in_dim(v, lax.axis_index("seq") * share_rows, share_rows, axis)

    sent = qkv_new.reshape(tok_rows, 3, owners, width_local).transpose(2, 1, 0, 3)
    fresh = lax.all_to_all(sent, "ep", split_axis=0, concat_axis=0, tiled=True)
    fresh = rows_of_seq(fresh, 2)
    tile = math.gcd(attend_rows, ROWS)
    if share_rows != tile:
        fresh = fresh.transpose(0, 2, 1, 3).reshape(attend_rows // tile, tile, 3, width_local)
        fresh = fresh.transpose(0, 2, 1, 3)

    w_both = w_in.transpose(0, 2, 1, 3)
    if inner == 2 and reps == 2:
        half = w_out.shape[0] // 2
        rep_first = lax.axis_index("rep") == 0
        w_mine = jnp.where(rep_first, w_out[:half], w_out[half:])
    else:
        w_mine = w_out
    fresh, w_both, w_mine = lax.optimization_barrier((fresh, w_both, w_mine))
    w_mine = across(w_mine) if inner == 2 else w_mine

    kv = kv_cache.reshape(2, attend_rows, positions, width_local)
    attended = attend(fresh, cache_len.reshape(attend_rows, 1), kv)
    attended, w_mine = lax.optimization_barrier((attended, w_mine))
    attended = attended.reshape(owners, share_rows, width_local)
    attended = lax.all_gather(attended, "seq", axis=1, tiled=True)

    attended = attended.reshape(outer, inner, tok_rows, width_local)
    if inner == 2:
        first = inner_me == 0
        kept = jnp.where(first, attended[:, 0], attended[:, 1])
        given = jnp.where(first, attended[:, 1], attended[:, 0])
        joined = jnp.concatenate([kept, across(given)], axis=2)
        if reps == 2:
            theirs = other(w_mine)
            both = jnp.concatenate(
                [jnp.where(rep_first, w_mine, theirs), jnp.where(rep_first, theirs, w_mine)],
                axis=0,
            )
        else:
            both = w_mine
        w_pair = jnp.concatenate([w_out, both], axis=0)
    else:
        joined, w_pair = attended[:, 0], w_out
    turned = lax.dynamic_slice_in_dim(
        jnp.concatenate([joined, joined], axis=0), outer_me, outer, 0
    )
    partial_out = jnp.dot(
        turned.reshape(outer * tok_rows, -1), w_pair, preferred_element_type=wide
    ).reshape(outer, tok_rows, feat_local)
    arrived = [along(partial_out[k].astype(narrow), k) for k in range(1, outer)]
    attn_out = partial_out[0]
    for part in arrived:
        attn_out = attn_out + part.astype(wide)
    residual = (hidden_in.astype(wide) + attn_out).astype(narrow)
    residual_wide = residual.astype(wide)

    is_live = jnp.arange(tok_rows, dtype=jnp.int32) < row_counts[0]
    experts_local = w_in.shape[0]
    expert_total = owners * reps * experts_local
    hits = route_ids[:, :, None] == jnp.arange(expert_total, dtype=jnp.int32)[None, None, :]
    hits = hits & is_live[:, None, None]
    coeffs = jnp.sum(jnp.where(hits, route_weight.astype(wide)[:, :, None], 0.0), axis=1)
    lanes = -(-expert_total // LANES) * LANES
    coeffs = jnp.pad(coeffs, ((0, 0), (0, lanes - expert_total))).astype(narrow)
    full_rows = lax.all_gather(residual, "seq", axis=1, tiled=True).astype(wide)
    width = full_rows.shape[1]
    inverse_rms = lax.rsqrt(jnp.mean(full_rows * full_rows, axis=1) + epsilon)
    normed = (full_rows * inverse_rms[:, None] * moe_gain).astype(narrow)
    packed = jnp.concatenate([normed, coeffs], axis=1)
    columns = [packed, across(packed)] if inner == 2 else [packed]
    ks = list(range(outer))
    groups = [ks[: outer // 2], ks[outer // 2 :]] if outer > 1 else [ks]
    gathered = [[along(c, k) if k else c for c in columns for k in group] for group in groups]
    first_expert = (me * reps + lax.axis_index("rep")) * experts_local

    def run_experts(slots):
        if reps == 2:
            slots = slots + [other(s) for s in slots]
        total = None
        for j in range(experts_local):
            mine = jnp.reshape(first_expert + j, (1,)).astype(jnp.int32)
            made = expert(slots, reps, mine, w_both[j], w_down[j])
            total = made if total is None else [t + m for t, m in zip(total, made)]
        if parts_seq > 1:
            total = [
                lax.psum_scatter(t.astype(wide), "seq", scatter_dimension=1, tiled=True).astype(
                    narrow
                )
                for t in total
            ]
        return [t.reshape(inner, -1, tok_rows, feat_local) for t in total]

    def over_reps(made):
        merged = made[0].astype(wide)
        return merged + other(made[1]).astype(wide) if reps == 2 else merged

    cut = feat_local // 2

    def pair(v, k):
        return along(v.astype(narrow), -k).astype(wide)

    if len(groups) == 2 and inner == 2:
        made = run_experts(gathered[0])
        made, late = lax.optimization_barrier((made, gathered[1]))
        early = over_reps(made)
        early_parts = [
            along(early[:, i].astype(narrow), -k) for i, k in enumerate(groups[0]) if k
        ]
        made = run_experts(late)
        made, early_parts = lax.optimization_barrier((made, early_parts))
        late_sum = over_reps(made)
        base = early[:, 0]
        for part in early_parts:
            base = base + part.astype(wide)
        right_far = across(
            jnp.concatenate([late_sum[1, :, :, cut:], base[None, 1, :, cut:]]).astype(narrow)
        ).astype(wide)
        left = base[..., :cut]
        for i, k in enumerate(groups[1]):
            left = left + pair(late_sum[:, i, :, :cut], k)
        right = base[0, :, cut:] + right_far[-1]
        for i, k in enumerate(groups[1]):
            right = right + pair(late_sum[0, i, :, cut:] + right_far[i], k)
        left = left[0] + across(left[1].astype(narrow)).astype(wide)
        moe_out = jnp.concatenate([left, right], axis=1)
    else:
        total = jnp.zeros((inner, tok_rows, feat_local), wide)
        for group, slots in zip(groups, gathered):
            made = over_reps(run_experts(slots))
            for i, k in enumerate(group):
                total = total + (pair(made[:, i], k) if k else made[:, i])
        moe_out = total[0]
        if inner == 2:
            moe_out = moe_out + across(total[1].astype(narrow)).astype(wide)
    return jnp.where(is_live[:, None], residual_wide + moe_out, 0.0).astype(narrow)


def solution(mesh):
    placed = (
        P(("grp", "ep", "rep"), "seq"),
        P(("grp", "ep", "rep")),
        P(("grp", "ep", "rep"), None, None),
        P("grp", ("rep", "seq")),
        P(None, "grp", ("rep", "seq"), None, "ep"),
        P("ep", "seq"),
        P(),
        P(("ep", "rep"), None, None, "seq"),
        P(("ep", "rep"), "seq", None),
        P(("grp", "ep", "rep"), None),
        P(("grp", "ep", "rep"), None),
    )
    return jax.shard_map(
        local, mesh=mesh, in_specs=placed, out_specs=P(("grp", "ep", "rep"), "seq"), check_vma=False
    )
```

time: 155 us -> 129 us (0.83)
  local copies, waits for them, and re-layouts: 35.1 us -> 13.6 us
  starting transfers between devices: 36.9 us -> 29.1 us
  waiting for transfers between devices: 44.3 us -> 49.6 us
  other arithmetic: 6.04 us -> 1.83 us
  Pallas kernels: 30.8 us -> 32.4 us
    unnamed x35 -> x13, local copies, waits for them, and re-layouts: 28.8 us -> 11.4 us
    ppermute x8 -> x5, starting transfers between devices: 11.1 us -> 3.25 us  [across(): return lax.ppermute(v, 'ep', [(i, i ^ 1) for i in range(owners)])]
    ppermute x12 -> x14, waiting for transfers between devices: 29.2 us -> 35.2 us  [along(): return lax.ppermute(v, 'ep', pairs)]
    ppermute x12 -> x14, starting transfers between devices: 13.1 us -> 16.8 us  [along(): return lax.ppermute(v, 'ep', pairs)]
    all_to_all x2 -> x1, starting transfers between devices: 10.6 us -> 7.25 us  [local(): fresh = lax.all_to_all(sent, 'ep', split_axis=0, concat_axis=0, tiled=True)]
    all_to_all x2 -> x1, waiting for transfers between devices: 3.1 us -> 0.27 us  [local(): fresh = lax.all_to_all(sent, 'ep', split_axis=0, concat_axis=0, tiled=True)]
    slice x5 -> x2, local copies, waits for them, and re-layouts: 1.91 us -> 0.04 us  [the longest x1 0.03 us: local(): arrived = [along(partial_out[k].astype(narrow), k) for k in range(1, outer)]]
    select_n x2, other arithmetic: 1.95 us -> 0.13 us  [the longest x1 0.07 us: local(): jnp.where(rep_first, w_mine, theirs)]
  transfers between devices with their start and end apart: 32 -> 31, of which waited for: 15 -> 15; matrix products, arithmetic and copies ran while one was open for 16% -> 9% of each run, Pallas kernels for 9% -> 25%
where the time goes in v2:
time: 129 us; the launch traced here: 128 us
  waiting for transfers between devices  49.6 us (38%)
  Pallas kernels  32.4 us (25%)
  starting transfers between devices  29.1 us (23%)
  local copies, waits for them, and re-layouts  13.6 us (11%)
  other arithmetic  1.83 us (1%)
    ppermute x14, waiting for transfers between devices, along(): return lax.ppermute(v, 'ep', pairs)  35.2 us
    pallas_call x2, Pallas kernels, expert(): pl.pallas_call(functools.partial(expert_kernel, len(slots), outs), in_spe...  17.9 us
    ppermute x14, starting transfers between devices, along(): return lax.ppermute(v, 'ep', pairs)  16.8 us
    pallas_call x1, Pallas kernels, attend(): pl.pallas_call(attend_kernel, grid=(n // rows,), in_specs=[pl.BlockSpec((...  14.5 us
    ppermute x5, waiting for transfers between devices, across(): return lax.ppermute(v, 'ep', [(i, i ^ 1) for i in range(owners)])  11.5 us
    unnamed x13, local copies, waits for them, and re-layouts  11.4 us
    all_to_all x1, starting transfers between devices, local(): fresh = lax.all_to_all(sent, 'ep', split_axis=0, concat_axis=0, tiled=True)  7.25 us
    ppermute x5, starting transfers between devices, across(): return lax.ppermute(v, 'ep', [(i, i ^ 1) for i in range(owners)])  3.25 us
  transfers between devices with their start and end apart: 31, of which 15 were waited for; matrix products, arithmetic and copies ran while one was open for 9% of the time, Pallas kernels for 25%

profile of v2, /device:TPU:0, one launch (start us, length us, event | category | flops | bytes accessed | tf_op | source)
XLA Modules:
  0.0 128.2 jit_solution(5965914855565354272)
XLA Ops:
  0.0 1.8 %copy.65 = bf16[3,4,8,8,256]{4,3,1,0,2:T(8,128)(2,1)} copy(bf16[3,4,8,8,256]{4,3,2,1,0:T(8,128)(2,1)} %bitcast.95) | data formatting | bytes 786432 | tf_op jit(solution)/shard_map/reshape | solution.py:265
  1.8 7.3 %all-to-all-start = ((bf16[8,3,32,256]{3,2,1,0:T(8,128)(2,1)}), bf16[8,3,32,256]{3,2,1,0:T(8,128)(2,1)S(1)}, u32[]{:S(2)}, u32[]{:S(2)}) async-start(bf16[8,3,32,256]{3,2,1,0:T(8,128)(2,1)} %bitcast.81), calls=%async_computation | async-start | bytes 786432 | tf_op jit(solution)/shard_map/all_to_all | solution.py:266
  9.1 11.3 %copy.64 = bf16[1,2048,2,1408]{3,1,2,0:T(8,128)(2,1)} copy(bf16[1,2048,2,1408]{3,2,1,0:T(2,128)(2,1)} %param.18) | data formatting | bytes 23068672 | tf_op args[7]
  20.7 1.8 %collective-permute-start = (bf16[128,2048]{1,0:T(8,128)(2,1)S(1)}, bf16[128,2048]{1,0:T(8,128)(2,1)S(1)}, u32[]{:S(2)}, u32[]{:S(2)}) collective-permute-start(bf16[128,2048]{1,0:T(8,128)(2,1)S(1)} %slice_select_fusion), channel_id=1, source_target_pairs={{0,2},{2,0},{4,6},{6,4},{8,10},{10,8},{12,14},{14,12},{1,3},{3,1},... | collective-permute-start | bytes 1572872 | tf_op jit(solution)/shard_map/ppermute | solution.py:251
  23.4 14.5 %shard_map.109 = bf16[256,256]{1,0:T(8,128)(2,1)S(1)} custom-call(bf16[8,3,32,256]{3,2,1,0:T(8,128)(2,1)S(1)} %all-to-all-done.fresh_ref, s32[256,1]{1,0:T(8,128)S(1)} %reshape.77.len_ref, bf16[2,256,128,256]{3,2,1,0:T(8,128)(2,1)} %bitcast.89, bf16[2,256,128,256]{3,2,1,0:T(8,128)(2,1)} %bitcast.90), custom_call_target="tpu_custom_call" | custom-call | flops 33554432 | bytes 33554432 | tf_op jit(solution)/shard_map/pallas_call | solution.py:103
  38.3 4.3 %collective-permute-done.1 = bf16[4,32,256]{2,1,0:T(8,128)(2,1)S(1)} collective-permute-done((bf16[4,32,256]{2,1,0:T(8,128)(2,1)S(1)}, bf16[4,32,256]{2,1,0:T(8,128)(2,1)S(1)}, u32[]{:S(2)}, u32[]{:S(2)}) %collective-permute-start.1) | collective-permute-done | bytes 65568 | tf_op jit(solution)/shard_map/ppermute | solution.py:251
  42.8 0.7 fusion.39
  43.5 1.5 %collective-permute-start.3 = (bf16[32,2048]{1,0:T(8,128)(2,1)S(1)}, bf16[32,2048]{1,0:T(8,128)(2,1)S(1)}, u32[]{:S(2)}, u32[]{:S(2)}) collective-permute-start(bf16[32,2048]{1,0:T(8,128)(2,1)S(1)} %get-tuple-element.51), channel_id=1, source_target_pairs={{0,4},{2,6},{4,8},{6,10},{8,12},{10,14},{12,0},{14,2},{1,5},{3,7},... | collective-permute-start | bytes 393224 | tf_op jit(solution)/shard_map/ppermute | solution.py:257
  45.0 2.4 %collective-permute-start.5 = (bf16[32,2048]{1,0:T(8,128)(2,1)S(1)}, bf16[32,2048]{1,0:T(8,128)(2,1)S(1)}, u32[]{:S(2)}, u32[]{:S(2)}) collective-permute-start(bf16[32,2048]{1,0:T(8,128)(2,1)S(1)} %get-tuple-element.52), channel_id=1, source_target_pairs={{0,12},{2,14},{4,0},{6,2},{8,4},{10,6},{12,8},{14,10},{1,13},{3,15... | collective-permute-start | bytes 393224 | tf_op jit(solution)/shard_map/ppermute | solution.py:257
  47.4 0.6 collective-permute-start.4
  48.1 3.7 %collective-permute-done.3 = bf16[32,2048]{1,0:T(8,128)(2,1)S(1)} collective-permute-done((bf16[32,2048]{1,0:T(8,128)(2,1)S(1)}, bf16[32,2048]{1,0:T(8,128)(2,1)S(1)}, u32[]{:S(2)}, u32[]{:S(2)}) %collective-permute-start.3) | collective-permute-done | bytes 131104 | tf_op jit(solution)/shard_map/ppermute | solution.py:257
  51.7 0.9 collective-permute-done.5
  52.6 6.2 %collective-permute-done.4 = bf16[32,2048]{1,0:T(8,128)(2,1)S(1)} collective-permute-done((bf16[32,2048]{1,0:T(8,128)(2,1)S(1)}, bf16[32,2048]{1,0:T(8,128)(2,1)S(1)}, u32[]{:S(2)}, u32[]{:S(2)}) %collective-permute-start.4) | collective-permute-done | bytes 131104 | tf_op jit(solution)/shard_map/ppermute | solution.py:257
  59.6 5.2 %collective-permute-done.7.refs_2_ = bf16[32,2176]{1,0:T(8,128)(2,1)S(1)} collective-permute-done((bf16[32,2176]{1,0:T(8,128)(2,1)S(1)}, bf16[32,2176]{1,0:T(8,128)(2,1)S(1)}, u32[]{:S(2)}, u32[]{:S(2)}) %collective-permute-start.7) | collective-permute-done | bytes 139296 | tf_op jit(solution)/shard_map/ppermute | solution.py:251
  64.8 0.5 collective-permute-start.11
  65.3 1.3 %collective-permute-done.6.refs_1_ = bf16[32,2176]{1,0:T(8,128)(2,1)S(1)} collective-permute-done((bf16[32,2176]{1,0:T(8,128)(2,1)S(1)}, bf16[32,2176]{1,0:T(8,128)(2,1)S(1)}, u32[]{:S(2)}, u32[]{:S(2)}) %collective-permute-start.6) | collective-permute-done | bytes 139296 | tf_op jit(solution)/shard_map/ppermute | solution.py:257
  66.7 5.0 %collective-permute-done.8.refs_3_ = bf16[32,2176]{1,0:T(8,128)(2,1)S(1)} collective-permute-done((bf16[32,2176]{1,0:T(8,128)(2,1)S(1)}, bf16[32,2176]{1,0:T(8,128)(2,1)S(1)}, u32[]{:S(2)}, u32[]{:S(2)}) %collective-permute-start.8) | collective-permute-done | bytes 139296 | tf_op jit(solution)/shard_map/ppermute | solution.py:257
  71.8 4.3 %collective-permute-start.16 = (bf16[32,2176]{1,0:T(8,128)(2,1)S(1)}, bf16[32,2176]{1,0:T(8,128)(2,1)S(1)}, u32[]{:S(2)}, u32[]{:S(2)}) collective-permute-start(bf16[32,2176]{1,0:T(8,128)(2,1)S(1)} %collective-permute-done.7.refs_2_), channel_id=1, source_target_pairs={{0,12},{2,14},{4,0},{6,2},{8,4},{10,6},{12,8},{14,10},{1,13},{3,15... | collective-permute-start | bytes 417800 | tf_op jit(solution)/shard_map/ppermute | solution.py:257
  76.1 8.9 %shard_map.110 = (bf16[128,2048]{1,0:T(8,128)(2,1)S(1)}, bf16[128,2048]{1,0:T(8,128)(2,1)S(1)}) custom-call(s32[1]{0:T(128)} %bitcast.11.mine_ref, bf16[32,2176]{1,0:T(8,128)(2,1)S(1)} %fusion.19.refs_0_, bf16[32,2176]{1,0:T(8,128)(2,1)S(1)} %collective-permute-done.6.refs_1_, bf16[32,2176]{1,0:T(8,128)(2,1)S(1)} %collective-permute-done.7.refs_2_, ...), custom_call_target="tpu_custom_call" | custom-call | flops 4429185024 | bytes 19398656 | tf_op jit(solution)/shard_map/pallas_call | solution.py:197
  85.1 5.6 %collective-permute-done.15.refs_2_ = bf16[32,2176]{1,0:T(8,128)(2,1)S(1)} collective-permute-done((bf16[32,2176]{1,0:T(8,128)(2,1)S(1)}, bf16[32,2176]{1,0:T(8,128)(2,1)S(1)}, u32[]{:S(2)}, u32[]{:S(2)}) %collective-permute-start.15) | collective-permute-done | bytes 139296 | tf_op jit(solution)/shard_map/ppermute | solution.py:257
  90.8 0.5 collective-permute-start.18
  91.9 0.8 collective-permute-done.17
  92.8 4.3 %collective-permute-start.22 = (bf16[2,32,2048]{2,1,0:T(8,128)(2,1)S(1)}, bf16[2,32,2048]{2,1,0:T(8,128)(2,1)S(1)}, u32[]{:S(2)}, u32[]{:S(2)}) collective-permute-start(bf16[2,32,2048]{2,1,0:T(8,128)(2,1)S(1)} %fusion.13), channel_id=1, source_target_pairs={{0,12},{2,14},{4,0},{6,2},{8,4},{10,6},{12,8},{14,10},{1,13},{3,15... | collective-permute-start | bytes 786440 | tf_op jit(solution)/shard_map/ppermute | solution.py:257
  97.2 8.9 %shard_map.111 = (bf16[128,2048]{1,0:T(8,128)(2,1)S(1)}, bf16[128,2048]{1,0:T(8,128)(2,1)S(1)}) custom-call(s32[1]{0:T(128)} %bitcast.11.mine_ref, bf16[32,2176]{1,0:T(8,128)(2,1)S(1)} %collective-permute-done.13.refs_0_, bf16[32,2176]{1,0:T(8,128)(2,1)S(1)} %collective-permute-done.14.refs_1_, bf16[32,2176]{1,0:T(8,128)(2,1)S(1)} %collective-permute-done.15.refs_2_, ...), custom_call_target="tpu_custom_call" | custom-call | flops 4429185024 | bytes 19398656 | tf_op jit(solution)/shard_map/pallas_call | solution.py:197
  106.4 1.8 %collective-permute-done.23 = bf16[2,2,32,2048]{3,2,0,1:T(8,128)(2,1)S(1)} collective-permute-done((bf16[2,2,32,2048]{3,2,0,1:T(8,128)(2,1)S(1)}, bf16[2,2,32,2048]{3,2,0,1:T(8,128)(2,1)S(1)}, u32[]{:S(2)}, u32[]{:S(2)}) %collective-permute-start.23) | collective-permute-done | bytes 524320 | tf_op jit(solution)/shard_map/ppermute | solution.py:260
  108.5 1.7 %collective-permute-start.25 = (bf16[2,32,1024]{2,1,0:T(8,128)(2,1)S(1)}, bf16[2,32,1024]{2,1,0:T(8,128)(2,1)S(1)}, u32[]{:S(2)}, u32[]{:S(2)}) collective-permute-start(bf16[2,32,1024]{2,1,0:T(8,128)(2,1)S(1)} %get-tuple-element.50), channel_id=1, source_target_pairs={{0,4},{2,6},{4,8},{6,10},{8,12},{10,14},{12,0},{14,2},{1,5},{3,7},... | collective-permute-start | bytes 393224 | tf_op jit(solution)/shard_map/ppermute | solution.py:257
  110.6 8.4 %collective-permute-done.24 = bf16[2,32,1024]{2,1,0:T(8,128)(2,1)S(1)} collective-permute-done((bf16[2,32,1024]{2,1,0:T(8,128)(2,1)S(1)}, bf16[2,32,1024]{2,1,0:T(8,128)(2,1)S(1)}, u32[]{:S(2)}, u32[]{:S(2)}) %collective-permute-start.24) | collective-permute-done | bytes 131104 | tf_op jit(solution)/shard_map/ppermute | solution.py:257
  119.5 1.8 %collective-permute-start.28 = (bf16[32,1024]{1,0:T(8,128)(2,1)S(1)}, bf16[32,1024]{1,0:T(8,128)(2,1)S(1)}, u32[]{:S(2)}, u32[]{:S(2)}) collective-permute-start(bf16[32,1024]{1,0:T(8,128)(2,1)S(1)} %get-tuple-element.43), channel_id=1, source_target_pairs={{0,8},{2,10},{4,12},{6,14},{8,0},{10,2},{12,4},{14,6},{1,9},{3,11}... | collective-permute-start | bytes 196616 | tf_op jit(solution)/shard_map/ppermute | solution.py:257
  121.4 2.0 %collective-permute-done.26 = bf16[32,1024]{1,0:T(8,128)(2,1)S(1)} collective-permute-done((bf16[32,1024]{1,0:T(8,128)(2,1)S(1)}, bf16[32,1024]{1,0:T(8,128)(2,1)S(1)}, u32[]{:S(2)}, u32[]{:S(2)}) %collective-permute-start.26) | collective-permute-done | bytes 65568 | tf_op jit(solution)/shard_map/ppermute | solution.py:251
  123.4 1.5 %collective-permute-done.28 = bf16[32,1024]{1,0:T(8,128)(2,1)S(1)} collective-permute-done((bf16[32,1024]{1,0:T(8,128)(2,1)S(1)}, bf16[32,1024]{1,0:T(8,128)(2,1)S(1)}, u32[]{:S(2)}, u32[]{:S(2)}) %collective-permute-start.28) | collective-permute-done | bytes 65568 | tf_op jit(solution)/shard_map/ppermute | solution.py:257
  125.0 2.5 %collective-permute-done.29 = bf16[32,1024]{1,0:T(8,128)(2,1)S(1)} collective-permute-done((bf16[32,1024]{1,0:T(8,128)(2,1)S(1)}, bf16[32,1024]{1,0:T(8,128)(2,1)S(1)}, u32[]{:S(2)}, u32[]{:S(2)}) %collective-permute-start.29) | collective-permute-done | bytes 65568 | tf_op jit(solution)/shard_map/ppermute | solution.py:257
  127.5 0.7 fusion.12
  (80 shorter events, 4.3 us)
Async XLA Ops:
  1.8 18.9 %all-to-all-start = ((bf16[8,3,32,256]{3,2,1,0:T(8,128)(2,1)}), bf16[8,3,32,256]{3,2,1,0:T(8,128)(2,1)S(1)}, u32[]{:S(2)}, u32[]{:S(2)}) async-start(bf16[8,3,32,256]{3,2,1,0:T(8,128)(2,1)} %bitcast.81), calls=%async_computation | async-start | bytes 786432 | tf_op jit(solution)/shard_map/all_to_all | solution.py:266
  20.7 17.1 %collective-permute-start = (bf16[128,2048]{1,0:T(8,128)(2,1)S(1)}, bf16[128,2048]{1,0:T(8,128)(2,1)S(1)}, u32[]{:S(2)}, u32[]{:S(2)}) collective-permute-start(bf16[128,2048]{1,0:T(8,128)(2,1)S(1)} %slice_select_fusion), channel_id=1, source_target_pairs={{0,2},{2,0},{4,6},{6,4},{8,10},{10,8},{12,14},{14,12},{1,3},{3,1},... | collective-permute-start | bytes 1572872 | tf_op jit(solution)/shard_map/ppermute | solution.py:251
  37.9 4.8 %collective-permute-start.2 = (bf16[128,2048]{1,0:T(8,128)(2,1)S(1)}, bf16[128,2048]{1,0:T(8,128)(2,1)S(1)}, u32[]{:S(2)}, u32[]{:S(2)}) collective-permute-start(bf16[128,2048]{1,0:T(8,128)(2,1)S(1)} %collective-permute-done), channel_id=1, source_target_pairs={{0,1},{1,0},{2,3},{3,2},{4,5},{5,4},{6,7},{7,6},{8,9},{9,8},{10,11... | collective-permute-start | bytes 1572872 | tf_op jit(solution)/shard_map/ppermute | solution.py:260
  38.0 4.6 %collective-permute-start.1 = (bf16[4,32,256]{2,1,0:T(8,128)(2,1)S(1)}, bf16[4,32,256]{2,1,0:T(8,128)(2,1)S(1)}, u32[]{:S(2)}, u32[]{:S(2)}) collective-permute-start(bf16[4,32,256]{2,1,0:T(8,128)(2,1)S(1)} %fusion.31), channel_id=1, source_target_pairs={{0,2},{2,0},{4,6},{6,4},{8,10},{10,8},{12,14},{14,12},{1,3},{3,1},... | collective-permute-start | bytes 196616 | tf_op jit(solution)/shard_map/ppermute | solution.py:251
  42.7 16.3 %copy-start.2 = (f32[2048]{0:T(1024)S(1)}, f32[2048]{0:T(1024)}, u32[]{:S(2)}) copy-start(f32[2048]{0:T(1024)} %param.17) | copy-start | bytes 24580
  43.5 8.3 %collective-permute-start.3 = (bf16[32,2048]{1,0:T(8,128)(2,1)S(1)}, bf16[32,2048]{1,0:T(8,128)(2,1)S(1)}, u32[]{:S(2)}, u32[]{:S(2)}) collective-permute-start(bf16[32,2048]{1,0:T(8,128)(2,1)S(1)} %get-tuple-element.51), channel_id=1, source_target_pairs={{0,4},{2,6},{4,8},{6,10},{8,12},{10,14},{12,0},{14,2},{1,5},{3,7},... | collective-permute-start | bytes 393224 | tf_op jit(solution)/shard_map/ppermute | solution.py:257
  45.0 7.6 %collective-permute-start.5 = (bf16[32,2048]{1,0:T(8,128)(2,1)S(1)}, bf16[32,2048]{1,0:T(8,128)(2,1)S(1)}, u32[]{:S(2)}, u32[]{:S(2)}) collective-permute-start(bf16[32,2048]{1,0:T(8,128)(2,1)S(1)} %get-tuple-element.52), channel_id=1, source_target_pairs={{0,12},{2,14},{4,0},{6,2},{8,4},{10,6},{12,8},{14,10},{1,13},{3,15... | collective-permute-start | bytes 393224 | tf_op jit(solution)/shard_map/ppermute | solution.py:257
  47.4 11.5 %collective-permute-start.4 = (bf16[32,2048]{1,0:T(8,128)(2,1)S(1)}, bf16[32,2048]{1,0:T(8,128)(2,1)S(1)}, u32[]{:S(2)}, u32[]{:S(2)}) collective-permute-start(bf16[32,2048]{1,0:T(8,128)(2,1)S(1)} %get-tuple-element.53), channel_id=1, source_target_pairs={{0,8},{2,10},{4,12},{6,14},{8,0},{10,2},{12,4},{14,6},{1,9},{3,11}... | collective-permute-start | bytes 393224 | tf_op jit(solution)/shard_map/ppermute | solution.py:257
  59.2 5.6 %collective-permute-start.7 = (bf16[32,2176]{1,0:T(8,128)(2,1)S(1)}, bf16[32,2176]{1,0:T(8,128)(2,1)S(1)}, u32[]{:S(2)}, u32[]{:S(2)}) collective-permute-start(bf16[32,2176]{1,0:T(8,128)(2,1)S(1)} %fusion.19.refs_0_), channel_id=1, source_target_pairs={{0,2},{2,0},{4,6},{6,4},{8,10},{10,8},{12,14},{14,12},{1,3},{3,1},... | collective-permute-start | bytes 417800 | tf_op jit(solution)/shard_map/ppermute | solution.py:251
  59.6 7.0 %collective-permute-start.6 = (bf16[32,2176]{1,0:T(8,128)(2,1)S(1)}, bf16[32,2176]{1,0:T(8,128)(2,1)S(1)}, u32[]{:S(2)}, u32[]{:S(2)}) collective-permute-start(bf16[32,2176]{1,0:T(8,128)(2,1)S(1)} %fusion.19.refs_0_), channel_id=1, source_target_pairs={{0,4},{2,6},{4,8},{6,10},{8,12},{10,14},{12,0},{14,2},{1,5},{3,7},... | collective-permute-start | bytes 417800 | tf_op jit(solution)/shard_map/ppermute | solution.py:257
  64.8 6.9 %collective-permute-start.8 = (bf16[32,2176]{1,0:T(8,128)(2,1)S(1)}, bf16[32,2176]{1,0:T(8,128)(2,1)S(1)}, u32[]{:S(2)}, u32[]{:S(2)}) collective-permute-start(bf16[32,2176]{1,0:T(8,128)(2,1)S(1)} %collective-permute-done.7.refs_2_), channel_id=1, source_target_pairs={{0,4},{2,6},{4,8},{6,10},{8,12},{10,14},{12,0},{14,2},{1,5},{3,7},... | collective-permute-start | bytes 417800 | tf_op jit(solution)/shard_map/ppermute | solution.py:257
  64.8 6.9 %collective-permute-start.9 = (bf16[32,2176]{1,0:T(8,128)(2,1)S(1)}, bf16[32,2176]{1,0:T(8,128)(2,1)S(1)}, u32[]{:S(2)}, u32[]{:S(2)}) collective-permute-start(bf16[32,2176]{1,0:T(8,128)(2,1)S(1)} %fusion.19.refs_0_), channel_id=1, source_target_pairs={{0,1},{1,0},{2,3},{3,2},{4,5},{5,4},{6,7},{7,6},{8,9},{9,8},{10,11... | collective-permute-start | bytes 417800 | tf_op jit(solution)/shard_map/ppermute | solution.py:260
  64.8 6.9 %collective-permute-start.11 = (bf16[32,2176]{1,0:T(8,128)(2,1)S(1)}, bf16[32,2176]{1,0:T(8,128)(2,1)S(1)}, u32[]{:S(2)}, u32[]{:S(2)}) collective-permute-start(bf16[32,2176]{1,0:T(8,128)(2,1)S(1)} %collective-permute-done.7.refs_2_), channel_id=1, source_target_pairs={{0,1},{1,0},{2,3},{3,2},{4,5},{5,4},{6,7},{7,6},{8,9},{9,8},{10,11... | collective-permute-start | bytes 417800 | tf_op jit(solution)/shard_map/ppermute | solution.py:260
  66.7 9.4 %collective-permute-start.10 = (bf16[32,2176]{1,0:T(8,128)(2,1)S(1)}, bf16[32,2176]{1,0:T(8,128)(2,1)S(1)}, u32[]{:S(2)}, u32[]{:S(2)}) collective-permute-start(bf16[32,2176]{1,0:T(8,128)(2,1)S(1)} %collective-permute-done.6.refs_1_), channel_id=1, source_target_pairs={{0,1},{1,0},{2,3},{3,2},{4,5},{5,4},{6,7},{7,6},{8,9},{9,8},{10,11... | collective-permute-start | bytes 417800 | tf_op jit(solution)/shard_map/ppermute | solution.py:260
  71.7 4.4 %collective-permute-start.12 = (bf16[32,2176]{1,0:T(8,128)(2,1)S(1)}, bf16[32,2176]{1,0:T(8,128)(2,1)S(1)}, u32[]{:S(2)}, u32[]{:S(2)}) collective-permute-start(bf16[32,2176]{1,0:T(8,128)(2,1)S(1)} %collective-permute-done.8.refs_3_), channel_id=1, source_target_pairs={{0,1},{1,0},{2,3},{3,2},{4,5},{5,4},{6,7},{7,6},{8,9},{9,8},{10,11... | collective-permute-start | bytes 417800 | tf_op jit(solution)/shard_map/ppermute | solution.py:260
  71.7 13.4 %collective-permute-start.14 = (bf16[32,2176]{1,0:T(8,128)(2,1)S(1)}, bf16[32,2176]{1,0:T(8,128)(2,1)S(1)}, u32[]{:S(2)}, u32[]{:S(2)}) collective-permute-start(bf16[32,2176]{1,0:T(8,128)(2,1)S(1)} %fusion.19.refs_0_), channel_id=1, source_target_pairs={{0,12},{2,14},{4,0},{6,2},{8,4},{10,6},{12,8},{14,10},{1,13},{3,15... | collective-permute-start | bytes 417800 | tf_op jit(solution)/shard_map/ppermute | solution.py:257
  71.7 13.4 %collective-permute-start.13 = (bf16[32,2176]{1,0:T(8,128)(2,1)S(1)}, bf16[32,2176]{1,0:T(8,128)(2,1)S(1)}, u32[]{:S(2)}, u32[]{:S(2)}) collective-permute-start(bf16[32,2176]{1,0:T(8,128)(2,1)S(1)} %fusion.19.refs_0_), channel_id=1, source_target_pairs={{0,8},{2,10},{4,12},{6,14},{8,0},{10,2},{12,4},{14,6},{1,9},{3,11}... | collective-permute-start | bytes 417800 | tf_op jit(solution)/shard_map/ppermute | solution.py:257
  71.8 13.3 %collective-permute-start.16 = (bf16[32,2176]{1,0:T(8,128)(2,1)S(1)}, bf16[32,2176]{1,0:T(8,128)(2,1)S(1)}, u32[]{:S(2)}, u32[]{:S(2)}) collective-permute-start(bf16[32,2176]{1,0:T(8,128)(2,1)S(1)} %collective-permute-done.7.refs_2_), channel_id=1, source_target_pairs={{0,12},{2,14},{4,0},{6,2},{8,4},{10,6},{12,8},{14,10},{1,13},{3,15... | collective-permute-start | bytes 417800 | tf_op jit(solution)/shard_map/ppermute | solution.py:257
  76.1 14.6 %collective-permute-start.15 = (bf16[32,2176]{1,0:T(8,128)(2,1)S(1)}, bf16[32,2176]{1,0:T(8,128)(2,1)S(1)}, u32[]{:S(2)}, u32[]{:S(2)}) collective-permute-start(bf16[32,2176]{1,0:T(8,128)(2,1)S(1)} %collective-permute-done.7.refs_2_), channel_id=1, source_target_pairs={{0,8},{2,10},{4,12},{6,14},{8,0},{10,2},{12,4},{14,6},{1,9},{3,11}... | collective-permute-start | bytes 417800 | tf_op jit(solution)/shard_map/ppermute | solution.py:257
  90.7 2.0 %collective-permute-start.17 = (bf16[2,2,32,2048]{3,2,0,1:T(8,128)(2,1)S(1)}, bf16[2,2,32,2048]{3,2,0,1:T(8,128)(2,1)S(1)}, u32[]{:S(2)}, u32[]{:S(2)}) collective-permute-start(bf16[2,2,32,2048]{3,2,0,1:T(8,128)(2,1)S(1)} %copy.53), channel_id=1, source_target_pairs={{0,1},{1,0},{2,3},{3,2},{4,5},{5,4},{6,7},{7,6},{8,9},{9,8},{10,11... | collective-permute-start | bytes 1572872 | tf_op jit(solution)/shard_map/ppermute | solution.py:260
  90.8 6.4 %collective-permute-start.18 = (bf16[32,2176]{1,0:T(8,128)(2,1)S(1)}, bf16[32,2176]{1,0:T(8,128)(2,1)S(1)}, u32[]{:S(2)}, u32[]{:S(2)}) collective-permute-start(bf16[32,2176]{1,0:T(8,128)(2,1)S(1)} %collective-permute-done.13.refs_0_), channel_id=1, source_target_pairs={{0,1},{1,0},{2,3},{3,2},{4,5},{5,4},{6,7},{7,6},{8,9},{9,8},{10,11... | collective-permute-start | bytes 417800 | tf_op jit(solution)/shard_map/ppermute | solution.py:260
  91.3 5.9 %collective-permute-start.19 = (bf16[32,2176]{1,0:T(8,128)(2,1)S(1)}, bf16[32,2176]{1,0:T(8,128)(2,1)S(1)}, u32[]{:S(2)}, u32[]{:S(2)}) collective-permute-start(bf16[32,2176]{1,0:T(8,128)(2,1)S(1)} %collective-permute-done.14.refs_1_), channel_id=1, source_target_pairs={{0,1},{1,0},{2,3},{3,2},{4,5},{5,4},{6,7},{7,6},{8,9},{9,8},{10,11... | collective-permute-start | bytes 417800 | tf_op jit(solution)/shard_map/ppermute | solution.py:260
  91.4 5.8 %collective-permute-start.20 = (bf16[32,2176]{1,0:T(8,128)(2,1)S(1)}, bf16[32,2176]{1,0:T(8,128)(2,1)S(1)}, u32[]{:S(2)}, u32[]{:S(2)}) collective-permute-start(bf16[32,2176]{1,0:T(8,128)(2,1)S(1)} %collective-permute-done.15.refs_2_), channel_id=1, source_target_pairs={{0,1},{1,0},{2,3},{3,2},{4,5},{5,4},{6,7},{7,6},{8,9},{9,8},{10,11... | collective-permute-start | bytes 417800 | tf_op jit(solution)/shard_map/ppermute | solution.py:260
  91.8 5.4 %collective-permute-start.21 = (bf16[32,2176]{1,0:T(8,128)(2,1)S(1)}, bf16[32,2176]{1,0:T(8,128)(2,1)S(1)}, u32[]{:S(2)}, u32[]{:S(2)}) collective-permute-start(bf16[32,2176]{1,0:T(8,128)(2,1)S(1)} %collective-permute-done.16.refs_3_), channel_id=1, source_target_pairs={{0,1},{1,0},{2,3},{3,2},{4,5},{5,4},{6,7},{7,6},{8,9},{9,8},{10,11... | collective-permute-start | bytes 417800 | tf_op jit(solution)/shard_map/ppermute | solution.py:260
  92.8 13.3 %collective-permute-start.22 = (bf16[2,32,2048]{2,1,0:T(8,128)(2,1)S(1)}, bf16[2,32,2048]{2,1,0:T(8,128)(2,1)S(1)}, u32[]{:S(2)}, u32[]{:S(2)}) collective-permute-start(bf16[2,32,2048]{2,1,0:T(8,128)(2,1)S(1)} %fusion.13), channel_id=1, source_target_pairs={{0,12},{2,14},{4,0},{6,2},{8,4},{10,6},{12,8},{14,10},{1,13},{3,15... | collective-permute-start | bytes 786440 | tf_op jit(solution)/shard_map/ppermute | solution.py:257
  106.2 2.0 %collective-permute-start.23 = (bf16[2,2,32,2048]{3,2,0,1:T(8,128)(2,1)S(1)}, bf16[2,2,32,2048]{3,2,0,1:T(8,128)(2,1)S(1)}, u32[]{:S(2)}, u32[]{:S(2)}) collective-permute-start(bf16[2,2,32,2048]{3,2,0,1:T(8,128)(2,1)S(1)} %copy.55), channel_id=1, source_target_pairs={{0,1},{1,0},{2,3},{3,2},{4,5},{5,4},{6,7},{7,6},{8,9},{9,8},{10,11... | collective-permute-start | bytes 1572872 | tf_op jit(solution)/shard_map/ppermute | solution.py:260
  108.4 10.6 %collective-permute-start.24 = (bf16[2,32,1024]{2,1,0:T(8,128)(2,1)S(1)}, bf16[2,32,1024]{2,1,0:T(8,128)(2,1)S(1)}, u32[]{:S(2)}, u32[]{:S(2)}) collective-permute-start(bf16[2,32,1024]{2,1,0:T(8,128)(2,1)S(1)} %get-tuple-element.49), channel_id=1, source_target_pairs={{0,8},{2,10},{4,12},{6,14},{8,0},{10,2},{12,4},{14,6},{1,9},{3,11}... | collective-permute-start | bytes 393224 | tf_op jit(solution)/shard_map/ppermute | solution.py:257
  108.5 10.6 %collective-permute-start.25 = (bf16[2,32,1024]{2,1,0:T(8,128)(2,1)S(1)}, bf16[2,32,1024]{2,1,0:T(8,128)(2,1)S(1)}, u32[]{:S(2)}, u32[]{:S(2)}) collective-permute-start(bf16[2,32,1024]{2,1,0:T(8,128)(2,1)S(1)} %get-tuple-element.50), channel_id=1, source_target_pairs={{0,4},{2,6},{4,8},{6,10},{8,12},{10,14},{12,0},{14,2},{1,5},{3,7},... | collective-permute-start | bytes 393224 | tf_op jit(solution)/shard_map/ppermute | solution.py:257
  110.2 9.2 %collective-permute-start.27 = (bf16[3,32,1024]{2,1,0:T(8,128)(2,1)S(1)}, bf16[3,32,1024]{2,1,0:T(8,128)(2,1)S(1)}, u32[]{:S(2)}, u32[]{:S(2)}) collective-permute-start(bf16[3,32,1024]{2,1,0:T(8,128)(2,1)S(1)} %pad_maximum_fusion), channel_id=1, source_target_pairs={{0,2},{2,0},{4,6},{6,4},{8,10},{10,8},{12,14},{14,12},{1,3},{3,1},... | collective-permute-start | bytes 589832 | tf_op jit(solution)/shard_map/ppermute | solution.py:251
  119.1 4.3 %collective-permute-start.26 = (bf16[32,1024]{1,0:T(8,128)(2,1)S(1)}, bf16[32,1024]{1,0:T(8,128)(2,1)S(1)}, u32[]{:S(2)}, u32[]{:S(2)}) collective-permute-start(bf16[32,1024]{1,0:T(8,128)(2,1)S(1)} %fusion.32), channel_id=1, source_target_pairs={{0,2},{2,0},{4,6},{6,4},{8,10},{10,8},{12,14},{14,12},{1,3},{3,1},... | collective-permute-start | bytes 196616 | tf_op jit(solution)/shard_map/ppermute | solution.py:251
  119.5 5.4 %collective-permute-start.28 = (bf16[32,1024]{1,0:T(8,128)(2,1)S(1)}, bf16[32,1024]{1,0:T(8,128)(2,1)S(1)}, u32[]{:S(2)}, u32[]{:S(2)}) collective-permute-start(bf16[32,1024]{1,0:T(8,128)(2,1)S(1)} %get-tuple-element.43), channel_id=1, source_target_pairs={{0,8},{2,10},{4,12},{6,14},{8,0},{10,2},{12,4},{14,6},{1,9},{3,11}... | collective-permute-start | bytes 196616 | tf_op jit(solution)/shard_map/ppermute | solution.py:257
  121.4 6.1 %collective-permute-start.29 = (bf16[32,1024]{1,0:T(8,128)(2,1)S(1)}, bf16[32,1024]{1,0:T(8,128)(2,1)S(1)}, u32[]{:S(2)}, u32[]{:S(2)}) collective-permute-start(bf16[32,1024]{1,0:T(8,128)(2,1)S(1)} %get-tuple-element.44), channel_id=1, source_target_pairs={{0,4},{2,6},{4,8},{6,10},{8,12},{10,14},{12,0},{14,2},{1,5},{3,7},... | collective-permute-start | bytes 196616 | tf_op jit(solution)/shard_map/ppermute | solution.py:257
  (5 other events, 52.4 us)

commit v3 on v2

--- a/solution.py
+++ b/solution.py
@@ -13,6 +13,7 @@
 PART = 8
 ROWS = 32
 VMEM_LIMIT = 50 << 20
+AHEAD = 4
 epsilon = 1e-06
 masked_score = -1e30
 
@@ -145,8 +146,15 @@
                 d_ref.at[:, pl.ds(at, size)], down_ref.at[:, pl.ds(at, size)], down_sem.at[n]
             )
         )
-    for copy in in_copies + down_copies:
-        copy.start()
+    copies = [in_copies[2 * n : 2 * n + 2] for n in range(len(in_cuts))]
+    copies += [[copy] for copy in down_copies]
+
+    def start(n):
+        for copy in copies[n] if n < len(copies) else []:
+            copy.start()
+
+    for n in range(AHEAD):
+        start(n)
     for n, slot in enumerate(slots):
         place = pl.ds(n * each, each)
         x_ref[place, :] = slot[:, :width]
@@ -168,6 +176,7 @@
 
     held = None
     for n, (at, size) in enumerate(in_cuts):
+        start(n + AHEAD)
         in_copies[2 * n].wait()
         in_copies[2 * n + 1].wait()
         place = slice(at, at + size)
@@ -179,6 +188,7 @@
     keep(*held)
     held = None
     for n, (at, size) in enumerate(down_cuts):
+        start(len(in_cuts) + n + AHEAD)
         down_copies[n].wait()
         place = slice(at, at + size)
         y = jnp.dot(h_ref[...], down_ref[:, place], preferred_element_type=jnp.float32)
@@ -259,6 +269,9 @@
     def other(v):
         return lax.ppermute(v, "rep", [(i, (i + 1) % reps) for i in range(reps)])
 
+    def fence(*values):
+        return lax.optimization_barrier(values)
+
     def rows_of_seq(v, axis):
         return lax.dynamic_slice_in_dim(v, lax.axis_index("seq") * share_rows, share_rows, axis)
 
@@ -329,10 +342,14 @@
     inverse_rms = lax.rsqrt(jnp.mean(full_rows * full_rows, axis=1) + epsilon)
     normed = (full_rows * inverse_rms[:, None] * moe_gain).astype(narrow)
     packed = jnp.concatenate([normed, coeffs], axis=1)
-    columns = [packed, across(packed)] if inner == 2 else [packed]
-    ks = list(range(outer))
-    groups = [ks[: outer // 2], ks[outer // 2 :]] if outer > 1 else [ks]
-    gathered = [[along(c, k) if k else c for c in columns for k in group] for group in groups]
+    near = [packed] + [along(packed, k) for k in range(1, outer)]
+    far = []
+    if inner == 2:
+        middle = outer // 2
+        far = [across(v) for k, v in enumerate(near) if k != middle or outer == 1]
+        if outer > 1:
+            *far, near[middle] = fence(*far, near[middle])
+            far.insert(middle, across(near[middle]))
     first_expert = (me * reps + lax.axis_index("rep")) * experts_local
 
     def run_experts(slots):
@@ -350,50 +367,38 @@
                 )
                 for t in total
             ]
-        return [t.reshape(inner, -1, tok_rows, feat_local) for t in total]
-
-    def over_reps(made):
-        merged = made[0].astype(wide)
-        return merged + other(made[1]).astype(wide) if reps == 2 else merged
-
-    cut = feat_local // 2
-
-    def pair(v, k):
-        return along(v.astype(narrow), -k).astype(wide)
-
-    if len(groups) == 2 and inner == 2:
-        made = run_experts(gathered[0])
-        made, late = lax.optimization_barrier((made, gathered[1]))
-        early = over_reps(made)
-        early_parts = [
-            along(early[:, i].astype(narrow), -k) for i, k in enumerate(groups[0]) if k
-        ]
-        made = run_experts(late)
-        made, early_parts = lax.optimization_barrier((made, early_parts))
-        late_sum = over_reps(made)
-        base = early[:, 0]
-        for part in early_parts:
-            base = base + part.astype(wide)
-        right_far = across(
-            jnp.concatenate([late_sum[1, :, :, cut:], base[None, 1, :, cut:]]).astype(narrow)
-        ).astype(wide)
-        left = base[..., :cut]
-        for i, k in enumerate(groups[1]):
-            left = left + pair(late_sum[:, i, :, :cut], k)
-        right = base[0, :, cut:] + right_far[-1]
-        for i, k in enumerate(groups[1]):
-            right = right + pair(late_sum[0, i, :, cut:] + right_far[i], k)
-        left = left[0] + across(left[1].astype(narrow)).astype(wide)
-        moe_out = jnp.concatenate([left, right], axis=1)
+        return [t.reshape(outer, tok_rows, feat_local) for t in total]
+
+    def back(v):
+        return [along(v[k].astype(narrow), -k) for k in range(1, outer)]
+
+    def summed(first, parts):
+        for part in parts:
+            first = first + part.astype(wide)
+        return first
+
+    made = run_experts(near)
+    if inner == 2:
+        made, far = fence(made, far)
+        swapped = [other(v) for v in made[1:]]
+        far_made = run_experts(far)
+        far_made, swapped = fence(far_made, swapped)
+        far_sum = summed(far_made[0].astype(wide), [other(v) for v in far_made[1:]])
+        near_sum = summed(made[0].astype(wide), swapped)
+        moe_out, moe_far = near_sum[0], far_sum[0]
+        inside = [outer // 2] + [k for k in range(1, outer - 1) if k != outer // 2]
+        given = {k: across(far_sum[k].astype(narrow)) for k in inside if outer > 2}
+        if outer > 1:
+            last = jnp.stack([near_sum[-1], far_sum[-1]]).astype(narrow)
+            last = along(last, 1 - outer).astype(wide)
+            moe_out, moe_far = moe_out + last[0], moe_far + last[1]
+        for k, part in given.items():
+            part = near_sum[k] + part.astype(wide)
+            moe_out = moe_out + along(part.astype(narrow), -k).astype(wide)
+        moe_out = moe_out + across(moe_far.astype(narrow)).astype(wide)
     else:
-        total = jnp.zeros((inner, tok_rows, feat_local), wide)
-        for group, slots in zip(groups, gathered):
-            made = over_reps(run_experts(slots))
-            for i, k in enumerate(group):
-                total = total + (pair(made[:, i], k) if k else made[:, i])
-        moe_out = total[0]
-        if inner == 2:
-            moe_out = moe_out + across(total[1].astype(narrow)).astype(wide)
+        near_sum = summed(made[0].astype(wide), [other(v) for v in made[1:]])
+        moe_out = summed(near_sum[0], back(near_sum))
     return jnp.where(is_live[:, None], residual_wide + moe_out, 0.0).astype(narrow)
 
 

time: 129 us -> 117 us (0.907)
  waiting for transfers between devices: 49.6 us -> 40.8 us
    ppermute x14 -> x9, waiting for transfers between devices: 35.2 us -> 27.5 us  [along(): return lax.ppermute(v, 'ep', pairs)]
    ppermute x14 -> x9, starting transfers between devices: 16.8 us -> 12 us  [along(): return lax.ppermute(v, 'ep', pairs)]
    ppermute x5 -> x9, starting transfers between devices: 3.25 us -> 6.73 us  [across(): return lax.ppermute(v, 'ep', [(i, i ^ 1) for i in range(owners)])]
    ppermute x5 -> x9, waiting for transfers between devices: 11.5 us -> 9.72 us  [across(): return lax.ppermute(v, 'ep', [(i, i ^ 1) for i in range(owners)])]
  transfers between devices with their start and end apart: 31 -> 30, of which waited for: 15 -> 20; matrix products, arithmetic and copies ran while one was open for 9% -> 10% of each run, Pallas kernels for 25% -> 27%
where the time goes in v3:
time: 117 us
  waiting for transfers between devices  40.8 us (35%)
  Pallas kernels  31.3 us (27%)
  starting transfers between devices  28.2 us (24%)
  local copies, waits for them, and re-layouts  13.5 us (12%)
  other arithmetic  1.8 us (2%)
    ppermute x9, waiting for transfers between devices, along(): return lax.ppermute(v, 'ep', pairs)  27.5 us
    pallas_call x2, Pallas kernels, expert(): pl.pallas_call(functools.partial(expert_kernel, len(slots), outs), in_spe...  16.8 us
    pallas_call x1, Pallas kernels, attend(): pl.pallas_call(attend_kernel, grid=(n // rows,), in_specs=[pl.BlockSpec((...  14.5 us
    ppermute x9, starting transfers between devices, along(): return lax.ppermute(v, 'ep', pairs)  12 us
    unnamed x13, local copies, waits for them, and re-layouts  11.4 us
    ppermute x9, waiting for transfers between devices, across(): return lax.ppermute(v, 'ep', [(i, i ^ 1) for i in range(owners)])  9.72 us
    all_to_all x1, starting transfers between devices, local(): fresh = lax.all_to_all(sent, 'ep', split_axis=0, concat_axis=0, tiled=True)  7.25 us
    ppermute x9, starting transfers between devices, across(): return lax.ppermute(v, 'ep', [(i, i ^ 1) for i in range(owners)])  6.73 us
  transfers between devices with their start and end apart: 30, of which 20 were waited for; matrix products, arithmetic and copies ran while one was open for 10% of the time, Pallas kernels for 27%

profile of v3, /device:TPU:0, one launch (start us, length us, event | category | flops | bytes accessed | tf_op | source)
XLA Modules:
  0.0 117.2 jit_solution(16039370537897428580)
XLA Ops:
  0.0 1.8 %copy.49 = bf16[3,4,8,8,256]{4,3,1,0,2:T(8,128)(2,1)} copy(bf16[3,4,8,8,256]{4,3,2,1,0:T(8,128)(2,1)} %bitcast.79) | data formatting | bytes 786432 | tf_op jit(solution)/shard_map/reshape | solution.py:278
  1.8 7.3 %all-to-all-start = ((bf16[8,3,32,256]{3,2,1,0:T(8,128)(2,1)}), bf16[8,3,32,256]{3,2,1,0:T(8,128)(2,1)S(1)}, u32[]{:S(2)}, u32[]{:S(2)}) async-start(bf16[8,3,32,256]{3,2,1,0:T(8,128)(2,1)} %bitcast.65), calls=%async_computation | async-start | bytes 786432 | tf_op jit(solution)/shard_map/all_to_all | solution.py:279
  9.1 11.3 %copy.48 = bf16[1,2048,2,1408]{3,1,2,0:T(8,128)(2,1)} copy(bf16[1,2048,2,1408]{3,2,1,0:T(2,128)(2,1)} %param.18) | data formatting | bytes 23068672 | tf_op args[7]
  20.8 1.8 %collective-permute-start = (bf16[128,2048]{1,0:T(8,128)(2,1)S(1)}, bf16[128,2048]{1,0:T(8,128)(2,1)S(1)}, u32[]{:S(2)}, u32[]{:S(2)}) collective-permute-start(bf16[128,2048]{1,0:T(8,128)(2,1)S(1)} %slice_select_fusion), channel_id=1, source_target_pairs={{0,2},{2,0},{4,6},{6,4},{8,10},{10,8},{12,14},{14,12},{1,3},{3,1},... | collective-permute-start | bytes 1572872 | tf_op jit(solution)/shard_map/ppermute | solution.py:261
  23.4 14.5 %shard_map.109 = bf16[256,256]{1,0:T(8,128)(2,1)S(1)} custom-call(bf16[8,3,32,256]{3,2,1,0:T(8,128)(2,1)S(1)} %all-to-all-done.fresh_ref, s32[256,1]{1,0:T(8,128)S(1)} %reshape.77.len_ref, bf16[2,256,128,256]{3,2,1,0:T(8,128)(2,1)} %bitcast.73, bf16[2,256,128,256]{3,2,1,0:T(8,128)(2,1)} %bitcast.74), custom_call_target="tpu_custom_call" | custom-call | flops 33554432 | bytes 33554432 | tf_op jit(solution)/shard_map/pallas_call | solution.py:104
  38.3 4.3 %collective-permute-done.1 = bf16[4,32,256]{2,1,0:T(8,128)(2,1)S(1)} collective-permute-done((bf16[4,32,256]{2,1,0:T(8,128)(2,1)S(1)}, bf16[4,32,256]{2,1,0:T(8,128)(2,1)S(1)}, u32[]{:S(2)}, u32[]{:S(2)}) %collective-permute-start.1) | collective-permute-done | bytes 65568 | tf_op jit(solution)/shard_map/ppermute | solution.py:261
  42.8 0.7 fusion.37
  43.5 1.5 %collective-permute-start.3 = (bf16[32,2048]{1,0:T(8,128)(2,1)S(1)}, bf16[32,2048]{1,0:T(8,128)(2,1)S(1)}, u32[]{:S(2)}, u32[]{:S(2)}) collective-permute-start(bf16[32,2048]{1,0:T(8,128)(2,1)S(1)} %get-tuple-element.60), channel_id=1, source_target_pairs={{0,4},{2,6},{4,8},{6,10},{8,12},{10,14},{12,0},{14,2},{1,5},{3,7},... | collective-permute-start | bytes 393224 | tf_op jit(solution)/shard_map/ppermute | solution.py:267
  45.0 2.4 %collective-permute-start.5 = (bf16[32,2048]{1,0:T(8,128)(2,1)S(1)}, bf16[32,2048]{1,0:T(8,128)(2,1)S(1)}, u32[]{:S(2)}, u32[]{:S(2)}) collective-permute-start(bf16[32,2048]{1,0:T(8,128)(2,1)S(1)} %get-tuple-element.61), channel_id=1, source_target_pairs={{0,12},{2,14},{4,0},{6,2},{8,4},{10,6},{12,8},{14,10},{1,13},{3,15... | collective-permute-start | bytes 393224 | tf_op jit(solution)/shard_map/ppermute | solution.py:267
  47.4 0.6 collective-permute-start.4
  48.1 3.7 %collective-permute-done.3 = bf16[32,2048]{1,0:T(8,128)(2,1)S(1)} collective-permute-done((bf16[32,2048]{1,0:T(8,128)(2,1)S(1)}, bf16[32,2048]{1,0:T(8,128)(2,1)S(1)}, u32[]{:S(2)}, u32[]{:S(2)}) %collective-permute-start.3) | collective-permute-done | bytes 131104 | tf_op jit(solution)/shard_map/ppermute | solution.py:267
  51.7 0.9 collective-permute-done.5
  52.7 6.2 %collective-permute-done.4 = bf16[32,2048]{1,0:T(8,128)(2,1)S(1)} collective-permute-done((bf16[32,2048]{1,0:T(8,128)(2,1)S(1)}, bf16[32,2048]{1,0:T(8,128)(2,1)S(1)}, u32[]{:S(2)}, u32[]{:S(2)}) %collective-permute-start.4) | collective-permute-done | bytes 131104 | tf_op jit(solution)/shard_map/ppermute | solution.py:267
  59.2 1.5 %collective-permute-start.9 = (bf16[32,2176]{1,0:T(8,128)(2,1)S(1)}, bf16[32,2176]{1,0:T(8,128)(2,1)S(1)}, u32[]{:S(2)}, u32[]{:S(2)}) collective-permute-start(bf16[32,2176]{1,0:T(8,128)(2,1)S(1)} %fusion.25.refs_0_), channel_id=1, source_target_pairs={{0,12},{2,14},{4,0},{6,2},{8,4},{10,6},{12,8},{14,10},{1,13},{3,15... | collective-permute-start | bytes 417800 | tf_op jit(solution)/shard_map/ppermute | solution.py:267
  61.6 0.6 collective-permute-start.7
  62.1 4.8 %collective-permute-done.9.refs_3_ = bf16[32,2176]{1,0:T(8,128)(2,1)S(1)} collective-permute-done((bf16[32,2176]{1,0:T(8,128)(2,1)S(1)}, bf16[32,2176]{1,0:T(8,128)(2,1)S(1)}, u32[]{:S(2)}, u32[]{:S(2)}) %collective-permute-start.9) | collective-permute-done | bytes 139296 | tf_op jit(solution)/shard_map/ppermute | solution.py:267
  67.3 1.7 %collective-permute-done.6.refs_1_ = bf16[32,2176]{1,0:T(8,128)(2,1)S(1)} collective-permute-done((bf16[32,2176]{1,0:T(8,128)(2,1)S(1)}, bf16[32,2176]{1,0:T(8,128)(2,1)S(1)}, u32[]{:S(2)}, u32[]{:S(2)}) %collective-permute-start.6) | collective-permute-done | bytes 139296 | tf_op jit(solution)/shard_map/ppermute | solution.py:267
  69.5 3.7 %collective-permute-done.11.refs_2_ = bf16[32,2176]{1,0:T(8,128)(2,1)S(1)} collective-permute-done((bf16[32,2176]{1,0:T(8,128)(2,1)S(1)}, bf16[32,2176]{1,0:T(8,128)(2,1)S(1)}, u32[]{:S(2)}, u32[]{:S(2)}) %collective-permute-start.11) | collective-permute-done | bytes 139296 | tf_op jit(solution)/shard_map/ppermute | solution.py:267
  74.8 0.7 collective-permute-done.14.refs_6_
  75.4 8.4 %shard_map.110 = (bf16[128,2048]{1,0:T(8,128)(2,1)S(1)}, bf16[128,2048]{1,0:T(8,128)(2,1)S(1)}) custom-call(s32[1]{0:T(128)} %bitcast.11.mine_ref, bf16[32,2176]{1,0:T(8,128)(2,1)S(1)} %fusion.25.refs_0_, bf16[32,2176]{1,0:T(8,128)(2,1)S(1)} %collective-permute-done.6.refs_1_, bf16[32,2176]{1,0:T(8,128)(2,1)S(1)} %collective-permute-done.11.refs_2_, ...), custom_call_target="tpu_custom_call" | custom-call | flops 4429185024 | bytes 19398656 | tf_op jit(solution)/shard_map/pallas_call | solution.py:207
  86.0 8.4 %shard_map.111 = (bf16[128,2048]{1,0:T(8,128)(2,1)S(1)}, bf16[128,2048]{1,0:T(8,128)(2,1)S(1)}) custom-call(s32[1]{0:T(128)} %bitcast.11.mine_ref, bf16[32,2176]{1,0:T(8,128)(2,1)S(1)} %collective-permute-done.7.refs_0_, bf16[32,2176]{1,0:T(8,128)(2,1)S(1)} %collective-permute-done.8.refs_1_, bf16[32,2176]{1,0:T(8,128)(2,1)S(1)} %collective-permute-done.16.refs_2_, ...), custom_call_target="tpu_custom_call" | custom-call | flops 4429185024 | bytes 19398656 | tf_op jit(solution)/shard_map/pallas_call | solution.py:207
  95.0 1.4 %collective-permute-done.22 = bf16[4,32,2048]{2,1,0:T(8,128)(2,1)S(1)} collective-permute-done((bf16[4,32,2048]{2,1,0:T(8,128)(2,1)S(1)}, bf16[4,32,2048]{2,1,0:T(8,128)(2,1)S(1)}, u32[]{:S(2)}, u32[]{:S(2)}) %collective-permute-start.22) | collective-permute-done | bytes 524320 | tf_op jit(solution)/shard_map/ppermute | solution.py:270
  96.6 0.8 collective-permute-start.24
  97.4 1.3 %collective-permute-start.26 = (bf16[32,2048]{1,0:T(8,128)(2,1)S(1)}, bf16[32,2048]{1,0:T(8,128)(2,1)S(1)}, u32[]{:S(2)}, u32[]{:S(2)}) collective-permute-start(bf16[32,2048]{1,0:T(8,128)(2,1)S(1)} %get-tuple-element.58), channel_id=1, source_target_pairs={{0,2},{2,0},{4,6},{6,4},{8,10},{10,8},{12,14},{14,12},{1,3},{3,1},... | collective-permute-start | bytes 393224 | tf_op jit(solution)/shard_map/ppermute | solution.py:261
  98.7 1.4 %collective-permute-start.23 = (bf16[2,32,2048]{2,1,0:T(8,128)(2,1)S(1)}, bf16[2,32,2048]{2,1,0:T(8,128)(2,1)S(1)}, u32[]{:S(2)}, u32[]{:S(2)}) collective-permute-start(bf16[2,32,2048]{2,1,0:T(8,128)(2,1)S(1)} %pad_maximum_fusion), channel_id=1, source_target_pairs={{0,4},{2,6},{4,8},{6,10},{8,12},{10,14},{12,0},{14,2},{1,5},{3,7},... | collective-permute-start | bytes 786440 | tf_op jit(solution)/shard_map/ppermute | solution.py:267
  100.1 2.9 %collective-permute-done.24 = bf16[32,2048]{1,0:T(8,128)(2,1)S(1)} collective-permute-done((bf16[32,2048]{1,0:T(8,128)(2,1)S(1)}, bf16[32,2048]{1,0:T(8,128)(2,1)S(1)}, u32[]{:S(2)}, u32[]{:S(2)}) %collective-permute-start.24) | collective-permute-done | bytes 131104 | tf_op jit(solution)/shard_map/ppermute | solution.py:261
  103.0 2.2 %collective-permute-done.26 = bf16[32,2048]{1,0:T(8,128)(2,1)S(1)} collective-permute-done((bf16[32,2048]{1,0:T(8,128)(2,1)S(1)}, bf16[32,2048]{1,0:T(8,128)(2,1)S(1)}, u32[]{:S(2)}, u32[]{:S(2)}) %collective-permute-start.26) | collective-permute-done | bytes 131104 | tf_op jit(solution)/shard_map/ppermute | solution.py:261
  105.3 3.9 %collective-permute-start.25 = (bf16[32,2048]{1,0:T(8,128)(2,1)S(1)}, bf16[32,2048]{1,0:T(8,128)(2,1)S(1)}, u32[]{:S(2)}, u32[]{:S(2)}) collective-permute-start(bf16[32,2048]{1,0:T(8,128)(2,1)S(1)} %get-tuple-element.51), channel_id=1, source_target_pairs={{0,8},{2,10},{4,12},{6,14},{8,0},{10,2},{12,4},{14,6},{1,9},{3,11}... | collective-permute-start | bytes 393224 | tf_op jit(solution)/shard_map/ppermute | solution.py:267
  109.2 0.8 collective-permute-start.28
  110.0 4.9 %collective-permute-done.25 = bf16[32,2048]{1,0:T(8,128)(2,1)S(1)} collective-permute-done((bf16[32,2048]{1,0:T(8,128)(2,1)S(1)}, bf16[32,2048]{1,0:T(8,128)(2,1)S(1)}, u32[]{:S(2)}, u32[]{:S(2)}) %collective-permute-start.25) | collective-permute-done | bytes 131104 | tf_op jit(solution)/shard_map/ppermute | solution.py:267
  114.8 1.6 %collective-permute-done.27 = bf16[32,2048]{1,0:T(8,128)(2,1)S(1)} collective-permute-done((bf16[32,2048]{1,0:T(8,128)(2,1)S(1)}, bf16[32,2048]{1,0:T(8,128)(2,1)S(1)}, u32[]{:S(2)}, u32[]{:S(2)}) %collective-permute-start.27) | collective-permute-done | bytes 131104 | tf_op jit(solution)/shard_map/ppermute | solution.py:267
  116.4 0.8 fusion.11
  (70 shorter events, 7.7 us)
Async XLA Ops:
  1.8 18.9 %all-to-all-start = ((bf16[8,3,32,256]{3,2,1,0:T(8,128)(2,1)}), bf16[8,3,32,256]{3,2,1,0:T(8,128)(2,1)S(1)}, u32[]{:S(2)}, u32[]{:S(2)}) async-start(bf16[8,3,32,256]{3,2,1,0:T(8,128)(2,1)} %bitcast.65), calls=%async_computation | async-start | bytes 786432 | tf_op jit(solution)/shard_map/all_to_all | solution.py:279
  20.8 17.1 %collective-permute-start = (bf16[128,2048]{1,0:T(8,128)(2,1)S(1)}, bf16[128,2048]{1,0:T(8,128)(2,1)S(1)}, u32[]{:S(2)}, u32[]{:S(2)}) collective-permute-start(bf16[128,2048]{1,0:T(8,128)(2,1)S(1)} %slice_select_fusion), channel_id=1, source_target_pairs={{0,2},{2,0},{4,6},{6,4},{8,10},{10,8},{12,14},{14,12},{1,3},{3,1},... | collective-permute-start | bytes 1572872 | tf_op jit(solution)/shard_map/ppermute | solution.py:261
  37.9 4.8 %collective-permute-start.2 = (bf16[128,2048]{1,0:T(8,128)(2,1)S(1)}, bf16[128,2048]{1,0:T(8,128)(2,1)S(1)}, u32[]{:S(2)}, u32[]{:S(2)}) collective-permute-start(bf16[128,2048]{1,0:T(8,128)(2,1)S(1)} %collective-permute-done), channel_id=1, source_target_pairs={{0,1},{1,0},{2,3},{3,2},{4,5},{5,4},{6,7},{7,6},{8,9},{9,8},{10,11... | collective-permute-start | bytes 1572872 | tf_op jit(solution)/shard_map/ppermute | solution.py:270
  38.0 4.6 %collective-permute-start.1 = (bf16[4,32,256]{2,1,0:T(8,128)(2,1)S(1)}, bf16[4,32,256]{2,1,0:T(8,128)(2,1)S(1)}, u32[]{:S(2)}, u32[]{:S(2)}) collective-permute-start(bf16[4,32,256]{2,1,0:T(8,128)(2,1)S(1)} %fusion.30), channel_id=1, source_target_pairs={{0,2},{2,0},{4,6},{6,4},{8,10},{10,8},{12,14},{14,12},{1,3},{3,1},... | collective-permute-start | bytes 196616 | tf_op jit(solution)/shard_map/ppermute | solution.py:261
  42.6 16.2 %copy-start.1 = (bf16[32,2048]{1,0:T(8,128)(2,1)S(1)}, bf16[32,2048]{1,0:T(8,128)(2,1)}, u32[]{:S(2)}) copy-start(bf16[32,2048]{1,0:T(8,128)(2,1)} %param.11) | copy-start | bytes 393220
  42.8 16.3 %copy-start.2 = (f32[2048]{0:T(1024)S(1)}, f32[2048]{0:T(1024)}, u32[]{:S(2)}) copy-start(f32[2048]{0:T(1024)} %param.17) | copy-start | bytes 24580
  43.5 8.3 %collective-permute-start.3 = (bf16[32,2048]{1,0:T(8,128)(2,1)S(1)}, bf16[32,2048]{1,0:T(8,128)(2,1)S(1)}, u32[]{:S(2)}, u32[]{:S(2)}) collective-permute-start(bf16[32,2048]{1,0:T(8,128)(2,1)S(1)} %get-tuple-element.60), channel_id=1, source_target_pairs={{0,4},{2,6},{4,8},{6,10},{8,12},{10,14},{12,0},{14,2},{1,5},{3,7},... | collective-permute-start | bytes 393224 | tf_op jit(solution)/shard_map/ppermute | solution.py:267
  45.0 7.6 %collective-permute-start.5 = (bf16[32,2048]{1,0:T(8,128)(2,1)S(1)}, bf16[32,2048]{1,0:T(8,128)(2,1)S(1)}, u32[]{:S(2)}, u32[]{:S(2)}) collective-permute-start(bf16[32,2048]{1,0:T(8,128)(2,1)S(1)} %get-tuple-element.61), channel_id=1, source_target_pairs={{0,12},{2,14},{4,0},{6,2},{8,4},{10,6},{12,8},{14,10},{1,13},{3,15... | collective-permute-start | bytes 393224 | tf_op jit(solution)/shard_map/ppermute | solution.py:267
  47.4 11.5 %collective-permute-start.4 = (bf16[32,2048]{1,0:T(8,128)(2,1)S(1)}, bf16[32,2048]{1,0:T(8,128)(2,1)S(1)}, u32[]{:S(2)}, u32[]{:S(2)}) collective-permute-start(bf16[32,2048]{1,0:T(8,128)(2,1)S(1)} %get-tuple-element.62), channel_id=1, source_target_pairs={{0,8},{2,10},{4,12},{6,14},{8,0},{10,2},{12,4},{14,6},{1,9},{3,11}... | collective-permute-start | bytes 393224 | tf_op jit(solution)/shard_map/ppermute | solution.py:267
  59.2 7.7 %collective-permute-start.9 = (bf16[32,2176]{1,0:T(8,128)(2,1)S(1)}, bf16[32,2176]{1,0:T(8,128)(2,1)S(1)}, u32[]{:S(2)}, u32[]{:S(2)}) collective-permute-start(bf16[32,2176]{1,0:T(8,128)(2,1)S(1)} %fusion.25.refs_0_), channel_id=1, source_target_pairs={{0,12},{2,14},{4,0},{6,2},{8,4},{10,6},{12,8},{14,10},{1,13},{3,15... | collective-permute-start | bytes 417800 | tf_op jit(solution)/shard_map/ppermute | solution.py:267
  60.7 8.3 %collective-permute-start.6 = (bf16[32,2176]{1,0:T(8,128)(2,1)S(1)}, bf16[32,2176]{1,0:T(8,128)(2,1)S(1)}, u32[]{:S(2)}, u32[]{:S(2)}) collective-permute-start(bf16[32,2176]{1,0:T(8,128)(2,1)S(1)} %fusion.25.refs_0_), channel_id=1, source_target_pairs={{0,4},{2,6},{4,8},{6,10},{8,12},{10,14},{12,0},{14,2},{1,5},{3,7},... | collective-permute-start | bytes 417800 | tf_op jit(solution)/shard_map/ppermute | solution.py:267
  61.3 11.9 %collective-permute-start.11 = (bf16[32,2176]{1,0:T(8,128)(2,1)S(1)}, bf16[32,2176]{1,0:T(8,128)(2,1)S(1)}, u32[]{:S(2)}, u32[]{:S(2)}) collective-permute-start(bf16[32,2176]{1,0:T(8,128)(2,1)S(1)} %fusion.25.refs_0_), channel_id=1, source_target_pairs={{0,8},{2,10},{4,12},{6,14},{8,0},{10,2},{12,4},{14,6},{1,9},{3,11}... | collective-permute-start | bytes 417800 | tf_op jit(solution)/shard_map/ppermute | solution.py:267
  61.6 11.7 %collective-permute-start.7 = (bf16[32,2176]{1,0:T(8,128)(2,1)S(1)}, bf16[32,2176]{1,0:T(8,128)(2,1)S(1)}, u32[]{:S(2)}, u32[]{:S(2)}) collective-permute-start(bf16[32,2176]{1,0:T(8,128)(2,1)S(1)} %fusion.25.refs_0_), channel_id=1, source_target_pairs={{0,2},{2,0},{4,6},{6,4},{8,10},{10,8},{12,14},{14,12},{1,3},{3,1},... | collective-permute-start | bytes 417800 | tf_op jit(solution)/shard_map/ppermute | solution.py:261
  67.0 6.8 %collective-permute-start.10 = (bf16[32,2176]{1,0:T(8,128)(2,1)S(1)}, bf16[32,2176]{1,0:T(8,128)(2,1)S(1)}, u32[]{:S(2)}, u32[]{:S(2)}) collective-permute-start(bf16[32,2176]{1,0:T(8,128)(2,1)S(1)} %collective-permute-done.9.refs_3_), channel_id=1, source_target_pairs={{0,2},{2,0},{4,6},{6,4},{8,10},{10,8},{12,14},{14,12},{1,3},{3,1},... | collective-permute-start | bytes 417800 | tf_op jit(solution)/shard_map/ppermute | solution.py:261
  69.0 5.1 %collective-permute-start.8 = (bf16[32,2176]{1,0:T(8,128)(2,1)S(1)}, bf16[32,2176]{1,0:T(8,128)(2,1)S(1)}, u32[]{:S(2)}, u32[]{:S(2)}) collective-permute-start(bf16[32,2176]{1,0:T(8,128)(2,1)S(1)} %collective-permute-done.6.refs_1_), channel_id=1, source_target_pairs={{0,2},{2,0},{4,6},{6,4},{8,10},{10,8},{12,14},{14,12},{1,3},{3,1},... | collective-permute-start | bytes 417800 | tf_op jit(solution)/shard_map/ppermute | solution.py:261
  69.5 5.1 %collective-permute-start.12 = (bf16[32,2176]{1,0:T(8,128)(2,1)S(1)}, bf16[32,2176]{1,0:T(8,128)(2,1)S(1)}, u32[]{:S(2)}, u32[]{:S(2)}) collective-permute-start(bf16[32,2176]{1,0:T(8,128)(2,1)S(1)} %fusion.25.refs_0_), channel_id=1, source_target_pairs={{0,1},{1,0},{2,3},{3,2},{4,5},{5,4},{6,7},{7,6},{8,9},{9,8},{10,11... | collective-permute-start | bytes 417800 | tf_op jit(solution)/shard_map/ppermute | solution.py:270
  73.2 1.4 %collective-permute-start.15 = (bf16[32,2176]{1,0:T(8,128)(2,1)S(1)}, bf16[32,2176]{1,0:T(8,128)(2,1)S(1)}, u32[]{:S(2)}, u32[]{:S(2)}) collective-permute-start(bf16[32,2176]{1,0:T(8,128)(2,1)S(1)} %collective-permute-done.9.refs_3_), channel_id=1, source_target_pairs={{0,1},{1,0},{2,3},{3,2},{4,5},{5,4},{6,7},{7,6},{8,9},{9,8},{10,11... | collective-permute-start | bytes 417800 | tf_op jit(solution)/shard_map/ppermute | solution.py:270
  73.2 1.6 %collective-permute-start.13 = (bf16[32,2176]{1,0:T(8,128)(2,1)S(1)}, bf16[32,2176]{1,0:T(8,128)(2,1)S(1)}, u32[]{:S(2)}, u32[]{:S(2)}) collective-permute-start(bf16[32,2176]{1,0:T(8,128)(2,1)S(1)} %collective-permute-done.6.refs_1_), channel_id=1, source_target_pairs={{0,1},{1,0},{2,3},{3,2},{4,5},{5,4},{6,7},{7,6},{8,9},{9,8},{10,11... | collective-permute-start | bytes 417800 | tf_op jit(solution)/shard_map/ppermute | solution.py:270
  74.1 1.4 %collective-permute-start.14 = (bf16[32,2176]{1,0:T(8,128)(2,1)S(1)}, bf16[32,2176]{1,0:T(8,128)(2,1)S(1)}, u32[]{:S(2)}, u32[]{:S(2)}) collective-permute-start(bf16[32,2176]{1,0:T(8,128)(2,1)S(1)} %collective-permute-done.11.refs_2_), channel_id=1, source_target_pairs={{0,1},{1,0},{2,3},{3,2},{4,5},{5,4},{6,7},{7,6},{8,9},{9,8},{10,11... | collective-permute-start | bytes 417800 | tf_op jit(solution)/shard_map/ppermute | solution.py:270
  74.1 9.8 %collective-permute-start.16 = (bf16[32,2176]{1,0:T(8,128)(2,1)S(1)}, bf16[32,2176]{1,0:T(8,128)(2,1)S(1)}, u32[]{:S(2)}, u32[]{:S(2)}) collective-permute-start(bf16[32,2176]{1,0:T(8,128)(2,1)S(1)} %collective-permute-done.11.refs_2_), channel_id=1, source_target_pairs={{0,2},{2,0},{4,6},{6,4},{8,10},{10,8},{12,14},{14,12},{1,3},{3,1},... | collective-permute-start | bytes 417800 | tf_op jit(solution)/shard_map/ppermute | solution.py:261
  83.9 1.4 %collective-permute-start.17 = (bf16[32,2176]{1,0:T(8,128)(2,1)S(1)}, bf16[32,2176]{1,0:T(8,128)(2,1)S(1)}, u32[]{:S(2)}, u32[]{:S(2)}) collective-permute-start(bf16[32,2176]{1,0:T(8,128)(2,1)S(1)} %collective-permute-done.7.refs_0_), channel_id=1, source_target_pairs={{0,1},{1,0},{2,3},{3,2},{4,5},{5,4},{6,7},{7,6},{8,9},{9,8},{10,11... | collective-permute-start | bytes 417800 | tf_op jit(solution)/shard_map/ppermute | solution.py:270
  84.1 1.4 %collective-permute-start.18 = (bf16[32,2176]{1,0:T(8,128)(2,1)S(1)}, bf16[32,2176]{1,0:T(8,128)(2,1)S(1)}, u32[]{:S(2)}, u32[]{:S(2)}) collective-permute-start(bf16[32,2176]{1,0:T(8,128)(2,1)S(1)} %collective-permute-done.8.refs_1_), channel_id=1, source_target_pairs={{0,1},{1,0},{2,3},{3,2},{4,5},{5,4},{6,7},{7,6},{8,9},{9,8},{10,11... | collective-permute-start | bytes 417800 | tf_op jit(solution)/shard_map/ppermute | solution.py:270
  84.4 1.4 %collective-permute-start.19 = (bf16[32,2176]{1,0:T(8,128)(2,1)S(1)}, bf16[32,2176]{1,0:T(8,128)(2,1)S(1)}, u32[]{:S(2)}, u32[]{:S(2)}) collective-permute-start(bf16[32,2176]{1,0:T(8,128)(2,1)S(1)} %collective-permute-done.16.refs_2_), channel_id=1, source_target_pairs={{0,1},{1,0},{2,3},{3,2},{4,5},{5,4},{6,7},{7,6},{8,9},{9,8},{10,11... | collective-permute-start | bytes 417800 | tf_op jit(solution)/shard_map/ppermute | solution.py:270
  84.6 1.4 %collective-permute-start.20 = (bf16[32,2176]{1,0:T(8,128)(2,1)S(1)}, bf16[32,2176]{1,0:T(8,128)(2,1)S(1)}, u32[]{:S(2)}, u32[]{:S(2)}) collective-permute-start(bf16[32,2176]{1,0:T(8,128)(2,1)S(1)} %collective-permute-done.10.refs_3_), channel_id=1, source_target_pairs={{0,1},{1,0},{2,3},{3,2},{4,5},{5,4},{6,7},{7,6},{8,9},{9,8},{10,11... | collective-permute-start | bytes 417800 | tf_op jit(solution)/shard_map/ppermute | solution.py:270
  84.9 9.5 %collective-permute-start.21 = (bf16[4,32,2048]{2,1,0:T(8,128)(2,1)S(1)}, bf16[4,32,2048]{2,1,0:T(8,128)(2,1)S(1)}, u32[]{:S(2)}, u32[]{:S(2)}) collective-permute-start(bf16[4,32,2048]{2,1,0:T(8,128)(2,1)S(1)} %bitcast.71), channel_id=1, source_target_pairs={{0,1},{1,0},{2,3},{3,2},{4,5},{5,4},{6,7},{7,6},{8,9},{9,8},{10,11... | collective-permute-start | bytes 1572872 | tf_op jit(solution)/shard_map/ppermute | solution.py:270
  94.4 2.0 %collective-permute-start.22 = (bf16[4,32,2048]{2,1,0:T(8,128)(2,1)S(1)}, bf16[4,32,2048]{2,1,0:T(8,128)(2,1)S(1)}, u32[]{:S(2)}, u32[]{:S(2)}) collective-permute-start(bf16[4,32,2048]{2,1,0:T(8,128)(2,1)S(1)} %bitcast.72), channel_id=1, source_target_pairs={{0,1},{1,0},{2,3},{3,2},{4,5},{5,4},{6,7},{7,6},{8,9},{9,8},{10,11... | collective-permute-start | bytes 1572872 | tf_op jit(solution)/shard_map/ppermute | solution.py:270
  96.6 6.4 %collective-permute-start.24 = (bf16[32,2048]{1,0:T(8,128)(2,1)S(1)}, bf16[32,2048]{1,0:T(8,128)(2,1)S(1)}, u32[]{:S(2)}, u32[]{:S(2)}) collective-permute-start(bf16[32,2048]{1,0:T(8,128)(2,1)S(1)} %get-tuple-element.57), channel_id=1, source_target_pairs={{0,2},{2,0},{4,6},{6,4},{8,10},{10,8},{12,14},{14,12},{1,3},{3,1},... | collective-permute-start | bytes 393224 | tf_op jit(solution)/shard_map/ppermute | solution.py:261
  97.4 7.8 %collective-permute-start.26 = (bf16[32,2048]{1,0:T(8,128)(2,1)S(1)}, bf16[32,2048]{1,0:T(8,128)(2,1)S(1)}, u32[]{:S(2)}, u32[]{:S(2)}) collective-permute-start(bf16[32,2048]{1,0:T(8,128)(2,1)S(1)} %get-tuple-element.58), channel_id=1, source_target_pairs={{0,2},{2,0},{4,6},{6,4},{8,10},{10,8},{12,14},{14,12},{1,3},{3,1},... | collective-permute-start | bytes 393224 | tf_op jit(solution)/shard_map/ppermute | solution.py:261
  98.7 10.4 %collective-permute-start.23 = (bf16[2,32,2048]{2,1,0:T(8,128)(2,1)S(1)}, bf16[2,32,2048]{2,1,0:T(8,128)(2,1)S(1)}, u32[]{:S(2)}, u32[]{:S(2)}) collective-permute-start(bf16[2,32,2048]{2,1,0:T(8,128)(2,1)S(1)} %pad_maximum_fusion), channel_id=1, source_target_pairs={{0,4},{2,6},{4,8},{6,10},{8,12},{10,14},{12,0},{14,2},{1,5},{3,7},... | collective-permute-start | bytes 786440 | tf_op jit(solution)/shard_map/ppermute | solution.py:267
  105.3 9.6 %collective-permute-start.25 = (bf16[32,2048]{1,0:T(8,128)(2,1)S(1)}, bf16[32,2048]{1,0:T(8,128)(2,1)S(1)}, u32[]{:S(2)}, u32[]{:S(2)}) collective-permute-start(bf16[32,2048]{1,0:T(8,128)(2,1)S(1)} %get-tuple-element.51), channel_id=1, source_target_pairs={{0,8},{2,10},{4,12},{6,14},{8,0},{10,2},{12,4},{14,6},{1,9},{3,11}... | collective-permute-start | bytes 393224 | tf_op jit(solution)/shard_map/ppermute | solution.py:267
  109.1 7.3 %collective-permute-start.27 = (bf16[32,2048]{1,0:T(8,128)(2,1)S(1)}, bf16[32,2048]{1,0:T(8,128)(2,1)S(1)}, u32[]{:S(2)}, u32[]{:S(2)}) collective-permute-start(bf16[32,2048]{1,0:T(8,128)(2,1)S(1)} %get-tuple-element.52), channel_id=1, source_target_pairs={{0,12},{2,14},{4,0},{6,2},{8,4},{10,6},{12,8},{14,10},{1,13},{3,15... | collective-permute-start | bytes 393224 | tf_op jit(solution)/shard_map/ppermute | solution.py:267
  109.2 7.2 %collective-permute-start.28 = (bf16[32,2048]{1,0:T(8,128)(2,1)S(1)}, bf16[32,2048]{1,0:T(8,128)(2,1)S(1)}, u32[]{:S(2)}, u32[]{:S(2)}) collective-permute-start(bf16[32,2048]{1,0:T(8,128)(2,1)S(1)} %fusion.29), channel_id=1, source_target_pairs={{0,2},{2,0},{4,6},{6,4},{8,10},{10,8},{12,14},{14,12},{1,3},{3,1},... | collective-permute-start | bytes 393224 | tf_op jit(solution)/shard_map/ppermute | solution.py:261
  (4 other events, 36.1 us)

commit v4 on v3

--- a/solution.py
+++ b/solution.py
@@ -18,13 +18,45 @@
 masked_score = -1e30
 
 
-def attend_kernel(fresh_ref, len_ref, k_ref, v_ref, o_ref):
-    rows, positions, width = k_ref.shape[1:]
+def attend_kernel(fresh_ref, len_ref, kv_ref, o_ref, near_ref, arrived):
+    steps, _, rows, width = fresh_ref.shape
+    positions = kv_ref.shape[2]
+
+    def copies(step):
+        place = pl.ds(pl.multiple_of(step * rows, rows), rows)
+        return [
+            pltpu.make_async_copy(
+                kv_ref.at[n, place], near_ref.at[n, place], arrived.at[step, n]
+            )
+            for n in range(2)
+        ]
+
+    def start(step):
+        for copy in copies(step):
+            copy.start()
+
+    for step in range(min(AHEAD, steps)):
+        start(step)
+
+    @pl.loop(0, steps)
+    def _(step):
+        @pl.when(step + AHEAD < steps)
+        def _():
+            start(step + AHEAD)
+
+        keys, values = copies(step)
+        attend_rows(step, fresh_ref, len_ref, near_ref, o_ref, keys.wait, values.wait)
+
+
+def attend_rows(step, fresh_ref, len_ref, near_ref, o_ref, keys_arrive, values_arrive):
+    rows, width = fresh_ref.shape[2:]
+    positions = near_ref.shape[2]
     heads = width // HEAD_DIM
     part = math.gcd(rows, PART)
     parts = rows // part
     group = heads * part
-    q, key_new, value_new = (fresh_ref[0, n].astype(jnp.float32) for n in range(3))
+    base = pl.multiple_of(step * rows, rows)
+    q, key_new, value_new = (fresh_ref[step, n].astype(jnp.float32) for n in range(3))
     score_scale = 1.0 / math.sqrt(HEAD_DIM)
     head_of = lax.broadcasted_iota(jnp.int32, (part, width), 1) // HEAD_DIM
     which = lax.broadcasted_iota(jnp.int32, (group, positions), 0) % part
@@ -40,13 +72,14 @@
         )
 
     own = jnp.sum(stacked(q * key_new), axis=1, keepdims=True) * score_scale
+    keys_arrive()
     pieces = []
     for g in range(parts):
         mine = q[g * part : (g + 1) * part]
         spread = jnp.concatenate(
             [jnp.where(head_of == h, mine, 0.0) for h in range(heads)], axis=0
         ).astype(jnp.bfloat16)
-        keys = k_ref[0, g * part : (g + 1) * part].reshape(part * positions, width)
+        keys = near_ref[0, pl.ds(base + g * part, part)].reshape(part * positions, width)
         every = lax.dot_general(
             spread, keys, (((1,), (1,)), ((), ())), preferred_element_type=jnp.float32
         )
@@ -57,7 +90,11 @@
             )
         pieces.append(scores)
     scores = jnp.concatenate(pieces, axis=0) * score_scale
-    lengths = len_ref[...]
+    mine = jnp.broadcast_to(len_ref[pl.ds(step, 1), :], (rows, rows))
+    diagonal = lax.broadcasted_iota(jnp.int32, (rows, rows), 0) == lax.broadcasted_iota(
+        jnp.int32, (rows, rows), 1
+    )
+    lengths = jnp.sum(jnp.where(diagonal, mine, 0), axis=1, keepdims=True)
     lengths = jnp.concatenate([lengths[g * part : (g + 1) * part] for g, h in order], axis=0)
     in_cache = lax.broadcasted_iota(jnp.int32, scores.shape, 1) < lengths
     scores = jnp.where(in_cache, scores, masked_score)
@@ -66,6 +103,7 @@
     own_weight = jnp.exp(own - top)
     total = jnp.sum(weights, axis=1, keepdims=True) + own_weight
     added = own_weight * stacked(value_new)
+    values_arrive()
     pieces = []
     for g in range(parts):
         mine = weights[g * group : (g + 1) * group]
@@ -73,7 +111,7 @@
             [jnp.where(which == row, mine, 0.0).astype(jnp.bfloat16) for row in range(part)],
             axis=1,
         )
-        values = v_ref[0, g * part : (g + 1) * part].reshape(part * positions, width)
+        values = near_ref[1, pl.ds(base + g * part, part)].reshape(part * positions, width)
         summed = lax.dot_general(
             blocks, values, (((1,), (0,)), ((), ())), preferred_element_type=jnp.float32
         )
@@ -95,30 +133,29 @@
         ],
         axis=0,
     )
-    o_ref[...] = attended.astype(jnp.bfloat16)
+    o_ref[pl.ds(base, rows), :] = attended.astype(jnp.bfloat16)
 
 
 def attend(fresh, lengths, kv):
     _, n, positions, width = kv.shape
-    rows = fresh.shape[2]
+    steps = fresh.shape[0]
+    inside = pl.BlockSpec(memory_space=pltpu.VMEM)
     return pl.pallas_call(
         attend_kernel,
-        grid=(n // rows,),
-        in_specs=[
-            pl.BlockSpec((1, 3, rows, width), lambda i: (i, 0, 0, 0)),
-            pl.BlockSpec((rows, 1), lambda i: (i, 0)),
-            pl.BlockSpec((1, rows, positions, width), lambda i: (0, i, 0, 0)),
-            pl.BlockSpec((1, rows, positions, width), lambda i: (1, i, 0, 0)),
+        in_specs=[inside, inside, pl.BlockSpec(memory_space=pl.ANY)],
+        out_specs=inside,
+        out_shape=jax.ShapeDtypeStruct((n, width), jnp.bfloat16),
+        scratch_shapes=[
+            pltpu.VMEM(kv.shape, kv.dtype),
+            pltpu.SemaphoreType.DMA((steps, 2)),
         ],
-        out_specs=pl.BlockSpec((rows, width), lambda i: (i, 0)),
-        out_shape=jax.ShapeDtypeStruct((n, width), jnp.bfloat16),
-        compiler_params=pltpu.CompilerParams(vmem_limit_bytes=28 << 20),
+        compiler_params=pltpu.CompilerParams(vmem_limit_bytes=VMEM_LIMIT),
         cost_estimate=pl.CostEstimate(
             flops=4 * n * positions * width,
             bytes_accessed=4 * n * positions * width,
             transcendentals=0,
         ),
-    )(fresh, lengths, kv, kv)
+    )(fresh, lengths, kv)
 
 
 def pieces_of(size, most):
@@ -290,11 +327,11 @@
         w_mine = jnp.where(rep_first, w_out[:half], w_out[half:])
     else:
         w_mine = w_out
-    fresh, w_both, w_mine = lax.optimization_barrier((fresh, w_both, w_mine))
+    fresh, w_both, w_mine = fence(fresh, w_both, w_mine)
     w_mine = across(w_mine) if inner == 2 else w_mine
 
     kv = kv_cache.reshape(2, attend_rows, positions, width_local)
-    attended = attend(fresh, cache_len.reshape(attend_rows, 1), kv)
+    attended = attend(fresh, cache_len.reshape(attend_rows // tile, tile), kv)
     attended, w_mine = lax.optimization_barrier((attended, w_mine))
     attended = attended.reshape(owners, share_rows, width_local)
     attended = lax.all_gather(attended, "seq", axis=1, tiled=True)

time: 117 us -> 115 us (0.983)
  Pallas kernels: 31.3 us -> 28.9 us
    pallas_call x1, Pallas kernels: 14.5 us -> 12.1 us  [attend(): pl.pallas_call(attend_kernel, in_specs=[inside, inside, pl.BlockSpec(memo...]
  transfers between devices with their start and end apart: 30 -> 30, of which waited for: 20 -> 20; matrix products, arithmetic and copies ran while one was open for 10% -> 10% of each run, Pallas kernels for 27% -> 25%
where the time goes in v4:
time: 115 us
  waiting for transfers between devices  40.7 us (35%)
  Pallas kernels  28.9 us (25%)
  starting transfers between devices  28.2 us (25%)
  local copies, waits for them, and re-layouts  13.3 us (12%)
  other arithmetic  1.8 us (2%)
    ppermute x9, waiting for transfers between devices, along(): return lax.ppermute(v, 'ep', pairs)  27.5 us
    pallas_call x2, Pallas kernels, expert(): pl.pallas_call(functools.partial(expert_kernel, len(slots), outs), in_spe...  16.8 us
    pallas_call x1, Pallas kernels, attend(): pl.pallas_call(attend_kernel, in_specs=[inside, inside, pl.BlockSpec(memo...  12.1 us
    ppermute x9, starting transfers between devices, along(): return lax.ppermute(v, 'ep', pairs)  12 us
    unnamed x13, local copies, waits for them, and re-layouts  11.4 us
    ppermute x9, waiting for transfers between devices, across(): return lax.ppermute(v, 'ep', [(i, i ^ 1) for i in range(owners)])  9.66 us
    all_to_all x1, starting transfers between devices, local(): fresh = lax.all_to_all(sent, 'ep', split_axis=0, concat_axis=0, tiled=True)  7.25 us
    ppermute x9, starting transfers between devices, across(): return lax.ppermute(v, 'ep', [(i, i ^ 1) for i in range(owners)])  6.77 us
  transfers between devices with their start and end apart: 30, of which 20 were waited for; matrix products, arithmetic and copies ran while one was open for 10% of the time, Pallas kernels for 25%

profile of v4, /device:TPU:0, one launch (start us, length us, event | category | flops | bytes accessed | tf_op | source)
XLA Modules:
  0.0 114.6 jit_solution(17584746655367638644)
XLA Ops:
  0.0 1.8 %copy.46 = bf16[3,4,8,8,256]{4,3,1,0,2:T(8,128)(2,1)} copy(bf16[3,4,8,8,256]{4,3,2,1,0:T(8,128)(2,1)} %bitcast.78) | data formatting | bytes 786432 | tf_op jit(solution)/shard_map/reshape | solution.py:315
  1.8 7.3 %all-to-all-start = ((bf16[8,3,32,256]{3,2,1,0:T(8,128)(2,1)}), bf16[8,3,32,256]{3,2,1,0:T(8,128)(2,1)S(1)}, u32[]{:S(2)}, u32[]{:S(2)}) async-start(bf16[8,3,32,256]{3,2,1,0:T(8,128)(2,1)} %bitcast.65), calls=%async_computation | async-start | bytes 786432 | tf_op jit(solution)/shard_map/all_to_all | solution.py:316
  9.1 11.3 %copy.45 = bf16[1,2048,2,1408]{3,1,2,0:T(8,128)(2,1)} copy(bf16[1,2048,2,1408]{3,2,1,0:T(2,128)(2,1)} %param.18) | data formatting | bytes 23068672 | tf_op args[7]
  20.8 1.8 %collective-permute-start = (bf16[128,2048]{1,0:T(8,128)(2,1)S(1)}, bf16[128,2048]{1,0:T(8,128)(2,1)S(1)}, u32[]{:S(2)}, u32[]{:S(2)}) collective-permute-start(bf16[128,2048]{1,0:T(8,128)(2,1)S(1)} %slice_select_fusion), channel_id=1, source_target_pairs={{0,2},{2,0},{4,6},{6,4},{8,10},{10,8},{12,14},{14,12},{1,3},{3,1},... | collective-permute-start | bytes 1572872 | tf_op jit(solution)/shard_map/ppermute | solution.py:298
  23.2 12.1 %shard_map.109 = bf16[256,256]{1,0:T(8,128)(2,1)S(1)} custom-call(bf16[8,3,32,256]{3,2,1,0:T(8,128)(2,1)S(1)} %all-to-all-done.fresh_ref, s32[8,32]{1,0:T(8,128)S(1)} %copy-done, bf16[2,256,128,256]{3,2,1,0:T(8,128)(2,1)} %bitcast.75), custom_call_target="tpu_custom_call" | custom-call | flops 33554432 | bytes 33554432 | tf_op jit(solution)/shard_map/pallas_call | solution.py:143
  35.8 4.2 %collective-permute-done.1 = bf16[4,32,256]{2,1,0:T(8,128)(2,1)S(1)} collective-permute-done((bf16[4,32,256]{2,1,0:T(8,128)(2,1)S(1)}, bf16[4,32,256]{2,1,0:T(8,128)(2,1)S(1)}, u32[]{:S(2)}, u32[]{:S(2)}) %collective-permute-start.1) | collective-permute-done | bytes 65568 | tf_op jit(solution)/shard_map/ppermute | solution.py:298
  40.2 0.7 fusion.37
  40.9 1.5 %collective-permute-start.3 = (bf16[32,2048]{1,0:T(8,128)(2,1)S(1)}, bf16[32,2048]{1,0:T(8,128)(2,1)S(1)}, u32[]{:S(2)}, u32[]{:S(2)}) collective-permute-start(bf16[32,2048]{1,0:T(8,128)(2,1)S(1)} %get-tuple-element.60), channel_id=1, source_target_pairs={{0,4},{2,6},{4,8},{6,10},{8,12},{10,14},{12,0},{14,2},{1,5},{3,7},... | collective-permute-start | bytes 393224 | tf_op jit(solution)/shard_map/ppermute | solution.py:304
  42.5 2.4 %collective-permute-start.5 = (bf16[32,2048]{1,0:T(8,128)(2,1)S(1)}, bf16[32,2048]{1,0:T(8,128)(2,1)S(1)}, u32[]{:S(2)}, u32[]{:S(2)}) collective-permute-start(bf16[32,2048]{1,0:T(8,128)(2,1)S(1)} %get-tuple-element.61), channel_id=1, source_target_pairs={{0,12},{2,14},{4,0},{6,2},{8,4},{10,6},{12,8},{14,10},{1,13},{3,15... | collective-permute-start | bytes 393224 | tf_op jit(solution)/shard_map/ppermute | solution.py:304
  44.8 0.6 collective-permute-start.4
  45.5 3.7 %collective-permute-done.3 = bf16[32,2048]{1,0:T(8,128)(2,1)S(1)} collective-permute-done((bf16[32,2048]{1,0:T(8,128)(2,1)S(1)}, bf16[32,2048]{1,0:T(8,128)(2,1)S(1)}, u32[]{:S(2)}, u32[]{:S(2)}) %collective-permute-start.3) | collective-permute-done | bytes 131104 | tf_op jit(solution)/shard_map/ppermute | solution.py:304
  49.2 0.9 collective-permute-done.5
  50.1 6.2 %collective-permute-done.4 = bf16[32,2048]{1,0:T(8,128)(2,1)S(1)} collective-permute-done((bf16[32,2048]{1,0:T(8,128)(2,1)S(1)}, bf16[32,2048]{1,0:T(8,128)(2,1)S(1)}, u32[]{:S(2)}, u32[]{:S(2)}) %collective-permute-start.4) | collective-permute-done | bytes 131104 | tf_op jit(solution)/shard_map/ppermute | solution.py:304
  56.7 1.5 %collective-permute-start.9 = (bf16[32,2176]{1,0:T(8,128)(2,1)S(1)}, bf16[32,2176]{1,0:T(8,128)(2,1)S(1)}, u32[]{:S(2)}, u32[]{:S(2)}) collective-permute-start(bf16[32,2176]{1,0:T(8,128)(2,1)S(1)} %fusion.25.refs_0_), channel_id=1, source_target_pairs={{0,12},{2,14},{4,0},{6,2},{8,4},{10,6},{12,8},{14,10},{1,13},{3,15... | collective-permute-start | bytes 417800 | tf_op jit(solution)/shard_map/ppermute | solution.py:304
  59.0 0.6 collective-permute-start.7
  59.6 4.8 %collective-permute-done.9.refs_3_ = bf16[32,2176]{1,0:T(8,128)(2,1)S(1)} collective-permute-done((bf16[32,2176]{1,0:T(8,128)(2,1)S(1)}, bf16[32,2176]{1,0:T(8,128)(2,1)S(1)}, u32[]{:S(2)}, u32[]{:S(2)}) %collective-permute-start.9) | collective-permute-done | bytes 139296 | tf_op jit(solution)/shard_map/ppermute | solution.py:304
  64.7 1.7 %collective-permute-done.6.refs_1_ = bf16[32,2176]{1,0:T(8,128)(2,1)S(1)} collective-permute-done((bf16[32,2176]{1,0:T(8,128)(2,1)S(1)}, bf16[32,2176]{1,0:T(8,128)(2,1)S(1)}, u32[]{:S(2)}, u32[]{:S(2)}) %collective-permute-start.6) | collective-permute-done | bytes 139296 | tf_op jit(solution)/shard_map/ppermute | solution.py:304
  66.9 3.7 %collective-permute-done.11.refs_2_ = bf16[32,2176]{1,0:T(8,128)(2,1)S(1)} collective-permute-done((bf16[32,2176]{1,0:T(8,128)(2,1)S(1)}, bf16[32,2176]{1,0:T(8,128)(2,1)S(1)}, u32[]{:S(2)}, u32[]{:S(2)}) %collective-permute-start.11) | collective-permute-done | bytes 139296 | tf_op jit(solution)/shard_map/ppermute | solution.py:304
  72.2 0.7 collective-permute-done.14.refs_6_
  72.9 8.4 %shard_map.110 = (bf16[128,2048]{1,0:T(8,128)(2,1)S(1)}, bf16[128,2048]{1,0:T(8,128)(2,1)S(1)}) custom-call(s32[1]{0:T(128)} %bitcast.11.mine_ref, bf16[32,2176]{1,0:T(8,128)(2,1)S(1)} %fusion.25.refs_0_, bf16[32,2176]{1,0:T(8,128)(2,1)S(1)} %collective-permute-done.6.refs_1_, bf16[32,2176]{1,0:T(8,128)(2,1)S(1)} %collective-permute-done.11.refs_2_, ...), custom_call_target="tpu_custom_call" | custom-call | flops 4429185024 | bytes 19398656 | tf_op jit(solution)/shard_map/pallas_call | solution.py:244
  83.4 8.4 %shard_map.111 = (bf16[128,2048]{1,0:T(8,128)(2,1)S(1)}, bf16[128,2048]{1,0:T(8,128)(2,1)S(1)}) custom-call(s32[1]{0:T(128)} %bitcast.11.mine_ref, bf16[32,2176]{1,0:T(8,128)(2,1)S(1)} %collective-permute-done.7.refs_0_, bf16[32,2176]{1,0:T(8,128)(2,1)S(1)} %collective-permute-done.8.refs_1_, bf16[32,2176]{1,0:T(8,128)(2,1)S(1)} %collective-permute-done.16.refs_2_, ...), custom_call_target="tpu_custom_call" | custom-call | flops 4429185024 | bytes 19398656 | tf_op jit(solution)/shard_map/pallas_call | solution.py:244
  92.4 1.4 %collective-permute-done.22 = bf16[4,32,2048]{2,1,0:T(8,128)(2,1)S(1)} collective-permute-done((bf16[4,32,2048]{2,1,0:T(8,128)(2,1)S(1)}, bf16[4,32,2048]{2,1,0:T(8,128)(2,1)S(1)}, u32[]{:S(2)}, u32[]{:S(2)}) %collective-permute-start.22) | collective-permute-done | bytes 524320 | tf_op jit(solution)/shard_map/ppermute | solution.py:307
  94.0 0.8 collective-permute-start.24
  94.8 1.3 %collective-permute-start.26 = (bf16[32,2048]{1,0:T(8,128)(2,1)S(1)}, bf16[32,2048]{1,0:T(8,128)(2,1)S(1)}, u32[]{:S(2)}, u32[]{:S(2)}) collective-permute-start(bf16[32,2048]{1,0:T(8,128)(2,1)S(1)} %get-tuple-element.58), channel_id=1, source_target_pairs={{0,2},{2,0},{4,6},{6,4},{8,10},{10,8},{12,14},{14,12},{1,3},{3,1},... | collective-permute-start | bytes 393224 | tf_op jit(solution)/shard_map/ppermute | solution.py:298
  96.2 1.4 %collective-permute-start.23 = (bf16[2,32,2048]{2,1,0:T(8,128)(2,1)S(1)}, bf16[2,32,2048]{2,1,0:T(8,128)(2,1)S(1)}, u32[]{:S(2)}, u32[]{:S(2)}) collective-permute-start(bf16[2,32,2048]{2,1,0:T(8,128)(2,1)S(1)} %pad_maximum_fusion), channel_id=1, source_target_pairs={{0,4},{2,6},{4,8},{6,10},{8,12},{10,14},{12,0},{14,2},{1,5},{3,7},... | collective-permute-start | bytes 786440 | tf_op jit(solution)/shard_map/ppermute | solution.py:304
  97.5 2.9 %collective-permute-done.24 = bf16[32,2048]{1,0:T(8,128)(2,1)S(1)} collective-permute-done((bf16[32,2048]{1,0:T(8,128)(2,1)S(1)}, bf16[32,2048]{1,0:T(8,128)(2,1)S(1)}, u32[]{:S(2)}, u32[]{:S(2)}) %collective-permute-start.24) | collective-permute-done | bytes 131104 | tf_op jit(solution)/shard_map/ppermute | solution.py:298
  100.4 2.2 %collective-permute-done.26 = bf16[32,2048]{1,0:T(8,128)(2,1)S(1)} collective-permute-done((bf16[32,2048]{1,0:T(8,128)(2,1)S(1)}, bf16[32,2048]{1,0:T(8,128)(2,1)S(1)}, u32[]{:S(2)}, u32[]{:S(2)}) %collective-permute-start.26) | collective-permute-done | bytes 131104 | tf_op jit(solution)/shard_map/ppermute | solution.py:298
  102.7 3.9 %collective-permute-start.25 = (bf16[32,2048]{1,0:T(8,128)(2,1)S(1)}, bf16[32,2048]{1,0:T(8,128)(2,1)S(1)}, u32[]{:S(2)}, u32[]{:S(2)}) collective-permute-start(bf16[32,2048]{1,0:T(8,128)(2,1)S(1)} %get-tuple-element.51), channel_id=1, source_target_pairs={{0,8},{2,10},{4,12},{6,14},{8,0},{10,2},{12,4},{14,6},{1,9},{3,11}... | collective-permute-start | bytes 393224 | tf_op jit(solution)/shard_map/ppermute | solution.py:304
  106.7 0.8 collective-permute-start.28
  107.4 4.9 %collective-permute-done.25 = bf16[32,2048]{1,0:T(8,128)(2,1)S(1)} collective-permute-done((bf16[32,2048]{1,0:T(8,128)(2,1)S(1)}, bf16[32,2048]{1,0:T(8,128)(2,1)S(1)}, u32[]{:S(2)}, u32[]{:S(2)}) %collective-permute-start.25) | collective-permute-done | bytes 131104 | tf_op jit(solution)/shard_map/ppermute | solution.py:304
  112.3 1.6 %collective-permute-done.27 = bf16[32,2048]{1,0:T(8,128)(2,1)S(1)} collective-permute-done((bf16[32,2048]{1,0:T(8,128)(2,1)S(1)}, bf16[32,2048]{1,0:T(8,128)(2,1)S(1)}, u32[]{:S(2)}, u32[]{:S(2)}) %collective-permute-start.27) | collective-permute-done | bytes 131104 | tf_op jit(solution)/shard_map/ppermute | solution.py:304
  113.8 0.8 fusion.11
  (69 shorter events, 7.6 us)
Async XLA Ops:
  1.8 18.9 %all-to-all-start = ((bf16[8,3,32,256]{3,2,1,0:T(8,128)(2,1)}), bf16[8,3,32,256]{3,2,1,0:T(8,128)(2,1)S(1)}, u32[]{:S(2)}, u32[]{:S(2)}) async-start(bf16[8,3,32,256]{3,2,1,0:T(8,128)(2,1)} %bitcast.65), calls=%async_computation | async-start | bytes 786432 | tf_op jit(solution)/shard_map/all_to_all | solution.py:316
  20.8 14.6 %collective-permute-start = (bf16[128,2048]{1,0:T(8,128)(2,1)S(1)}, bf16[128,2048]{1,0:T(8,128)(2,1)S(1)}, u32[]{:S(2)}, u32[]{:S(2)}) collective-permute-start(bf16[128,2048]{1,0:T(8,128)(2,1)S(1)} %slice_select_fusion), channel_id=1, source_target_pairs={{0,2},{2,0},{4,6},{6,4},{8,10},{10,8},{12,14},{14,12},{1,3},{3,1},... | collective-permute-start | bytes 1572872 | tf_op jit(solution)/shard_map/ppermute | solution.py:298
  35.3 4.8 %collective-permute-start.2 = (bf16[128,2048]{1,0:T(8,128)(2,1)S(1)}, bf16[128,2048]{1,0:T(8,128)(2,1)S(1)}, u32[]{:S(2)}, u32[]{:S(2)}) collective-permute-start(bf16[128,2048]{1,0:T(8,128)(2,1)S(1)} %collective-permute-done), channel_id=1, source_target_pairs={{0,1},{1,0},{2,3},{3,2},{4,5},{5,4},{6,7},{7,6},{8,9},{9,8},{10,11... | collective-permute-start | bytes 1572872 | tf_op jit(solution)/shard_map/ppermute | solution.py:307
  35.4 4.6 %collective-permute-start.1 = (bf16[4,32,256]{2,1,0:T(8,128)(2,1)S(1)}, bf16[4,32,256]{2,1,0:T(8,128)(2,1)S(1)}, u32[]{:S(2)}, u32[]{:S(2)}) collective-permute-start(bf16[4,32,256]{2,1,0:T(8,128)(2,1)S(1)} %fusion.30), channel_id=1, source_target_pairs={{0,2},{2,0},{4,6},{6,4},{8,10},{10,8},{12,14},{14,12},{1,3},{3,1},... | collective-permute-start | bytes 196616 | tf_op jit(solution)/shard_map/ppermute | solution.py:298
  40.1 16.2 %copy-start.2 = (bf16[32,2048]{1,0:T(8,128)(2,1)S(1)}, bf16[32,2048]{1,0:T(8,128)(2,1)}, u32[]{:S(2)}) copy-start(bf16[32,2048]{1,0:T(8,128)(2,1)} %param.11) | copy-start | bytes 393220
  40.2 16.3 %copy-start.3 = (f32[2048]{0:T(1024)S(1)}, f32[2048]{0:T(1024)}, u32[]{:S(2)}) copy-start(f32[2048]{0:T(1024)} %param.17) | copy-start | bytes 24580
  40.9 8.3 %collective-permute-start.3 = (bf16[32,2048]{1,0:T(8,128)(2,1)S(1)}, bf16[32,2048]{1,0:T(8,128)(2,1)S(1)}, u32[]{:S(2)}, u32[]{:S(2)}) collective-permute-start(bf16[32,2048]{1,0:T(8,128)(2,1)S(1)} %get-tuple-element.60), channel_id=1, source_target_pairs={{0,4},{2,6},{4,8},{6,10},{8,12},{10,14},{12,0},{14,2},{1,5},{3,7},... | collective-permute-start | bytes 393224 | tf_op jit(solution)/shard_map/ppermute | solution.py:304
  42.5 7.6 %collective-permute-start.5 = (bf16[32,2048]{1,0:T(8,128)(2,1)S(1)}, bf16[32,2048]{1,0:T(8,128)(2,1)S(1)}, u32[]{:S(2)}, u32[]{:S(2)}) collective-permute-start(bf16[32,2048]{1,0:T(8,128)(2,1)S(1)} %get-tuple-element.61), channel_id=1, source_target_pairs={{0,12},{2,14},{4,0},{6,2},{8,4},{10,6},{12,8},{14,10},{1,13},{3,15... | collective-permute-start | bytes 393224 | tf_op jit(solution)/shard_map/ppermute | solution.py:304
  44.8 11.5 %collective-permute-start.4 = (bf16[32,2048]{1,0:T(8,128)(2,1)S(1)}, bf16[32,2048]{1,0:T(8,128)(2,1)S(1)}, u32[]{:S(2)}, u32[]{:S(2)}) collective-permute-start(bf16[32,2048]{1,0:T(8,128)(2,1)S(1)} %get-tuple-element.62), channel_id=1, source_target_pairs={{0,8},{2,10},{4,12},{6,14},{8,0},{10,2},{12,4},{14,6},{1,9},{3,11}... | collective-permute-start | bytes 393224 | tf_op jit(solution)/shard_map/ppermute | solution.py:304
  56.7 7.7 %collective-permute-start.9 = (bf16[32,2176]{1,0:T(8,128)(2,1)S(1)}, bf16[32,2176]{1,0:T(8,128)(2,1)S(1)}, u32[]{:S(2)}, u32[]{:S(2)}) collective-permute-start(bf16[32,2176]{1,0:T(8,128)(2,1)S(1)} %fusion.25.refs_0_), channel_id=1, source_target_pairs={{0,12},{2,14},{4,0},{6,2},{8,4},{10,6},{12,8},{14,10},{1,13},{3,15... | collective-permute-start | bytes 417800 | tf_op jit(solution)/shard_map/ppermute | solution.py:304
  58.2 8.3 %collective-permute-start.6 = (bf16[32,2176]{1,0:T(8,128)(2,1)S(1)}, bf16[32,2176]{1,0:T(8,128)(2,1)S(1)}, u32[]{:S(2)}, u32[]{:S(2)}) collective-permute-start(bf16[32,2176]{1,0:T(8,128)(2,1)S(1)} %fusion.25.refs_0_), channel_id=1, source_target_pairs={{0,4},{2,6},{4,8},{6,10},{8,12},{10,14},{12,0},{14,2},{1,5},{3,7},... | collective-permute-start | bytes 417800 | tf_op jit(solution)/shard_map/ppermute | solution.py:304
  58.8 11.9 %collective-permute-start.11 = (bf16[32,2176]{1,0:T(8,128)(2,1)S(1)}, bf16[32,2176]{1,0:T(8,128)(2,1)S(1)}, u32[]{:S(2)}, u32[]{:S(2)}) collective-permute-start(bf16[32,2176]{1,0:T(8,128)(2,1)S(1)} %fusion.25.refs_0_), channel_id=1, source_target_pairs={{0,8},{2,10},{4,12},{6,14},{8,0},{10,2},{12,4},{14,6},{1,9},{3,11}... | collective-permute-start | bytes 417800 | tf_op jit(solution)/shard_map/ppermute | solution.py:304
  59.0 11.6 %collective-permute-start.7 = (bf16[32,2176]{1,0:T(8,128)(2,1)S(1)}, bf16[32,2176]{1,0:T(8,128)(2,1)S(1)}, u32[]{:S(2)}, u32[]{:S(2)}) collective-permute-start(bf16[32,2176]{1,0:T(8,128)(2,1)S(1)} %fusion.25.refs_0_), channel_id=1, source_target_pairs={{0,2},{2,0},{4,6},{6,4},{8,10},{10,8},{12,14},{14,12},{1,3},{3,1},... | collective-permute-start | bytes 417800 | tf_op jit(solution)/shard_map/ppermute | solution.py:298
  64.4 6.8 %collective-permute-start.10 = (bf16[32,2176]{1,0:T(8,128)(2,1)S(1)}, bf16[32,2176]{1,0:T(8,128)(2,1)S(1)}, u32[]{:S(2)}, u32[]{:S(2)}) collective-permute-start(bf16[32,2176]{1,0:T(8,128)(2,1)S(1)} %collective-permute-done.9.refs_3_), channel_id=1, source_target_pairs={{0,2},{2,0},{4,6},{6,4},{8,10},{10,8},{12,14},{14,12},{1,3},{3,1},... | collective-permute-start | bytes 417800 | tf_op jit(solution)/shard_map/ppermute | solution.py:298
  66.4 5.1 %collective-permute-start.8 = (bf16[32,2176]{1,0:T(8,128)(2,1)S(1)}, bf16[32,2176]{1,0:T(8,128)(2,1)S(1)}, u32[]{:S(2)}, u32[]{:S(2)}) collective-permute-start(bf16[32,2176]{1,0:T(8,128)(2,1)S(1)} %collective-permute-done.6.refs_1_), channel_id=1, source_target_pairs={{0,2},{2,0},{4,6},{6,4},{8,10},{10,8},{12,14},{14,12},{1,3},{3,1},... | collective-permute-start | bytes 417800 | tf_op jit(solution)/shard_map/ppermute | solution.py:298
  66.9 5.1 %collective-permute-start.12 = (bf16[32,2176]{1,0:T(8,128)(2,1)S(1)}, bf16[32,2176]{1,0:T(8,128)(2,1)S(1)}, u32[]{:S(2)}, u32[]{:S(2)}) collective-permute-start(bf16[32,2176]{1,0:T(8,128)(2,1)S(1)} %fusion.25.refs_0_), channel_id=1, source_target_pairs={{0,1},{1,0},{2,3},{3,2},{4,5},{5,4},{6,7},{7,6},{8,9},{9,8},{10,11... | collective-permute-start | bytes 417800 | tf_op jit(solution)/shard_map/ppermute | solution.py:307
  70.6 1.4 %collective-permute-start.15 = (bf16[32,2176]{1,0:T(8,128)(2,1)S(1)}, bf16[32,2176]{1,0:T(8,128)(2,1)S(1)}, u32[]{:S(2)}, u32[]{:S(2)}) collective-permute-start(bf16[32,2176]{1,0:T(8,128)(2,1)S(1)} %collective-permute-done.9.refs_3_), channel_id=1, source_target_pairs={{0,1},{1,0},{2,3},{3,2},{4,5},{5,4},{6,7},{7,6},{8,9},{9,8},{10,11... | collective-permute-start | bytes 417800 | tf_op jit(solution)/shard_map/ppermute | solution.py:307
  70.6 1.6 %collective-permute-start.13 = (bf16[32,2176]{1,0:T(8,128)(2,1)S(1)}, bf16[32,2176]{1,0:T(8,128)(2,1)S(1)}, u32[]{:S(2)}, u32[]{:S(2)}) collective-permute-start(bf16[32,2176]{1,0:T(8,128)(2,1)S(1)} %collective-permute-done.6.refs_1_), channel_id=1, source_target_pairs={{0,1},{1,0},{2,3},{3,2},{4,5},{5,4},{6,7},{7,6},{8,9},{9,8},{10,11... | collective-permute-start | bytes 417800 | tf_op jit(solution)/shard_map/ppermute | solution.py:307
  71.5 1.4 %collective-permute-start.14 = (bf16[32,2176]{1,0:T(8,128)(2,1)S(1)}, bf16[32,2176]{1,0:T(8,128)(2,1)S(1)}, u32[]{:S(2)}, u32[]{:S(2)}) collective-permute-start(bf16[32,2176]{1,0:T(8,128)(2,1)S(1)} %collective-permute-done.11.refs_2_), channel_id=1, source_target_pairs={{0,1},{1,0},{2,3},{3,2},{4,5},{5,4},{6,7},{7,6},{8,9},{9,8},{10,11... | collective-permute-start | bytes 417800 | tf_op jit(solution)/shard_map/ppermute | solution.py:307
  71.5 9.8 %collective-permute-start.16 = (bf16[32,2176]{1,0:T(8,128)(2,1)S(1)}, bf16[32,2176]{1,0:T(8,128)(2,1)S(1)}, u32[]{:S(2)}, u32[]{:S(2)}) collective-permute-start(bf16[32,2176]{1,0:T(8,128)(2,1)S(1)} %collective-permute-done.11.refs_2_), channel_id=1, source_target_pairs={{0,2},{2,0},{4,6},{6,4},{8,10},{10,8},{12,14},{14,12},{1,3},{3,1},... | collective-permute-start | bytes 417800 | tf_op jit(solution)/shard_map/ppermute | solution.py:298
  81.3 1.4 %collective-permute-start.17 = (bf16[32,2176]{1,0:T(8,128)(2,1)S(1)}, bf16[32,2176]{1,0:T(8,128)(2,1)S(1)}, u32[]{:S(2)}, u32[]{:S(2)}) collective-permute-start(bf16[32,2176]{1,0:T(8,128)(2,1)S(1)} %collective-permute-done.7.refs_0_), channel_id=1, source_target_pairs={{0,1},{1,0},{2,3},{3,2},{4,5},{5,4},{6,7},{7,6},{8,9},{9,8},{10,11... | collective-permute-start | bytes 417800 | tf_op jit(solution)/shard_map/ppermute | solution.py:307
  81.5 1.4 %collective-permute-start.18 = (bf16[32,2176]{1,0:T(8,128)(2,1)S(1)}, bf16[32,2176]{1,0:T(8,128)(2,1)S(1)}, u32[]{:S(2)}, u32[]{:S(2)}) collective-permute-start(bf16[32,2176]{1,0:T(8,128)(2,1)S(1)} %collective-permute-done.8.refs_1_), channel_id=1, source_target_pairs={{0,1},{1,0},{2,3},{3,2},{4,5},{5,4},{6,7},{7,6},{8,9},{9,8},{10,11... | collective-permute-start | bytes 417800 | tf_op jit(solution)/shard_map/ppermute | solution.py:307
  81.9 1.4 %collective-permute-start.19 = (bf16[32,2176]{1,0:T(8,128)(2,1)S(1)}, bf16[32,2176]{1,0:T(8,128)(2,1)S(1)}, u32[]{:S(2)}, u32[]{:S(2)}) collective-permute-start(bf16[32,2176]{1,0:T(8,128)(2,1)S(1)} %collective-permute-done.16.refs_2_), channel_id=1, source_target_pairs={{0,1},{1,0},{2,3},{3,2},{4,5},{5,4},{6,7},{7,6},{8,9},{9,8},{10,11... | collective-permute-start | bytes 417800 | tf_op jit(solution)/shard_map/ppermute | solution.py:307
  82.0 1.4 %collective-permute-start.20 = (bf16[32,2176]{1,0:T(8,128)(2,1)S(1)}, bf16[32,2176]{1,0:T(8,128)(2,1)S(1)}, u32[]{:S(2)}, u32[]{:S(2)}) collective-permute-start(bf16[32,2176]{1,0:T(8,128)(2,1)S(1)} %collective-permute-done.10.refs_3_), channel_id=1, source_target_pairs={{0,1},{1,0},{2,3},{3,2},{4,5},{5,4},{6,7},{7,6},{8,9},{9,8},{10,11... | collective-permute-start | bytes 417800 | tf_op jit(solution)/shard_map/ppermute | solution.py:307
  82.4 9.5 %collective-permute-start.21 = (bf16[4,32,2048]{2,1,0:T(8,128)(2,1)S(1)}, bf16[4,32,2048]{2,1,0:T(8,128)(2,1)S(1)}, u32[]{:S(2)}, u32[]{:S(2)}) collective-permute-start(bf16[4,32,2048]{2,1,0:T(8,128)(2,1)S(1)} %bitcast.71), channel_id=1, source_target_pairs={{0,1},{1,0},{2,3},{3,2},{4,5},{5,4},{6,7},{7,6},{8,9},{9,8},{10,11... | collective-permute-start | bytes 1572872 | tf_op jit(solution)/shard_map/ppermute | solution.py:307
  91.9 2.0 %collective-permute-start.22 = (bf16[4,32,2048]{2,1,0:T(8,128)(2,1)S(1)}, bf16[4,32,2048]{2,1,0:T(8,128)(2,1)S(1)}, u32[]{:S(2)}, u32[]{:S(2)}) collective-permute-start(bf16[4,32,2048]{2,1,0:T(8,128)(2,1)S(1)} %bitcast.72), channel_id=1, source_target_pairs={{0,1},{1,0},{2,3},{3,2},{4,5},{5,4},{6,7},{7,6},{8,9},{9,8},{10,11... | collective-permute-start | bytes 1572872 | tf_op jit(solution)/shard_map/ppermute | solution.py:307
  94.0 6.4 %collective-permute-start.24 = (bf16[32,2048]{1,0:T(8,128)(2,1)S(1)}, bf16[32,2048]{1,0:T(8,128)(2,1)S(1)}, u32[]{:S(2)}, u32[]{:S(2)}) collective-permute-start(bf16[32,2048]{1,0:T(8,128)(2,1)S(1)} %get-tuple-element.57), channel_id=1, source_target_pairs={{0,2},{2,0},{4,6},{6,4},{8,10},{10,8},{12,14},{14,12},{1,3},{3,1},... | collective-permute-start | bytes 393224 | tf_op jit(solution)/shard_map/ppermute | solution.py:298
  94.8 7.8 %collective-permute-start.26 = (bf16[32,2048]{1,0:T(8,128)(2,1)S(1)}, bf16[32,2048]{1,0:T(8,128)(2,1)S(1)}, u32[]{:S(2)}, u32[]{:S(2)}) collective-permute-start(bf16[32,2048]{1,0:T(8,128)(2,1)S(1)} %get-tuple-element.58), channel_id=1, source_target_pairs={{0,2},{2,0},{4,6},{6,4},{8,10},{10,8},{12,14},{14,12},{1,3},{3,1},... | collective-permute-start | bytes 393224 | tf_op jit(solution)/shard_map/ppermute | solution.py:298
  96.2 10.4 %collective-permute-start.23 = (bf16[2,32,2048]{2,1,0:T(8,128)(2,1)S(1)}, bf16[2,32,2048]{2,1,0:T(8,128)(2,1)S(1)}, u32[]{:S(2)}, u32[]{:S(2)}) collective-permute-start(bf16[2,32,2048]{2,1,0:T(8,128)(2,1)S(1)} %pad_maximum_fusion), channel_id=1, source_target_pairs={{0,4},{2,6},{4,8},{6,10},{8,12},{10,14},{12,0},{14,2},{1,5},{3,7},... | collective-permute-start | bytes 786440 | tf_op jit(solution)/shard_map/ppermute | solution.py:304
  102.7 9.6 %collective-permute-start.25 = (bf16[32,2048]{1,0:T(8,128)(2,1)S(1)}, bf16[32,2048]{1,0:T(8,128)(2,1)S(1)}, u32[]{:S(2)}, u32[]{:S(2)}) collective-permute-start(bf16[32,2048]{1,0:T(8,128)(2,1)S(1)} %get-tuple-element.51), channel_id=1, source_target_pairs={{0,8},{2,10},{4,12},{6,14},{8,0},{10,2},{12,4},{14,6},{1,9},{3,11}... | collective-permute-start | bytes 393224 | tf_op jit(solution)/shard_map/ppermute | solution.py:304
  106.6 7.3 %collective-permute-start.27 = (bf16[32,2048]{1,0:T(8,128)(2,1)S(1)}, bf16[32,2048]{1,0:T(8,128)(2,1)S(1)}, u32[]{:S(2)}, u32[]{:S(2)}) collective-permute-start(bf16[32,2048]{1,0:T(8,128)(2,1)S(1)} %get-tuple-element.52), channel_id=1, source_target_pairs={{0,12},{2,14},{4,0},{6,2},{8,4},{10,6},{12,8},{14,10},{1,13},{3,15... | collective-permute-start | bytes 393224 | tf_op jit(solution)/shard_map/ppermute | solution.py:304
  106.7 7.2 %collective-permute-start.28 = (bf16[32,2048]{1,0:T(8,128)(2,1)S(1)}, bf16[32,2048]{1,0:T(8,128)(2,1)S(1)}, u32[]{:S(2)}, u32[]{:S(2)}) collective-permute-start(bf16[32,2048]{1,0:T(8,128)(2,1)S(1)} %fusion.29), channel_id=1, source_target_pairs={{0,2},{2,0},{4,6},{6,4},{8,10},{10,8},{12,14},{14,12},{1,3},{3,1},... | collective-permute-start | bytes 393224 | tf_op jit(solution)/shard_map/ppermute | solution.py:298
  (4 other events, 36.1 us)

commit v5 on v4

--- a/solution.py
+++ b/solution.py
@@ -161,7 +161,9 @@
 def pieces_of(size, most):
     if size % LANES:
         return [(0, size)]
-    return [(at, min(most, size - at)) for at in range(0, size, most)]
+    short = size % most
+    pieces = [(0, short)] if short else []
+    return pieces + [(at, most) for at in range(short, size, most)]
 
 
 def expert_kernel(count, outs, mine_ref, *refs):

time: 115 us -> 114 us (level)
  no operation moved by 1% of the time
where the time goes in v5:
time: 114 us
  waiting for transfers between devices  40.7 us (36%)
  starting transfers between devices  28.2 us (25%)
  Pallas kernels  28.2 us (25%)
  local copies, waits for them, and re-layouts  13.3 us (12%)
  other arithmetic  1.8 us (2%)
    ppermute x9, waiting for transfers between devices, along(): return lax.ppermute(v, 'ep', pairs)  27.5 us
    pallas_call x2, Pallas kernels, expert(): pl.pallas_call(functools.partial(expert_kernel, len(slots), outs), in_spe...  16.1 us
    pallas_call x1, Pallas kernels, attend(): pl.pallas_call(attend_kernel, in_specs=[inside, inside, pl.BlockSpec(memo...  12.1 us
    ppermute x9, starting transfers between devices, along(): return lax.ppermute(v, 'ep', pairs)  12 us
    unnamed x13, local copies, waits for them, and re-layouts  11.4 us
    ppermute x9, waiting for transfers between devices, across(): return lax.ppermute(v, 'ep', [(i, i ^ 1) for i in range(owners)])  9.65 us
    all_to_all x1, starting transfers between devices, local(): fresh = lax.all_to_all(sent, 'ep', split_axis=0, concat_axis=0, tiled=True)  7.25 us
    ppermute x9, starting transfers between devices, across(): return lax.ppermute(v, 'ep', [(i, i ^ 1) for i in range(owners)])  6.77 us
  transfers between devices with their start and end apart: 30, of which 20 were waited for; matrix products, arithmetic and copies ran while one was open for 10% of the time, Pallas kernels for 25%

profile of v5, /device:TPU:0, one launch (start us, length us, event | category | flops | bytes accessed | tf_op | source)
XLA Modules:
  0.0 113.9 jit_solution(2971194209482118625)
XLA Ops:
  0.0 1.8 %copy.46 = bf16[3,4,8,8,256]{4,3,1,0,2:T(8,128)(2,1)} copy(bf16[3,4,8,8,256]{4,3,2,1,0:T(8,128)(2,1)} %bitcast.78) | data formatting | bytes 786432 | tf_op jit(solution)/shard_map/reshape | solution.py:317
  1.8 7.3 %all-to-all-start = ((bf16[8,3,32,256]{3,2,1,0:T(8,128)(2,1)}), bf16[8,3,32,256]{3,2,1,0:T(8,128)(2,1)S(1)}, u32[]{:S(2)}, u32[]{:S(2)}) async-start(bf16[8,3,32,256]{3,2,1,0:T(8,128)(2,1)} %bitcast.65), calls=%async_computation | async-start | bytes 786432 | tf_op jit(solution)/shard_map/all_to_all | solution.py:318
  9.1 11.3 %copy.45 = bf16[1,2048,2,1408]{3,1,2,0:T(8,128)(2,1)} copy(bf16[1,2048,2,1408]{3,2,1,0:T(2,128)(2,1)} %param.18) | data formatting | bytes 23068672 | tf_op args[7]
  20.8 1.8 %collective-permute-start = (bf16[128,2048]{1,0:T(8,128)(2,1)S(1)}, bf16[128,2048]{1,0:T(8,128)(2,1)S(1)}, u32[]{:S(2)}, u32[]{:S(2)}) collective-permute-start(bf16[128,2048]{1,0:T(8,128)(2,1)S(1)} %slice_select_fusion), channel_id=1, source_target_pairs={{0,2},{2,0},{4,6},{6,4},{8,10},{10,8},{12,14},{14,12},{1,3},{3,1},... | collective-permute-start | bytes 1572872 | tf_op jit(solution)/shard_map/ppermute | solution.py:300
  23.2 12.1 %shard_map.109 = bf16[256,256]{1,0:T(8,128)(2,1)S(1)} custom-call(bf16[8,3,32,256]{3,2,1,0:T(8,128)(2,1)S(1)} %all-to-all-done.fresh_ref, s32[8,32]{1,0:T(8,128)S(1)} %copy-done, bf16[2,256,128,256]{3,2,1,0:T(8,128)(2,1)} %bitcast.75), custom_call_target="tpu_custom_call" | custom-call | flops 33554432 | bytes 33554432 | tf_op jit(solution)/shard_map/pallas_call | solution.py:143
  35.8 4.2 %collective-permute-done.1 = bf16[4,32,256]{2,1,0:T(8,128)(2,1)S(1)} collective-permute-done((bf16[4,32,256]{2,1,0:T(8,128)(2,1)S(1)}, bf16[4,32,256]{2,1,0:T(8,128)(2,1)S(1)}, u32[]{:S(2)}, u32[]{:S(2)}) %collective-permute-start.1) | collective-permute-done | bytes 65568 | tf_op jit(solution)/shard_map/ppermute | solution.py:300
  40.2 0.7 fusion.37
  40.9 1.5 %collective-permute-start.3 = (bf16[32,2048]{1,0:T(8,128)(2,1)S(1)}, bf16[32,2048]{1,0:T(8,128)(2,1)S(1)}, u32[]{:S(2)}, u32[]{:S(2)}) collective-permute-start(bf16[32,2048]{1,0:T(8,128)(2,1)S(1)} %get-tuple-element.60), channel_id=1, source_target_pairs={{0,4},{2,6},{4,8},{6,10},{8,12},{10,14},{12,0},{14,2},{1,5},{3,7},... | collective-permute-start | bytes 393224 | tf_op jit(solution)/shard_map/ppermute | solution.py:306
  42.5 2.4 %collective-permute-start.5 = (bf16[32,2048]{1,0:T(8,128)(2,1)S(1)}, bf16[32,2048]{1,0:T(8,128)(2,1)S(1)}, u32[]{:S(2)}, u32[]{:S(2)}) collective-permute-start(bf16[32,2048]{1,0:T(8,128)(2,1)S(1)} %get-tuple-element.61), channel_id=1, source_target_pairs={{0,12},{2,14},{4,0},{6,2},{8,4},{10,6},{12,8},{14,10},{1,13},{3,15... | collective-permute-start | bytes 393224 | tf_op jit(solution)/shard_map/ppermute | solution.py:306
  44.8 0.6 collective-permute-start.4
  45.5 3.7 %collective-permute-done.3 = bf16[32,2048]{1,0:T(8,128)(2,1)S(1)} collective-permute-done((bf16[32,2048]{1,0:T(8,128)(2,1)S(1)}, bf16[32,2048]{1,0:T(8,128)(2,1)S(1)}, u32[]{:S(2)}, u32[]{:S(2)}) %collective-permute-start.3) | collective-permute-done | bytes 131104 | tf_op jit(solution)/shard_map/ppermute | solution.py:306
  49.2 0.9 collective-permute-done.5
  50.1 6.2 %collective-permute-done.4 = bf16[32,2048]{1,0:T(8,128)(2,1)S(1)} collective-permute-done((bf16[32,2048]{1,0:T(8,128)(2,1)S(1)}, bf16[32,2048]{1,0:T(8,128)(2,1)S(1)}, u32[]{:S(2)}, u32[]{:S(2)}) %collective-permute-start.4) | collective-permute-done | bytes 131104 | tf_op jit(solution)/shard_map/ppermute | solution.py:306
  56.7 1.5 %collective-permute-start.9 = (bf16[32,2176]{1,0:T(8,128)(2,1)S(1)}, bf16[32,2176]{1,0:T(8,128)(2,1)S(1)}, u32[]{:S(2)}, u32[]{:S(2)}) collective-permute-start(bf16[32,2176]{1,0:T(8,128)(2,1)S(1)} %fusion.25.refs_0_), channel_id=1, source_target_pairs={{0,12},{2,14},{4,0},{6,2},{8,4},{10,6},{12,8},{14,10},{1,13},{3,15... | collective-permute-start | bytes 417800 | tf_op jit(solution)/shard_map/ppermute | solution.py:306
  59.0 0.6 collective-permute-start.7
  59.6 4.8 %collective-permute-done.9.refs_3_ = bf16[32,2176]{1,0:T(8,128)(2,1)S(1)} collective-permute-done((bf16[32,2176]{1,0:T(8,128)(2,1)S(1)}, bf16[32,2176]{1,0:T(8,128)(2,1)S(1)}, u32[]{:S(2)}, u32[]{:S(2)}) %collective-permute-start.9) | collective-permute-done | bytes 139296 | tf_op jit(solution)/shard_map/ppermute | solution.py:306
  64.7 1.7 %collective-permute-done.6.refs_1_ = bf16[32,2176]{1,0:T(8,128)(2,1)S(1)} collective-permute-done((bf16[32,2176]{1,0:T(8,128)(2,1)S(1)}, bf16[32,2176]{1,0:T(8,128)(2,1)S(1)}, u32[]{:S(2)}, u32[]{:S(2)}) %collective-permute-start.6) | collective-permute-done | bytes 139296 | tf_op jit(solution)/shard_map/ppermute | solution.py:306
  66.9 3.7 %collective-permute-done.11.refs_2_ = bf16[32,2176]{1,0:T(8,128)(2,1)S(1)} collective-permute-done((bf16[32,2176]{1,0:T(8,128)(2,1)S(1)}, bf16[32,2176]{1,0:T(8,128)(2,1)S(1)}, u32[]{:S(2)}, u32[]{:S(2)}) %collective-permute-start.11) | collective-permute-done | bytes 139296 | tf_op jit(solution)/shard_map/ppermute | solution.py:306
  72.2 0.7 collective-permute-done.14.refs_6_
  72.9 8.1 %shard_map.110 = (bf16[128,2048]{1,0:T(8,128)(2,1)S(1)}, bf16[128,2048]{1,0:T(8,128)(2,1)S(1)}) custom-call(s32[1]{0:T(128)} %bitcast.11.mine_ref, bf16[32,2176]{1,0:T(8,128)(2,1)S(1)} %fusion.25.refs_0_, bf16[32,2176]{1,0:T(8,128)(2,1)S(1)} %collective-permute-done.6.refs_1_, bf16[32,2176]{1,0:T(8,128)(2,1)S(1)} %collective-permute-done.11.refs_2_, ...), custom_call_target="tpu_custom_call" | custom-call | flops 4429185024 | bytes 19398656 | tf_op jit(solution)/shard_map/pallas_call | solution.py:246
  83.1 8.1 %shard_map.111 = (bf16[128,2048]{1,0:T(8,128)(2,1)S(1)}, bf16[128,2048]{1,0:T(8,128)(2,1)S(1)}) custom-call(s32[1]{0:T(128)} %bitcast.11.mine_ref, bf16[32,2176]{1,0:T(8,128)(2,1)S(1)} %collective-permute-done.7.refs_0_, bf16[32,2176]{1,0:T(8,128)(2,1)S(1)} %collective-permute-done.8.refs_1_, bf16[32,2176]{1,0:T(8,128)(2,1)S(1)} %collective-permute-done.16.refs_2_, ...), custom_call_target="tpu_custom_call" | custom-call | flops 4429185024 | bytes 19398656 | tf_op jit(solution)/shard_map/pallas_call | solution.py:246
  91.7 1.4 %collective-permute-done.22 = bf16[4,32,2048]{2,1,0:T(8,128)(2,1)S(1)} collective-permute-done((bf16[4,32,2048]{2,1,0:T(8,128)(2,1)S(1)}, bf16[4,32,2048]{2,1,0:T(8,128)(2,1)S(1)}, u32[]{:S(2)}, u32[]{:S(2)}) %collective-permute-start.22) | collective-permute-done | bytes 524320 | tf_op jit(solution)/shard_map/ppermute | solution.py:309
  93.3 0.8 collective-permute-start.24
  94.1 1.3 %collective-permute-start.26 = (bf16[32,2048]{1,0:T(8,128)(2,1)S(1)}, bf16[32,2048]{1,0:T(8,128)(2,1)S(1)}, u32[]{:S(2)}, u32[]{:S(2)}) collective-permute-start(bf16[32,2048]{1,0:T(8,128)(2,1)S(1)} %get-tuple-element.58), channel_id=1, source_target_pairs={{0,2},{2,0},{4,6},{6,4},{8,10},{10,8},{12,14},{14,12},{1,3},{3,1},... | collective-permute-start | bytes 393224 | tf_op jit(solution)/shard_map/ppermute | solution.py:300
  95.4 1.4 %collective-permute-start.23 = (bf16[2,32,2048]{2,1,0:T(8,128)(2,1)S(1)}, bf16[2,32,2048]{2,1,0:T(8,128)(2,1)S(1)}, u32[]{:S(2)}, u32[]{:S(2)}) collective-permute-start(bf16[2,32,2048]{2,1,0:T(8,128)(2,1)S(1)} %pad_maximum_fusion), channel_id=1, source_target_pairs={{0,4},{2,6},{4,8},{6,10},{8,12},{10,14},{12,0},{14,2},{1,5},{3,7},... | collective-permute-start | bytes 786440 | tf_op jit(solution)/shard_map/ppermute | solution.py:306
  96.8 2.9 %collective-permute-done.24 = bf16[32,2048]{1,0:T(8,128)(2,1)S(1)} collective-permute-done((bf16[32,2048]{1,0:T(8,128)(2,1)S(1)}, bf16[32,2048]{1,0:T(8,128)(2,1)S(1)}, u32[]{:S(2)}, u32[]{:S(2)}) %collective-permute-start.24) | collective-permute-done | bytes 131104 | tf_op jit(solution)/shard_map/ppermute | solution.py:300
  99.7 2.2 %collective-permute-done.26 = bf16[32,2048]{1,0:T(8,128)(2,1)S(1)} collective-permute-done((bf16[32,2048]{1,0:T(8,128)(2,1)S(1)}, bf16[32,2048]{1,0:T(8,128)(2,1)S(1)}, u32[]{:S(2)}, u32[]{:S(2)}) %collective-permute-start.26) | collective-permute-done | bytes 131104 | tf_op jit(solution)/shard_map/ppermute | solution.py:300
  102.0 3.9 %collective-permute-start.25 = (bf16[32,2048]{1,0:T(8,128)(2,1)S(1)}, bf16[32,2048]{1,0:T(8,128)(2,1)S(1)}, u32[]{:S(2)}, u32[]{:S(2)}) collective-permute-start(bf16[32,2048]{1,0:T(8,128)(2,1)S(1)} %get-tuple-element.51), channel_id=1, source_target_pairs={{0,8},{2,10},{4,12},{6,14},{8,0},{10,2},{12,4},{14,6},{1,9},{3,11}... | collective-permute-start | bytes 393224 | tf_op jit(solution)/shard_map/ppermute | solution.py:306
  105.9 0.8 collective-permute-start.28
  106.7 4.8 %collective-permute-done.25 = bf16[32,2048]{1,0:T(8,128)(2,1)S(1)} collective-permute-done((bf16[32,2048]{1,0:T(8,128)(2,1)S(1)}, bf16[32,2048]{1,0:T(8,128)(2,1)S(1)}, u32[]{:S(2)}, u32[]{:S(2)}) %collective-permute-start.25) | collective-permute-done | bytes 131104 | tf_op jit(solution)/shard_map/ppermute | solution.py:306
  111.6 1.6 %collective-permute-done.27 = bf16[32,2048]{1,0:T(8,128)(2,1)S(1)} collective-permute-done((bf16[32,2048]{1,0:T(8,128)(2,1)S(1)}, bf16[32,2048]{1,0:T(8,128)(2,1)S(1)}, u32[]{:S(2)}, u32[]{:S(2)}) %collective-permute-start.27) | collective-permute-done | bytes 131104 | tf_op jit(solution)/shard_map/ppermute | solution.py:306
  113.1 0.8 fusion.11
  (69 shorter events, 7.6 us)
Async XLA Ops:
  1.8 18.9 %all-to-all-start = ((bf16[8,3,32,256]{3,2,1,0:T(8,128)(2,1)}), bf16[8,3,32,256]{3,2,1,0:T(8,128)(2,1)S(1)}, u32[]{:S(2)}, u32[]{:S(2)}) async-start(bf16[8,3,32,256]{3,2,1,0:T(8,128)(2,1)} %bitcast.65), calls=%async_computation | async-start | bytes 786432 | tf_op jit(solution)/shard_map/all_to_all | solution.py:318
  20.8 14.6 %collective-permute-start = (bf16[128,2048]{1,0:T(8,128)(2,1)S(1)}, bf16[128,2048]{1,0:T(8,128)(2,1)S(1)}, u32[]{:S(2)}, u32[]{:S(2)}) collective-permute-start(bf16[128,2048]{1,0:T(8,128)(2,1)S(1)} %slice_select_fusion), channel_id=1, source_target_pairs={{0,2},{2,0},{4,6},{6,4},{8,10},{10,8},{12,14},{14,12},{1,3},{3,1},... | collective-permute-start | bytes 1572872 | tf_op jit(solution)/shard_map/ppermute | solution.py:300
  35.3 4.8 %collective-permute-start.2 = (bf16[128,2048]{1,0:T(8,128)(2,1)S(1)}, bf16[128,2048]{1,0:T(8,128)(2,1)S(1)}, u32[]{:S(2)}, u32[]{:S(2)}) collective-permute-start(bf16[128,2048]{1,0:T(8,128)(2,1)S(1)} %collective-permute-done), channel_id=1, source_target_pairs={{0,1},{1,0},{2,3},{3,2},{4,5},{5,4},{6,7},{7,6},{8,9},{9,8},{10,11... | collective-permute-start | bytes 1572872 | tf_op jit(solution)/shard_map/ppermute | solution.py:309
  35.4 4.6 %collective-permute-start.1 = (bf16[4,32,256]{2,1,0:T(8,128)(2,1)S(1)}, bf16[4,32,256]{2,1,0:T(8,128)(2,1)S(1)}, u32[]{:S(2)}, u32[]{:S(2)}) collective-permute-start(bf16[4,32,256]{2,1,0:T(8,128)(2,1)S(1)} %fusion.30), channel_id=1, source_target_pairs={{0,2},{2,0},{4,6},{6,4},{8,10},{10,8},{12,14},{14,12},{1,3},{3,1},... | collective-permute-start | bytes 196616 | tf_op jit(solution)/shard_map/ppermute | solution.py:300
  40.1 16.2 %copy-start.2 = (bf16[32,2048]{1,0:T(8,128)(2,1)S(1)}, bf16[32,2048]{1,0:T(8,128)(2,1)}, u32[]{:S(2)}) copy-start(bf16[32,2048]{1,0:T(8,128)(2,1)} %param.11) | copy-start | bytes 393220
  40.2 16.3 %copy-start.3 = (f32[2048]{0:T(1024)S(1)}, f32[2048]{0:T(1024)}, u32[]{:S(2)}) copy-start(f32[2048]{0:T(1024)} %param.17) | copy-start | bytes 24580
  40.9 8.3 %collective-permute-start.3 = (bf16[32,2048]{1,0:T(8,128)(2,1)S(1)}, bf16[32,2048]{1,0:T(8,128)(2,1)S(1)}, u32[]{:S(2)}, u32[]{:S(2)}) collective-permute-start(bf16[32,2048]{1,0:T(8,128)(2,1)S(1)} %get-tuple-element.60), channel_id=1, source_target_pairs={{0,4},{2,6},{4,8},{6,10},{8,12},{10,14},{12,0},{14,2},{1,5},{3,7},... | collective-permute-start | bytes 393224 | tf_op jit(solution)/shard_map/ppermute | solution.py:306
  42.5 7.6 %collective-permute-start.5 = (bf16[32,2048]{1,0:T(8,128)(2,1)S(1)}, bf16[32,2048]{1,0:T(8,128)(2,1)S(1)}, u32[]{:S(2)}, u32[]{:S(2)}) collective-permute-start(bf16[32,2048]{1,0:T(8,128)(2,1)S(1)} %get-tuple-element.61), channel_id=1, source_target_pairs={{0,12},{2,14},{4,0},{6,2},{8,4},{10,6},{12,8},{14,10},{1,13},{3,15... | collective-permute-start | bytes 393224 | tf_op jit(solution)/shard_map/ppermute | solution.py:306
  44.8 11.5 %collective-permute-start.4 = (bf16[32,2048]{1,0:T(8,128)(2,1)S(1)}, bf16[32,2048]{1,0:T(8,128)(2,1)S(1)}, u32[]{:S(2)}, u32[]{:S(2)}) collective-permute-start(bf16[32,2048]{1,0:T(8,128)(2,1)S(1)} %get-tuple-element.62), channel_id=1, source_target_pairs={{0,8},{2,10},{4,12},{6,14},{8,0},{10,2},{12,4},{14,6},{1,9},{3,11}... | collective-permute-start | bytes 393224 | tf_op jit(solution)/shard_map/ppermute | solution.py:306
  56.7 7.7 %collective-permute-start.9 = (bf16[32,2176]{1,0:T(8,128)(2,1)S(1)}, bf16[32,2176]{1,0:T(8,128)(2,1)S(1)}, u32[]{:S(2)}, u32[]{:S(2)}) collective-permute-start(bf16[32,2176]{1,0:T(8,128)(2,1)S(1)} %fusion.25.refs_0_), channel_id=1, source_target_pairs={{0,12},{2,14},{4,0},{6,2},{8,4},{10,6},{12,8},{14,10},{1,13},{3,15... | collective-permute-start | bytes 417800 | tf_op jit(solution)/shard_map/ppermute | solution.py:306
  58.2 8.3 %collective-permute-start.6 = (bf16[32,2176]{1,0:T(8,128)(2,1)S(1)}, bf16[32,2176]{1,0:T(8,128)(2,1)S(1)}, u32[]{:S(2)}, u32[]{:S(2)}) collective-permute-start(bf16[32,2176]{1,0:T(8,128)(2,1)S(1)} %fusion.25.refs_0_), channel_id=1, source_target_pairs={{0,4},{2,6},{4,8},{6,10},{8,12},{10,14},{12,0},{14,2},{1,5},{3,7},... | collective-permute-start | bytes 417800 | tf_op jit(solution)/shard_map/ppermute | solution.py:306
  58.8 11.9 %collective-permute-start.11 = (bf16[32,2176]{1,0:T(8,128)(2,1)S(1)}, bf16[32,2176]{1,0:T(8,128)(2,1)S(1)}, u32[]{:S(2)}, u32[]{:S(2)}) collective-permute-start(bf16[32,2176]{1,0:T(8,128)(2,1)S(1)} %fusion.25.refs_0_), channel_id=1, source_target_pairs={{0,8},{2,10},{4,12},{6,14},{8,0},{10,2},{12,4},{14,6},{1,9},{3,11}... | collective-permute-start | bytes 417800 | tf_op jit(solution)/shard_map/ppermute | solution.py:306
  59.0 11.6 %collective-permute-start.7 = (bf16[32,2176]{1,0:T(8,128)(2,1)S(1)}, bf16[32,2176]{1,0:T(8,128)(2,1)S(1)}, u32[]{:S(2)}, u32[]{:S(2)}) collective-permute-start(bf16[32,2176]{1,0:T(8,128)(2,1)S(1)} %fusion.25.refs_0_), channel_id=1, source_target_pairs={{0,2},{2,0},{4,6},{6,4},{8,10},{10,8},{12,14},{14,12},{1,3},{3,1},... | collective-permute-start | bytes 417800 | tf_op jit(solution)/shard_map/ppermute | solution.py:300
  64.4 6.8 %collective-permute-start.10 = (bf16[32,2176]{1,0:T(8,128)(2,1)S(1)}, bf16[32,2176]{1,0:T(8,128)(2,1)S(1)}, u32[]{:S(2)}, u32[]{:S(2)}) collective-permute-start(bf16[32,2176]{1,0:T(8,128)(2,1)S(1)} %collective-permute-done.9.refs_3_), channel_id=1, source_target_pairs={{0,2},{2,0},{4,6},{6,4},{8,10},{10,8},{12,14},{14,12},{1,3},{3,1},... | collective-permute-start | bytes 417800 | tf_op jit(solution)/shard_map/ppermute | solution.py:300
  66.4 5.1 %collective-permute-start.8 = (bf16[32,2176]{1,0:T(8,128)(2,1)S(1)}, bf16[32,2176]{1,0:T(8,128)(2,1)S(1)}, u32[]{:S(2)}, u32[]{:S(2)}) collective-permute-start(bf16[32,2176]{1,0:T(8,128)(2,1)S(1)} %collective-permute-done.6.refs_1_), channel_id=1, source_target_pairs={{0,2},{2,0},{4,6},{6,4},{8,10},{10,8},{12,14},{14,12},{1,3},{3,1},... | collective-permute-start | bytes 417800 | tf_op jit(solution)/shard_map/ppermute | solution.py:300
  66.9 5.1 %collective-permute-start.12 = (bf16[32,2176]{1,0:T(8,128)(2,1)S(1)}, bf16[32,2176]{1,0:T(8,128)(2,1)S(1)}, u32[]{:S(2)}, u32[]{:S(2)}) collective-permute-start(bf16[32,2176]{1,0:T(8,128)(2,1)S(1)} %fusion.25.refs_0_), channel_id=1, source_target_pairs={{0,1},{1,0},{2,3},{3,2},{4,5},{5,4},{6,7},{7,6},{8,9},{9,8},{10,11... | collective-permute-start | bytes 417800 | tf_op jit(solution)/shard_map/ppermute | solution.py:309
  70.6 1.4 %collective-permute-start.15 = (bf16[32,2176]{1,0:T(8,128)(2,1)S(1)}, bf16[32,2176]{1,0:T(8,128)(2,1)S(1)}, u32[]{:S(2)}, u32[]{:S(2)}) collective-permute-start(bf16[32,2176]{1,0:T(8,128)(2,1)S(1)} %collective-permute-done.9.refs_3_), channel_id=1, source_target_pairs={{0,1},{1,0},{2,3},{3,2},{4,5},{5,4},{6,7},{7,6},{8,9},{9,8},{10,11... | collective-permute-start | bytes 417800 | tf_op jit(solution)/shard_map/ppermute | solution.py:309
  70.6 1.6 %collective-permute-start.13 = (bf16[32,2176]{1,0:T(8,128)(2,1)S(1)}, bf16[32,2176]{1,0:T(8,128)(2,1)S(1)}, u32[]{:S(2)}, u32[]{:S(2)}) collective-permute-start(bf16[32,2176]{1,0:T(8,128)(2,1)S(1)} %collective-permute-done.6.refs_1_), channel_id=1, source_target_pairs={{0,1},{1,0},{2,3},{3,2},{4,5},{5,4},{6,7},{7,6},{8,9},{9,8},{10,11... | collective-permute-start | bytes 417800 | tf_op jit(solution)/shard_map/ppermute | solution.py:309
  71.5 1.4 %collective-permute-start.14 = (bf16[32,2176]{1,0:T(8,128)(2,1)S(1)}, bf16[32,2176]{1,0:T(8,128)(2,1)S(1)}, u32[]{:S(2)}, u32[]{:S(2)}) collective-permute-start(bf16[32,2176]{1,0:T(8,128)(2,1)S(1)} %collective-permute-done.11.refs_2_), channel_id=1, source_target_pairs={{0,1},{1,0},{2,3},{3,2},{4,5},{5,4},{6,7},{7,6},{8,9},{9,8},{10,11... | collective-permute-start | bytes 417800 | tf_op jit(solution)/shard_map/ppermute | solution.py:309
  71.5 9.4 %collective-permute-start.16 = (bf16[32,2176]{1,0:T(8,128)(2,1)S(1)}, bf16[32,2176]{1,0:T(8,128)(2,1)S(1)}, u32[]{:S(2)}, u32[]{:S(2)}) collective-permute-start(bf16[32,2176]{1,0:T(8,128)(2,1)S(1)} %collective-permute-done.11.refs_2_), channel_id=1, source_target_pairs={{0,2},{2,0},{4,6},{6,4},{8,10},{10,8},{12,14},{14,12},{1,3},{3,1},... | collective-permute-start | bytes 417800 | tf_op jit(solution)/shard_map/ppermute | solution.py:300
  80.9 1.4 %collective-permute-start.17 = (bf16[32,2176]{1,0:T(8,128)(2,1)S(1)}, bf16[32,2176]{1,0:T(8,128)(2,1)S(1)}, u32[]{:S(2)}, u32[]{:S(2)}) collective-permute-start(bf16[32,2176]{1,0:T(8,128)(2,1)S(1)} %collective-permute-done.7.refs_0_), channel_id=1, source_target_pairs={{0,1},{1,0},{2,3},{3,2},{4,5},{5,4},{6,7},{7,6},{8,9},{9,8},{10,11... | collective-permute-start | bytes 417800 | tf_op jit(solution)/shard_map/ppermute | solution.py:309
  81.2 1.4 %collective-permute-start.18 = (bf16[32,2176]{1,0:T(8,128)(2,1)S(1)}, bf16[32,2176]{1,0:T(8,128)(2,1)S(1)}, u32[]{:S(2)}, u32[]{:S(2)}) collective-permute-start(bf16[32,2176]{1,0:T(8,128)(2,1)S(1)} %collective-permute-done.8.refs_1_), channel_id=1, source_target_pairs={{0,1},{1,0},{2,3},{3,2},{4,5},{5,4},{6,7},{7,6},{8,9},{9,8},{10,11... | collective-permute-start | bytes 417800 | tf_op jit(solution)/shard_map/ppermute | solution.py:309
  81.5 1.4 %collective-permute-start.19 = (bf16[32,2176]{1,0:T(8,128)(2,1)S(1)}, bf16[32,2176]{1,0:T(8,128)(2,1)S(1)}, u32[]{:S(2)}, u32[]{:S(2)}) collective-permute-start(bf16[32,2176]{1,0:T(8,128)(2,1)S(1)} %collective-permute-done.16.refs_2_), channel_id=1, source_target_pairs={{0,1},{1,0},{2,3},{3,2},{4,5},{5,4},{6,7},{7,6},{8,9},{9,8},{10,11... | collective-permute-start | bytes 417800 | tf_op jit(solution)/shard_map/ppermute | solution.py:309
  81.7 1.4 %collective-permute-start.20 = (bf16[32,2176]{1,0:T(8,128)(2,1)S(1)}, bf16[32,2176]{1,0:T(8,128)(2,1)S(1)}, u32[]{:S(2)}, u32[]{:S(2)}) collective-permute-start(bf16[32,2176]{1,0:T(8,128)(2,1)S(1)} %collective-permute-done.10.refs_3_), channel_id=1, source_target_pairs={{0,1},{1,0},{2,3},{3,2},{4,5},{5,4},{6,7},{7,6},{8,9},{9,8},{10,11... | collective-permute-start | bytes 417800 | tf_op jit(solution)/shard_map/ppermute | solution.py:309
  82.0 9.1 %collective-permute-start.21 = (bf16[4,32,2048]{2,1,0:T(8,128)(2,1)S(1)}, bf16[4,32,2048]{2,1,0:T(8,128)(2,1)S(1)}, u32[]{:S(2)}, u32[]{:S(2)}) collective-permute-start(bf16[4,32,2048]{2,1,0:T(8,128)(2,1)S(1)} %bitcast.71), channel_id=1, source_target_pairs={{0,1},{1,0},{2,3},{3,2},{4,5},{5,4},{6,7},{7,6},{8,9},{9,8},{10,11... | collective-permute-start | bytes 1572872 | tf_op jit(solution)/shard_map/ppermute | solution.py:309
  91.2 2.0 %collective-permute-start.22 = (bf16[4,32,2048]{2,1,0:T(8,128)(2,1)S(1)}, bf16[4,32,2048]{2,1,0:T(8,128)(2,1)S(1)}, u32[]{:S(2)}, u32[]{:S(2)}) collective-permute-start(bf16[4,32,2048]{2,1,0:T(8,128)(2,1)S(1)} %bitcast.72), channel_id=1, source_target_pairs={{0,1},{1,0},{2,3},{3,2},{4,5},{5,4},{6,7},{7,6},{8,9},{9,8},{10,11... | collective-permute-start | bytes 1572872 | tf_op jit(solution)/shard_map/ppermute | solution.py:309
  93.3 6.4 %collective-permute-start.24 = (bf16[32,2048]{1,0:T(8,128)(2,1)S(1)}, bf16[32,2048]{1,0:T(8,128)(2,1)S(1)}, u32[]{:S(2)}, u32[]{:S(2)}) collective-permute-start(bf16[32,2048]{1,0:T(8,128)(2,1)S(1)} %get-tuple-element.57), channel_id=1, source_target_pairs={{0,2},{2,0},{4,6},{6,4},{8,10},{10,8},{12,14},{14,12},{1,3},{3,1},... | collective-permute-start | bytes 393224 | tf_op jit(solution)/shard_map/ppermute | solution.py:300
  94.1 7.8 %collective-permute-start.26 = (bf16[32,2048]{1,0:T(8,128)(2,1)S(1)}, bf16[32,2048]{1,0:T(8,128)(2,1)S(1)}, u32[]{:S(2)}, u32[]{:S(2)}) collective-permute-start(bf16[32,2048]{1,0:T(8,128)(2,1)S(1)} %get-tuple-element.58), channel_id=1, source_target_pairs={{0,2},{2,0},{4,6},{6,4},{8,10},{10,8},{12,14},{14,12},{1,3},{3,1},... | collective-permute-start | bytes 393224 | tf_op jit(solution)/shard_map/ppermute | solution.py:300
  95.4 10.4 %collective-permute-start.23 = (bf16[2,32,2048]{2,1,0:T(8,128)(2,1)S(1)}, bf16[2,32,2048]{2,1,0:T(8,128)(2,1)S(1)}, u32[]{:S(2)}, u32[]{:S(2)}) collective-permute-start(bf16[2,32,2048]{2,1,0:T(8,128)(2,1)S(1)} %pad_maximum_fusion), channel_id=1, source_target_pairs={{0,4},{2,6},{4,8},{6,10},{8,12},{10,14},{12,0},{14,2},{1,5},{3,7},... | collective-permute-start | bytes 786440 | tf_op jit(solution)/shard_map/ppermute | solution.py:306
  102.0 9.6 %collective-permute-start.25 = (bf16[32,2048]{1,0:T(8,128)(2,1)S(1)}, bf16[32,2048]{1,0:T(8,128)(2,1)S(1)}, u32[]{:S(2)}, u32[]{:S(2)}) collective-permute-start(bf16[32,2048]{1,0:T(8,128)(2,1)S(1)} %get-tuple-element.51), channel_id=1, source_target_pairs={{0,8},{2,10},{4,12},{6,14},{8,0},{10,2},{12,4},{14,6},{1,9},{3,11}... | collective-permute-start | bytes 393224 | tf_op jit(solution)/shard_map/ppermute | solution.py:306
  105.8 7.3 %collective-permute-start.27 = (bf16[32,2048]{1,0:T(8,128)(2,1)S(1)}, bf16[32,2048]{1,0:T(8,128)(2,1)S(1)}, u32[]{:S(2)}, u32[]{:S(2)}) collective-permute-start(bf16[32,2048]{1,0:T(8,128)(2,1)S(1)} %get-tuple-element.52), channel_id=1, source_target_pairs={{0,12},{2,14},{4,0},{6,2},{8,4},{10,6},{12,8},{14,10},{1,13},{3,15... | collective-permute-start | bytes 393224 | tf_op jit(solution)/shard_map/ppermute | solution.py:306
  105.9 7.2 %collective-permute-start.28 = (bf16[32,2048]{1,0:T(8,128)(2,1)S(1)}, bf16[32,2048]{1,0:T(8,128)(2,1)S(1)}, u32[]{:S(2)}, u32[]{:S(2)}) collective-permute-start(bf16[32,2048]{1,0:T(8,128)(2,1)S(1)} %fusion.29), channel_id=1, source_target_pairs={{0,2},{2,0},{4,6},{6,4},{8,10},{10,8},{12,14},{14,12},{1,3},{3,1},... | collective-permute-start | bytes 393224 | tf_op jit(solution)/shard_map/ppermute | solution.py:300
  (4 other events, 36.1 us)

commit v6 on v5

--- a/solution.py
+++ b/solution.py
@@ -361,6 +361,7 @@
     partial_out = jnp.dot(
         turned.reshape(outer * tok_rows, -1), w_pair, preferred_element_type=wide
     ).reshape(outer, tok_rows, feat_local)
+    partial_out, row_counts = fence(partial_out, row_counts)
     arrived = [along(partial_out[k].astype(narrow), k) for k in range(1, outer)]
     attn_out = partial_out[0]
     for part in arrived:

time: 114 us -> 114 us (level)
  waiting for transfers between devices: 40.7 us -> 37.6 us
  starting transfers between devices: 28.2 us -> 31.2 us
    ppermute x9, starting transfers between devices: 6.77 us -> 9.81 us  [across(): return lax.ppermute(v, 'ep', [(i, i ^ 1) for i in range(owners)])]
    ppermute x9, waiting for transfers between devices: 27.5 us -> 25.7 us  [along(): return lax.ppermute(v, 'ep', pairs)]
where the time goes in v6:
time: 114 us
  waiting for transfers between devices  37.6 us (33%)
  starting transfers between devices  31.2 us (27%)
  Pallas kernels  28.2 us (25%)
  local copies, waits for them, and re-layouts  13.3 us (12%)
  other arithmetic  1.76 us (2%)
    ppermute x9, waiting for transfers between devices, along(): return lax.ppermute(v, 'ep', pairs)  25.7 us
    pallas_call x2, Pallas kernels, expert(): pl.pallas_call(functools.partial(expert_kernel, len(slots), outs), in_spe...  16.1 us
    pallas_call x1, Pallas kernels, attend(): pl.pallas_call(attend_kernel, in_specs=[inside, inside, pl.BlockSpec(memo...  12.1 us
    ppermute x9, starting transfers between devices, along(): return lax.ppermute(v, 'ep', pairs)  12 us
    unnamed x13, local copies, waits for them, and re-layouts  11.4 us
    ppermute x9, starting transfers between devices, across(): return lax.ppermute(v, 'ep', [(i, i ^ 1) for i in range(owners)])  9.81 us
    ppermute x9, waiting for transfers between devices, across(): return lax.ppermute(v, 'ep', [(i, i ^ 1) for i in range(owners)])  8.72 us
    all_to_all x1, starting transfers between devices, local(): fresh = lax.all_to_all(sent, 'ep', split_axis=0, concat_axis=0, tiled=True)  7.25 us
  transfers between devices with their start and end apart: 30, of which 20 were waited for; matrix products, arithmetic and copies ran while one was open for 10% of the time, Pallas kernels for 25%

profile of v6, /device:TPU:0, one launch (start us, length us, event | category | flops | bytes accessed | tf_op | source)
XLA Modules:
  0.0 113.6 jit_solution(9234988624240729440)
XLA Ops:
  0.0 1.8 %copy.39 = bf16[3,4,8,8,256]{4,3,1,0,2:T(8,128)(2,1)} copy(bf16[3,4,8,8,256]{4,3,2,1,0:T(8,128)(2,1)} %bitcast.95) | data formatting | bytes 786432 | tf_op jit(solution)/shard_map/reshape | solution.py:317
  1.8 7.3 %all-to-all-start = ((bf16[8,3,32,256]{3,2,1,0:T(8,128)(2,1)}), bf16[8,3,32,256]{3,2,1,0:T(8,128)(2,1)S(1)}, u32[]{:S(2)}, u32[]{:S(2)}) async-start(bf16[8,3,32,256]{3,2,1,0:T(8,128)(2,1)} %bitcast.83), calls=%async_computation | async-start | bytes 786432 | tf_op jit(solution)/shard_map/all_to_all | solution.py:318
  9.1 11.3 %copy.38 = bf16[1,2048,2,1408]{3,1,2,0:T(8,128)(2,1)} copy(bf16[1,2048,2,1408]{3,2,1,0:T(2,128)(2,1)} %param.18) | data formatting | bytes 23068672 | tf_op args[7]
  20.8 1.8 %collective-permute-start = (bf16[128,2048]{1,0:T(8,128)(2,1)S(1)}, bf16[128,2048]{1,0:T(8,128)(2,1)S(1)}, u32[]{:S(2)}, u32[]{:S(2)}) collective-permute-start(bf16[128,2048]{1,0:T(8,128)(2,1)S(1)} %slice_select_fusion), channel_id=1, source_target_pairs={{0,2},{2,0},{4,6},{6,4},{8,10},{10,8},{12,14},{14,12},{1,3},{3,1},... | collective-permute-start | bytes 1572872 | tf_op jit(solution)/shard_map/ppermute | solution.py:300
  22.6 12.1 %shard_map.109 = bf16[256,256]{1,0:T(8,128)(2,1)S(1)} custom-call(bf16[8,3,32,256]{3,2,1,0:T(8,128)(2,1)S(1)} %all-to-all-done.fresh_ref, s32[8,32]{1,0:T(8,128)S(1)} %copy-done, bf16[2,256,128,256]{3,2,1,0:T(8,128)(2,1)} %bitcast.92), custom_call_target="tpu_custom_call" | custom-call | flops 33554432 | bytes 33554432 | tf_op jit(solution)/shard_map/pallas_call | solution.py:143
  35.4 1.0 collective-permute-start.1
  36.7 3.3 %collective-permute-done.1 = bf16[4,32,256]{2,1,0:T(8,128)(2,1)S(1)} collective-permute-done((bf16[4,32,256]{2,1,0:T(8,128)(2,1)S(1)}, bf16[4,32,256]{2,1,0:T(8,128)(2,1)S(1)}, u32[]{:S(2)}, u32[]{:S(2)}) %collective-permute-start.1) | collective-permute-done | bytes 65568 | tf_op jit(solution)/shard_map/ppermute | solution.py:300
  40.6 1.5 %collective-permute-start.3 = (bf16[32,2048]{1,0:T(8,128)(2,1)S(1)}, bf16[32,2048]{1,0:T(8,128)(2,1)S(1)}, u32[]{:S(2)}, u32[]{:S(2)}) collective-permute-start(bf16[32,2048]{1,0:T(8,128)(2,1)S(1)} %get-tuple-element.64), channel_id=1, source_target_pairs={{0,4},{2,6},{4,8},{6,10},{8,12},{10,14},{12,0},{14,2},{1,5},{3,7},... | collective-permute-start | bytes 393224 | tf_op jit(solution)/shard_map/ppermute | solution.py:306
  42.2 2.4 %collective-permute-start.5 = (bf16[32,2048]{1,0:T(8,128)(2,1)S(1)}, bf16[32,2048]{1,0:T(8,128)(2,1)S(1)}, u32[]{:S(2)}, u32[]{:S(2)}) collective-permute-start(bf16[32,2048]{1,0:T(8,128)(2,1)S(1)} %get-tuple-element.65), channel_id=1, source_target_pairs={{0,12},{2,14},{4,0},{6,2},{8,4},{10,6},{12,8},{14,10},{1,13},{3,15... | collective-permute-start | bytes 393224 | tf_op jit(solution)/shard_map/ppermute | solution.py:306
  45.2 3.7 %collective-permute-done.3 = bf16[32,2048]{1,0:T(8,128)(2,1)S(1)} collective-permute-done((bf16[32,2048]{1,0:T(8,128)(2,1)S(1)}, bf16[32,2048]{1,0:T(8,128)(2,1)S(1)}, u32[]{:S(2)}, u32[]{:S(2)}) %collective-permute-start.3) | collective-permute-done | bytes 131104 | tf_op jit(solution)/shard_map/ppermute | solution.py:306
  48.9 0.9 collective-permute-done.5
  49.8 6.2 %collective-permute-done.4 = bf16[32,2048]{1,0:T(8,128)(2,1)S(1)} collective-permute-done((bf16[32,2048]{1,0:T(8,128)(2,1)S(1)}, bf16[32,2048]{1,0:T(8,128)(2,1)S(1)}, u32[]{:S(2)}, u32[]{:S(2)}) %collective-permute-start.4) | collective-permute-done | bytes 131104 | tf_op jit(solution)/shard_map/ppermute | solution.py:306
  56.4 1.5 %collective-permute-start.9 = (bf16[32,2176]{1,0:T(8,128)(2,1)S(1)}, bf16[32,2176]{1,0:T(8,128)(2,1)S(1)}, u32[]{:S(2)}, u32[]{:S(2)}) collective-permute-start(bf16[32,2176]{1,0:T(8,128)(2,1)S(1)} %fusion.24.refs_0_), channel_id=1, source_target_pairs={{0,12},{2,14},{4,0},{6,2},{8,4},{10,6},{12,8},{14,10},{1,13},{3,15... | collective-permute-start | bytes 417800 | tf_op jit(solution)/shard_map/ppermute | solution.py:306
  58.7 1.0 collective-permute-start.7
  59.7 4.4 %collective-permute-done.9.refs_3_ = bf16[32,2176]{1,0:T(8,128)(2,1)S(1)} collective-permute-done((bf16[32,2176]{1,0:T(8,128)(2,1)S(1)}, bf16[32,2176]{1,0:T(8,128)(2,1)S(1)}, u32[]{:S(2)}, u32[]{:S(2)}) %collective-permute-start.9) | collective-permute-done | bytes 139296 | tf_op jit(solution)/shard_map/ppermute | solution.py:306
  64.1 1.0 collective-permute-start.10
  65.1 1.1 collective-permute-done.6.refs_1_
  66.1 1.0 collective-permute-start.8
  67.1 3.2 %collective-permute-done.11.refs_2_ = bf16[32,2176]{1,0:T(8,128)(2,1)S(1)} collective-permute-done((bf16[32,2176]{1,0:T(8,128)(2,1)S(1)}, bf16[32,2176]{1,0:T(8,128)(2,1)S(1)}, u32[]{:S(2)}, u32[]{:S(2)}) %collective-permute-start.11) | collective-permute-done | bytes 139296 | tf_op jit(solution)/shard_map/ppermute | solution.py:306
  71.2 1.0 collective-permute-start.16
  72.6 8.1 %shard_map.110 = (bf16[128,2048]{1,0:T(8,128)(2,1)S(1)}, bf16[128,2048]{1,0:T(8,128)(2,1)S(1)}) custom-call(s32[1]{0:T(128)} %bitcast.12.mine_ref, bf16[32,2176]{1,0:T(8,128)(2,1)S(1)} %fusion.24.refs_0_, bf16[32,2176]{1,0:T(8,128)(2,1)S(1)} %collective-permute-done.6.refs_1_, bf16[32,2176]{1,0:T(8,128)(2,1)S(1)} %collective-permute-done.11.refs_2_, ...), custom_call_target="tpu_custom_call" | custom-call | flops 4429185024 | bytes 19398656 | tf_op jit(solution)/shard_map/pallas_call | solution.py:246
  82.8 8.1 %shard_map.111 = (bf16[128,2048]{1,0:T(8,128)(2,1)S(1)}, bf16[128,2048]{1,0:T(8,128)(2,1)S(1)}) custom-call(s32[1]{0:T(128)} %bitcast.12.mine_ref, bf16[32,2176]{1,0:T(8,128)(2,1)S(1)} %collective-permute-done.7.refs_0_, bf16[32,2176]{1,0:T(8,128)(2,1)S(1)} %collective-permute-done.8.refs_1_, bf16[32,2176]{1,0:T(8,128)(2,1)S(1)} %collective-permute-done.16.refs_2_, ...), custom_call_target="tpu_custom_call" | custom-call | flops 4429185024 | bytes 19398656 | tf_op jit(solution)/shard_map/pallas_call | solution.py:246
  91.4 1.4 %collective-permute-done.22 = bf16[4,32,2048]{2,1,0:T(8,128)(2,1)S(1)} collective-permute-done((bf16[4,32,2048]{2,1,0:T(8,128)(2,1)S(1)}, bf16[4,32,2048]{2,1,0:T(8,128)(2,1)S(1)}, u32[]{:S(2)}, u32[]{:S(2)}) %collective-permute-start.22) | collective-permute-done | bytes 524320 | tf_op jit(solution)/shard_map/ppermute | solution.py:309
  93.0 1.0 collective-permute-start.24
  94.1 1.1 collective-permute-start.26
  95.1 1.4 %collective-permute-start.23 = (bf16[2,32,2048]{2,1,0:T(8,128)(2,1)S(1)}, bf16[2,32,2048]{2,1,0:T(8,128)(2,1)S(1)}, u32[]{:S(2)}, u32[]{:S(2)}) collective-permute-start(bf16[2,32,2048]{2,1,0:T(8,128)(2,1)S(1)} %pad_maximum_fusion), channel_id=1, source_target_pairs={{0,4},{2,6},{4,8},{6,10},{8,12},{10,14},{12,0},{14,2},{1,5},{3,7},... | collective-permute-start | bytes 786440 | tf_op jit(solution)/shard_map/ppermute | solution.py:306
  96.5 2.9 %collective-permute-done.24 = bf16[32,2048]{1,0:T(8,128)(2,1)S(1)} collective-permute-done((bf16[32,2048]{1,0:T(8,128)(2,1)S(1)}, bf16[32,2048]{1,0:T(8,128)(2,1)S(1)}, u32[]{:S(2)}, u32[]{:S(2)}) %collective-permute-start.24) | collective-permute-done | bytes 131104 | tf_op jit(solution)/shard_map/ppermute | solution.py:300
  99.4 2.2 %collective-permute-done.26 = bf16[32,2048]{1,0:T(8,128)(2,1)S(1)} collective-permute-done((bf16[32,2048]{1,0:T(8,128)(2,1)S(1)}, bf16[32,2048]{1,0:T(8,128)(2,1)S(1)}, u32[]{:S(2)}, u32[]{:S(2)}) %collective-permute-start.26) | collective-permute-done | bytes 131104 | tf_op jit(solution)/shard_map/ppermute | solution.py:300
  101.7 3.9 %collective-permute-start.25 = (bf16[32,2048]{1,0:T(8,128)(2,1)S(1)}, bf16[32,2048]{1,0:T(8,128)(2,1)S(1)}, u32[]{:S(2)}, u32[]{:S(2)}) collective-permute-start(bf16[32,2048]{1,0:T(8,128)(2,1)S(1)} %get-tuple-element.55), channel_id=1, source_target_pairs={{0,8},{2,10},{4,12},{6,14},{8,0},{10,2},{12,4},{14,6},{1,9},{3,11}... | collective-permute-start | bytes 393224 | tf_op jit(solution)/shard_map/ppermute | solution.py:306
  105.6 1.0 collective-permute-start.28
  106.7 4.6 %collective-permute-done.25 = bf16[32,2048]{1,0:T(8,128)(2,1)S(1)} collective-permute-done((bf16[32,2048]{1,0:T(8,128)(2,1)S(1)}, bf16[32,2048]{1,0:T(8,128)(2,1)S(1)}, u32[]{:S(2)}, u32[]{:S(2)}) %collective-permute-start.25) | collective-permute-done | bytes 131104 | tf_op jit(solution)/shard_map/ppermute | solution.py:306
  111.2 1.6 %collective-permute-done.27 = bf16[32,2048]{1,0:T(8,128)(2,1)S(1)} collective-permute-done((bf16[32,2048]{1,0:T(8,128)(2,1)S(1)}, bf16[32,2048]{1,0:T(8,128)(2,1)S(1)}, u32[]{:S(2)}, u32[]{:S(2)}) %collective-permute-start.27) | collective-permute-done | bytes 131104 | tf_op jit(solution)/shard_map/ppermute | solution.py:306
  (68 shorter events, 8.2 us)
Async XLA Ops:
  1.8 18.9 %all-to-all-start = ((bf16[8,3,32,256]{3,2,1,0:T(8,128)(2,1)}), bf16[8,3,32,256]{3,2,1,0:T(8,128)(2,1)S(1)}, u32[]{:S(2)}, u32[]{:S(2)}) async-start(bf16[8,3,32,256]{3,2,1,0:T(8,128)(2,1)} %bitcast.83), calls=%async_computation | async-start | bytes 786432 | tf_op jit(solution)/shard_map/all_to_all | solution.py:318
  20.8 13.9 %collective-permute-start = (bf16[128,2048]{1,0:T(8,128)(2,1)S(1)}, bf16[128,2048]{1,0:T(8,128)(2,1)S(1)}, u32[]{:S(2)}, u32[]{:S(2)}) collective-permute-start(bf16[128,2048]{1,0:T(8,128)(2,1)S(1)} %slice_select_fusion), channel_id=1, source_target_pairs={{0,2},{2,0},{4,6},{6,4},{8,10},{10,8},{12,14},{14,12},{1,3},{3,1},... | collective-permute-start | bytes 1572872 | tf_op jit(solution)/shard_map/ppermute | solution.py:300
  34.7 2.0 %collective-permute-start.2 = (bf16[128,2048]{1,0:T(8,128)(2,1)S(1)}, bf16[128,2048]{1,0:T(8,128)(2,1)S(1)}, u32[]{:S(2)}, u32[]{:S(2)}) collective-permute-start(bf16[128,2048]{1,0:T(8,128)(2,1)S(1)} %collective-permute-done), channel_id=1, source_target_pairs={{0,1},{1,0},{2,3},{3,2},{4,5},{5,4},{6,7},{7,6},{8,9},{9,8},{10,11... | collective-permute-start | bytes 1572872 | tf_op jit(solution)/shard_map/ppermute | solution.py:309
  35.4 4.5 %collective-permute-start.1 = (bf16[4,32,256]{2,1,0:T(8,128)(2,1)S(1)}, bf16[4,32,256]{2,1,0:T(8,128)(2,1)S(1)}, u32[]{:S(2)}, u32[]{:S(2)}) collective-permute-start(bf16[4,32,256]{2,1,0:T(8,128)(2,1)S(1)} %get-tuple-element.67), channel_id=1, source_target_pairs={{0,2},{2,0},{4,6},{6,4},{8,10},{10,8},{12,14},{14,12},{1,3},{3,1},... | collective-permute-start | bytes 196616 | tf_op jit(solution)/shard_map/ppermute | solution.py:300
  40.0 16.1 %copy-start.2 = (bf16[32,2048]{1,0:T(8,128)(2,1)S(1)}, bf16[32,2048]{1,0:T(8,128)(2,1)}, u32[]{:S(2)}) copy-start(bf16[32,2048]{1,0:T(8,128)(2,1)} %param.11) | copy-start | bytes 393220
  40.0 16.3 %copy-start.3 = (f32[2048]{0:T(1024)S(1)}, f32[2048]{0:T(1024)}, u32[]{:S(2)}) copy-start(f32[2048]{0:T(1024)} %param.17) | copy-start | bytes 24580
  40.6 8.3 %collective-permute-start.3 = (bf16[32,2048]{1,0:T(8,128)(2,1)S(1)}, bf16[32,2048]{1,0:T(8,128)(2,1)S(1)}, u32[]{:S(2)}, u32[]{:S(2)}) collective-permute-start(bf16[32,2048]{1,0:T(8,128)(2,1)S(1)} %get-tuple-element.64), channel_id=1, source_target_pairs={{0,4},{2,6},{4,8},{6,10},{8,12},{10,14},{12,0},{14,2},{1,5},{3,7},... | collective-permute-start | bytes 393224 | tf_op jit(solution)/shard_map/ppermute | solution.py:306
  42.2 7.6 %collective-permute-start.5 = (bf16[32,2048]{1,0:T(8,128)(2,1)S(1)}, bf16[32,2048]{1,0:T(8,128)(2,1)S(1)}, u32[]{:S(2)}, u32[]{:S(2)}) collective-permute-start(bf16[32,2048]{1,0:T(8,128)(2,1)S(1)} %get-tuple-element.65), channel_id=1, source_target_pairs={{0,12},{2,14},{4,0},{6,2},{8,4},{10,6},{12,8},{14,10},{1,13},{3,15... | collective-permute-start | bytes 393224 | tf_op jit(solution)/shard_map/ppermute | solution.py:306
  44.5 11.5 %collective-permute-start.4 = (bf16[32,2048]{1,0:T(8,128)(2,1)S(1)}, bf16[32,2048]{1,0:T(8,128)(2,1)S(1)}, u32[]{:S(2)}, u32[]{:S(2)}) collective-permute-start(bf16[32,2048]{1,0:T(8,128)(2,1)S(1)} %get-tuple-element.66), channel_id=1, source_target_pairs={{0,8},{2,10},{4,12},{6,14},{8,0},{10,2},{12,4},{14,6},{1,9},{3,11}... | collective-permute-start | bytes 393224 | tf_op jit(solution)/shard_map/ppermute | solution.py:306
  56.4 7.7 %collective-permute-start.9 = (bf16[32,2176]{1,0:T(8,128)(2,1)S(1)}, bf16[32,2176]{1,0:T(8,128)(2,1)S(1)}, u32[]{:S(2)}, u32[]{:S(2)}) collective-permute-start(bf16[32,2176]{1,0:T(8,128)(2,1)S(1)} %fusion.24.refs_0_), channel_id=1, source_target_pairs={{0,12},{2,14},{4,0},{6,2},{8,4},{10,6},{12,8},{14,10},{1,13},{3,15... | collective-permute-start | bytes 417800 | tf_op jit(solution)/shard_map/ppermute | solution.py:306
  57.9 8.3 %collective-permute-start.6 = (bf16[32,2176]{1,0:T(8,128)(2,1)S(1)}, bf16[32,2176]{1,0:T(8,128)(2,1)S(1)}, u32[]{:S(2)}, u32[]{:S(2)}) collective-permute-start(bf16[32,2176]{1,0:T(8,128)(2,1)S(1)} %fusion.24.refs_0_), channel_id=1, source_target_pairs={{0,4},{2,6},{4,8},{6,10},{8,12},{10,14},{12,0},{14,2},{1,5},{3,7},... | collective-permute-start | bytes 417800 | tf_op jit(solution)/shard_map/ppermute | solution.py:306
  58.5 11.9 %collective-permute-start.11 = (bf16[32,2176]{1,0:T(8,128)(2,1)S(1)}, bf16[32,2176]{1,0:T(8,128)(2,1)S(1)}, u32[]{:S(2)}, u32[]{:S(2)}) collective-permute-start(bf16[32,2176]{1,0:T(8,128)(2,1)S(1)} %fusion.24.refs_0_), channel_id=1, source_target_pairs={{0,8},{2,10},{4,12},{6,14},{8,0},{10,2},{12,4},{14,6},{1,9},{3,11}... | collective-permute-start | bytes 417800 | tf_op jit(solution)/shard_map/ppermute | solution.py:306
  58.7 11.7 %collective-permute-start.7 = (bf16[32,2176]{1,0:T(8,128)(2,1)S(1)}, bf16[32,2176]{1,0:T(8,128)(2,1)S(1)}, u32[]{:S(2)}, u32[]{:S(2)}) collective-permute-start(bf16[32,2176]{1,0:T(8,128)(2,1)S(1)} %fusion.24.refs_0_), channel_id=1, source_target_pairs={{0,2},{2,0},{4,6},{6,4},{8,10},{10,8},{12,14},{14,12},{1,3},{3,1},... | collective-permute-start | bytes 417800 | tf_op jit(solution)/shard_map/ppermute | solution.py:300
  64.1 6.7 %collective-permute-start.10 = (bf16[32,2176]{1,0:T(8,128)(2,1)S(1)}, bf16[32,2176]{1,0:T(8,128)(2,1)S(1)}, u32[]{:S(2)}, u32[]{:S(2)}) collective-permute-start(bf16[32,2176]{1,0:T(8,128)(2,1)S(1)} %collective-permute-done.9.refs_3_), channel_id=1, source_target_pairs={{0,2},{2,0},{4,6},{6,4},{8,10},{10,8},{12,14},{14,12},{1,3},{3,1},... | collective-permute-start | bytes 417800 | tf_op jit(solution)/shard_map/ppermute | solution.py:300
  66.1 5.1 %collective-permute-start.8 = (bf16[32,2176]{1,0:T(8,128)(2,1)S(1)}, bf16[32,2176]{1,0:T(8,128)(2,1)S(1)}, u32[]{:S(2)}, u32[]{:S(2)}) collective-permute-start(bf16[32,2176]{1,0:T(8,128)(2,1)S(1)} %collective-permute-done.6.refs_1_), channel_id=1, source_target_pairs={{0,2},{2,0},{4,6},{6,4},{8,10},{10,8},{12,14},{14,12},{1,3},{3,1},... | collective-permute-start | bytes 417800 | tf_op jit(solution)/shard_map/ppermute | solution.py:300
  67.1 5.1 %collective-permute-start.12 = (bf16[32,2176]{1,0:T(8,128)(2,1)S(1)}, bf16[32,2176]{1,0:T(8,128)(2,1)S(1)}, u32[]{:S(2)}, u32[]{:S(2)}) collective-permute-start(bf16[32,2176]{1,0:T(8,128)(2,1)S(1)} %fusion.24.refs_0_), channel_id=1, source_target_pairs={{0,1},{1,0},{2,3},{3,2},{4,5},{5,4},{6,7},{7,6},{8,9},{9,8},{10,11... | collective-permute-start | bytes 417800 | tf_op jit(solution)/shard_map/ppermute | solution.py:309
  70.3 1.9 %collective-permute-start.15 = (bf16[32,2176]{1,0:T(8,128)(2,1)S(1)}, bf16[32,2176]{1,0:T(8,128)(2,1)S(1)}, u32[]{:S(2)}, u32[]{:S(2)}) collective-permute-start(bf16[32,2176]{1,0:T(8,128)(2,1)S(1)} %collective-permute-done.9.refs_3_), channel_id=1, source_target_pairs={{0,1},{1,0},{2,3},{3,2},{4,5},{5,4},{6,7},{7,6},{8,9},{9,8},{10,11... | collective-permute-start | bytes 417800 | tf_op jit(solution)/shard_map/ppermute | solution.py:309
  70.3 1.9 %collective-permute-start.13 = (bf16[32,2176]{1,0:T(8,128)(2,1)S(1)}, bf16[32,2176]{1,0:T(8,128)(2,1)S(1)}, u32[]{:S(2)}, u32[]{:S(2)}) collective-permute-start(bf16[32,2176]{1,0:T(8,128)(2,1)S(1)} %collective-permute-done.6.refs_1_), channel_id=1, source_target_pairs={{0,1},{1,0},{2,3},{3,2},{4,5},{5,4},{6,7},{7,6},{8,9},{9,8},{10,11... | collective-permute-start | bytes 417800 | tf_op jit(solution)/shard_map/ppermute | solution.py:309
  71.2 1.4 %collective-permute-start.14 = (bf16[32,2176]{1,0:T(8,128)(2,1)S(1)}, bf16[32,2176]{1,0:T(8,128)(2,1)S(1)}, u32[]{:S(2)}, u32[]{:S(2)}) collective-permute-start(bf16[32,2176]{1,0:T(8,128)(2,1)S(1)} %collective-permute-done.11.refs_2_), channel_id=1, source_target_pairs={{0,1},{1,0},{2,3},{3,2},{4,5},{5,4},{6,7},{7,6},{8,9},{9,8},{10,11... | collective-permute-start | bytes 417800 | tf_op jit(solution)/shard_map/ppermute | solution.py:309
  71.2 9.4 %collective-permute-start.16 = (bf16[32,2176]{1,0:T(8,128)(2,1)S(1)}, bf16[32,2176]{1,0:T(8,128)(2,1)S(1)}, u32[]{:S(2)}, u32[]{:S(2)}) collective-permute-start(bf16[32,2176]{1,0:T(8,128)(2,1)S(1)} %collective-permute-done.11.refs_2_), channel_id=1, source_target_pairs={{0,2},{2,0},{4,6},{6,4},{8,10},{10,8},{12,14},{14,12},{1,3},{3,1},... | collective-permute-start | bytes 417800 | tf_op jit(solution)/shard_map/ppermute | solution.py:300
  80.6 1.4 %collective-permute-start.17 = (bf16[32,2176]{1,0:T(8,128)(2,1)S(1)}, bf16[32,2176]{1,0:T(8,128)(2,1)S(1)}, u32[]{:S(2)}, u32[]{:S(2)}) collective-permute-start(bf16[32,2176]{1,0:T(8,128)(2,1)S(1)} %collective-permute-done.7.refs_0_), channel_id=1, source_target_pairs={{0,1},{1,0},{2,3},{3,2},{4,5},{5,4},{6,7},{7,6},{8,9},{9,8},{10,11... | collective-permute-start | bytes 417800 | tf_op jit(solution)/shard_map/ppermute | solution.py:309
  80.9 1.4 %collective-permute-start.18 = (bf16[32,2176]{1,0:T(8,128)(2,1)S(1)}, bf16[32,2176]{1,0:T(8,128)(2,1)S(1)}, u32[]{:S(2)}, u32[]{:S(2)}) collective-permute-start(bf16[32,2176]{1,0:T(8,128)(2,1)S(1)} %collective-permute-done.8.refs_1_), channel_id=1, source_target_pairs={{0,1},{1,0},{2,3},{3,2},{4,5},{5,4},{6,7},{7,6},{8,9},{9,8},{10,11... | collective-permute-start | bytes 417800 | tf_op jit(solution)/shard_map/ppermute | solution.py:309
  81.2 1.4 %collective-permute-start.19 = (bf16[32,2176]{1,0:T(8,128)(2,1)S(1)}, bf16[32,2176]{1,0:T(8,128)(2,1)S(1)}, u32[]{:S(2)}, u32[]{:S(2)}) collective-permute-start(bf16[32,2176]{1,0:T(8,128)(2,1)S(1)} %collective-permute-done.16.refs_2_), channel_id=1, source_target_pairs={{0,1},{1,0},{2,3},{3,2},{4,5},{5,4},{6,7},{7,6},{8,9},{9,8},{10,11... | collective-permute-start | bytes 417800 | tf_op jit(solution)/shard_map/ppermute | solution.py:309
  81.4 1.4 %collective-permute-start.20 = (bf16[32,2176]{1,0:T(8,128)(2,1)S(1)}, bf16[32,2176]{1,0:T(8,128)(2,1)S(1)}, u32[]{:S(2)}, u32[]{:S(2)}) collective-permute-start(bf16[32,2176]{1,0:T(8,128)(2,1)S(1)} %collective-permute-done.10.refs_3_), channel_id=1, source_target_pairs={{0,1},{1,0},{2,3},{3,2},{4,5},{5,4},{6,7},{7,6},{8,9},{9,8},{10,11... | collective-permute-start | bytes 417800 | tf_op jit(solution)/shard_map/ppermute | solution.py:309
  81.7 9.1 %collective-permute-start.21 = (bf16[4,32,2048]{2,1,0:T(8,128)(2,1)S(1)}, bf16[4,32,2048]{2,1,0:T(8,128)(2,1)S(1)}, u32[]{:S(2)}, u32[]{:S(2)}) collective-permute-start(bf16[4,32,2048]{2,1,0:T(8,128)(2,1)S(1)} %bitcast.88), channel_id=1, source_target_pairs={{0,1},{1,0},{2,3},{3,2},{4,5},{5,4},{6,7},{7,6},{8,9},{9,8},{10,11... | collective-permute-start | bytes 1572872 | tf_op jit(solution)/shard_map/ppermute | solution.py:309
  90.9 2.0 %collective-permute-start.22 = (bf16[4,32,2048]{2,1,0:T(8,128)(2,1)S(1)}, bf16[4,32,2048]{2,1,0:T(8,128)(2,1)S(1)}, u32[]{:S(2)}, u32[]{:S(2)}) collective-permute-start(bf16[4,32,2048]{2,1,0:T(8,128)(2,1)S(1)} %bitcast.89), channel_id=1, source_target_pairs={{0,1},{1,0},{2,3},{3,2},{4,5},{5,4},{6,7},{7,6},{8,9},{9,8},{10,11... | collective-permute-start | bytes 1572872 | tf_op jit(solution)/shard_map/ppermute | solution.py:309
  93.0 6.4 %collective-permute-start.24 = (bf16[32,2048]{1,0:T(8,128)(2,1)S(1)}, bf16[32,2048]{1,0:T(8,128)(2,1)S(1)}, u32[]{:S(2)}, u32[]{:S(2)}) collective-permute-start(bf16[32,2048]{1,0:T(8,128)(2,1)S(1)} %get-tuple-element.61), channel_id=1, source_target_pairs={{0,2},{2,0},{4,6},{6,4},{8,10},{10,8},{12,14},{14,12},{1,3},{3,1},... | collective-permute-start | bytes 393224 | tf_op jit(solution)/shard_map/ppermute | solution.py:300
  94.1 7.5 %collective-permute-start.26 = (bf16[32,2048]{1,0:T(8,128)(2,1)S(1)}, bf16[32,2048]{1,0:T(8,128)(2,1)S(1)}, u32[]{:S(2)}, u32[]{:S(2)}) collective-permute-start(bf16[32,2048]{1,0:T(8,128)(2,1)S(1)} %get-tuple-element.62), channel_id=1, source_target_pairs={{0,2},{2,0},{4,6},{6,4},{8,10},{10,8},{12,14},{14,12},{1,3},{3,1},... | collective-permute-start | bytes 393224 | tf_op jit(solution)/shard_map/ppermute | solution.py:300
  95.1 10.4 %collective-permute-start.23 = (bf16[2,32,2048]{2,1,0:T(8,128)(2,1)S(1)}, bf16[2,32,2048]{2,1,0:T(8,128)(2,1)S(1)}, u32[]{:S(2)}, u32[]{:S(2)}) collective-permute-start(bf16[2,32,2048]{2,1,0:T(8,128)(2,1)S(1)} %pad_maximum_fusion), channel_id=1, source_target_pairs={{0,4},{2,6},{4,8},{6,10},{8,12},{10,14},{12,0},{14,2},{1,5},{3,7},... | collective-permute-start | bytes 786440 | tf_op jit(solution)/shard_map/ppermute | solution.py:306
  101.7 9.6 %collective-permute-start.25 = (bf16[32,2048]{1,0:T(8,128)(2,1)S(1)}, bf16[32,2048]{1,0:T(8,128)(2,1)S(1)}, u32[]{:S(2)}, u32[]{:S(2)}) collective-permute-start(bf16[32,2048]{1,0:T(8,128)(2,1)S(1)} %get-tuple-element.55), channel_id=1, source_target_pairs={{0,8},{2,10},{4,12},{6,14},{8,0},{10,2},{12,4},{14,6},{1,9},{3,11}... | collective-permute-start | bytes 393224 | tf_op jit(solution)/shard_map/ppermute | solution.py:306
  105.5 7.3 %collective-permute-start.27 = (bf16[32,2048]{1,0:T(8,128)(2,1)S(1)}, bf16[32,2048]{1,0:T(8,128)(2,1)S(1)}, u32[]{:S(2)}, u32[]{:S(2)}) collective-permute-start(bf16[32,2048]{1,0:T(8,128)(2,1)S(1)} %get-tuple-element.56), channel_id=1, source_target_pairs={{0,12},{2,14},{4,0},{6,2},{8,4},{10,6},{12,8},{14,10},{1,13},{3,15... | collective-permute-start | bytes 393224 | tf_op jit(solution)/shard_map/ppermute | solution.py:306
  105.6 7.2 %collective-permute-start.28 = (bf16[32,2048]{1,0:T(8,128)(2,1)S(1)}, bf16[32,2048]{1,0:T(8,128)(2,1)S(1)}, u32[]{:S(2)}, u32[]{:S(2)}) collective-permute-start(bf16[32,2048]{1,0:T(8,128)(2,1)S(1)} %fusion.30), channel_id=1, source_target_pairs={{0,2},{2,0},{4,6},{6,4},{8,10},{10,8},{12,14},{14,12},{1,3},{3,1},... | collective-permute-start | bytes 393224 | tf_op jit(solution)/shard_map/ppermute | solution.py:300
  (4 other events, 35.1 us)

commit v7 on v6

--- a/solution.py
+++ b/solution.py
@@ -392,9 +392,9 @@
             far.insert(middle, across(near[middle]))
     first_expert = (me * reps + lax.axis_index("rep")) * experts_local
 
-    def run_experts(slots):
+    def run_experts(slots, swapped=None):
         if reps == 2:
-            slots = slots + [other(s) for s in slots]
+            slots = slots + (swapped or [other(s) for s in slots])
         total = None
         for j in range(experts_local):
             mine = jnp.reshape(first_expert + j, (1,)).astype(jnp.int32)
@@ -419,9 +419,12 @@
 
     made = run_experts(near)
     if inner == 2:
-        made, far = fence(made, far)
+        ready = [k for k in range(outer) if k != outer // 2] if reps == 2 else []
+        here = {k: other(far[k]) for k in ready}
+        made, far, here = fence(made, far, here)
+        swapped_far = [here[k] if k in here else other(v) for k, v in enumerate(far)]
         swapped = [other(v) for v in made[1:]]
-        far_made = run_experts(far)
+        far_made = run_experts(far, swapped_far if reps == 2 else None)
         far_made, swapped = fence(far_made, swapped)
         far_sum = summed(far_made[0].astype(wide), [other(v) for v in far_made[1:]])
         near_sum = summed(made[0].astype(wide), swapped)

time: 114 us -> 114 us (level)
  transfers between devices with their start and end apart: 30 -> 30, of which waited for: 20 -> 16; matrix products, arithmetic and copies ran while one was open for 10% -> 11% of each run, Pallas kernels for 25% -> 25%
where the time goes in v7:
time: 114 us; the launch traced here: 113 us
  waiting for transfers between devices  37.1 us (33%)
  starting transfers between devices  31.4 us (28%)
  Pallas kernels  28.2 us (25%)
  local copies, waits for them, and re-layouts  13.3 us (12%)
  other arithmetic  1.75 us (2%)
    ppermute x9, waiting for transfers between devices, along(): return lax.ppermute(v, 'ep', pairs)  25.6 us
    pallas_call x2, Pallas kernels, expert(): pl.pallas_call(functools.partial(expert_kernel, len(slots), outs), in_spe...  16.1 us
    pallas_call x1, Pallas kernels, attend(): pl.pallas_call(attend_kernel, in_specs=[inside, inside, pl.BlockSpec(memo...  12.1 us
    ppermute x9, starting transfers between devices, along(): return lax.ppermute(v, 'ep', pairs)  12 us
    unnamed x13, local copies, waits for them, and re-layouts  11.4 us
    ppermute x9, starting transfers between devices, across(): return lax.ppermute(v, 'ep', [(i, i ^ 1) for i in range(owners)])  9.88 us
    ppermute x9, waiting for transfers between devices, across(): return lax.ppermute(v, 'ep', [(i, i ^ 1) for i in range(owners)])  8.69 us
    all_to_all x1, starting transfers between devices, local(): fresh = lax.all_to_all(sent, 'ep', split_axis=0, concat_axis=0, tiled=True)  7.25 us
  transfers between devices with their start and end apart: 30, of which 16 were waited for; matrix products, arithmetic and copies ran while one was open for 11% of the time, Pallas kernels for 25%

profile of v7, /device:TPU:0, one launch (start us, length us, event | category | flops | bytes accessed | tf_op | source)
XLA Modules:
  0.0 113.2 jit_solution(7531383073907147277)
XLA Ops:
  0.0 1.8 %copy.39 = bf16[3,4,8,8,256]{4,3,1,0,2:T(8,128)(2,1)} copy(bf16[3,4,8,8,256]{4,3,2,1,0:T(8,128)(2,1)} %bitcast.95) | data formatting | bytes 786432 | tf_op jit(solution)/shard_map/reshape | solution.py:317
  1.8 7.3 %all-to-all-start = ((bf16[8,3,32,256]{3,2,1,0:T(8,128)(2,1)}), bf16[8,3,32,256]{3,2,1,0:T(8,128)(2,1)S(1)}, u32[]{:S(2)}, u32[]{:S(2)}) async-start(bf16[8,3,32,256]{3,2,1,0:T(8,128)(2,1)} %bitcast.83), calls=%async_computation | async-start | bytes 786432 | tf_op jit(solution)/shard_map/all_to_all | solution.py:318
  9.1 11.3 %copy.38 = bf16[1,2048,2,1408]{3,1,2,0:T(8,128)(2,1)} copy(bf16[1,2048,2,1408]{3,2,1,0:T(2,128)(2,1)} %param.18) | data formatting | bytes 23068672 | tf_op args[7]
  20.8 1.8 %collective-permute-start = (bf16[128,2048]{1,0:T(8,128)(2,1)S(1)}, bf16[128,2048]{1,0:T(8,128)(2,1)S(1)}, u32[]{:S(2)}, u32[]{:S(2)}) collective-permute-start(bf16[128,2048]{1,0:T(8,128)(2,1)S(1)} %slice_select_fusion), channel_id=1, source_target_pairs={{0,2},{2,0},{4,6},{6,4},{8,10},{10,8},{12,14},{14,12},{1,3},{3,1},... | collective-permute-start | bytes 1572872 | tf_op jit(solution)/shard_map/ppermute | solution.py:300
  22.6 12.1 %shard_map.109 = bf16[256,256]{1,0:T(8,128)(2,1)S(1)} custom-call(bf16[8,3,32,256]{3,2,1,0:T(8,128)(2,1)S(1)} %all-to-all-done.fresh_ref, s32[8,32]{1,0:T(8,128)S(1)} %copy-done, bf16[2,256,128,256]{3,2,1,0:T(8,128)(2,1)} %bitcast.92), custom_call_target="tpu_custom_call" | custom-call | flops 33554432 | bytes 33554432 | tf_op jit(solution)/shard_map/pallas_call | solution.py:143
  35.4 1.0 collective-permute-start.1
  36.7 3.3 %collective-permute-done.1 = bf16[4,32,256]{2,1,0:T(8,128)(2,1)S(1)} collective-permute-done((bf16[4,32,256]{2,1,0:T(8,128)(2,1)S(1)}, bf16[4,32,256]{2,1,0:T(8,128)(2,1)S(1)}, u32[]{:S(2)}, u32[]{:S(2)}) %collective-permute-start.1) | collective-permute-done | bytes 65568 | tf_op jit(solution)/shard_map/ppermute | solution.py:300
  40.6 1.5 %collective-permute-start.3 = (bf16[32,2048]{1,0:T(8,128)(2,1)S(1)}, bf16[32,2048]{1,0:T(8,128)(2,1)S(1)}, u32[]{:S(2)}, u32[]{:S(2)}) collective-permute-start(bf16[32,2048]{1,0:T(8,128)(2,1)S(1)} %get-tuple-element.70), channel_id=1, source_target_pairs={{0,4},{2,6},{4,8},{6,10},{8,12},{10,14},{12,0},{14,2},{1,5},{3,7},... | collective-permute-start | bytes 393224 | tf_op jit(solution)/shard_map/ppermute | solution.py:306
  42.2 2.4 %collective-permute-start.5 = (bf16[32,2048]{1,0:T(8,128)(2,1)S(1)}, bf16[32,2048]{1,0:T(8,128)(2,1)S(1)}, u32[]{:S(2)}, u32[]{:S(2)}) collective-permute-start(bf16[32,2048]{1,0:T(8,128)(2,1)S(1)} %get-tuple-element.71), channel_id=1, source_target_pairs={{0,12},{2,14},{4,0},{6,2},{8,4},{10,6},{12,8},{14,10},{1,13},{3,15... | collective-permute-start | bytes 393224 | tf_op jit(solution)/shard_map/ppermute | solution.py:306
  45.2 3.7 %collective-permute-done.3 = bf16[32,2048]{1,0:T(8,128)(2,1)S(1)} collective-permute-done((bf16[32,2048]{1,0:T(8,128)(2,1)S(1)}, bf16[32,2048]{1,0:T(8,128)(2,1)S(1)}, u32[]{:S(2)}, u32[]{:S(2)}) %collective-permute-start.3) | collective-permute-done | bytes 131104 | tf_op jit(solution)/shard_map/ppermute | solution.py:306
  48.9 0.9 collective-permute-done.5
  49.8 6.2 %collective-permute-done.4 = bf16[32,2048]{1,0:T(8,128)(2,1)S(1)} collective-permute-done((bf16[32,2048]{1,0:T(8,128)(2,1)S(1)}, bf16[32,2048]{1,0:T(8,128)(2,1)S(1)}, u32[]{:S(2)}, u32[]{:S(2)}) %collective-permute-start.4) | collective-permute-done | bytes 131104 | tf_op jit(solution)/shard_map/ppermute | solution.py:306
  56.4 1.5 %collective-permute-start.9 = (bf16[32,2176]{1,0:T(8,128)(2,1)S(1)}, bf16[32,2176]{1,0:T(8,128)(2,1)S(1)}, u32[]{:S(2)}, u32[]{:S(2)}) collective-permute-start(bf16[32,2176]{1,0:T(8,128)(2,1)S(1)} %fusion.24.refs_0_), channel_id=1, source_target_pairs={{0,12},{2,14},{4,0},{6,2},{8,4},{10,6},{12,8},{14,10},{1,13},{3,15... | collective-permute-start | bytes 417800 | tf_op jit(solution)/shard_map/ppermute | solution.py:306
  58.7 1.0 collective-permute-start.7
  59.7 4.4 %collective-permute-done.9.refs_3_ = bf16[32,2176]{1,0:T(8,128)(2,1)S(1)} collective-permute-done((bf16[32,2176]{1,0:T(8,128)(2,1)S(1)}, bf16[32,2176]{1,0:T(8,128)(2,1)S(1)}, u32[]{:S(2)}, u32[]{:S(2)}) %collective-permute-start.9) | collective-permute-done | bytes 139296 | tf_op jit(solution)/shard_map/ppermute | solution.py:306
  64.1 1.0 collective-permute-start.10
  65.1 1.1 collective-permute-done.6.refs_1_
  66.1 1.0 collective-permute-start.8
  67.1 3.2 %collective-permute-done.11.refs_2_ = bf16[32,2176]{1,0:T(8,128)(2,1)S(1)} collective-permute-done((bf16[32,2176]{1,0:T(8,128)(2,1)S(1)}, bf16[32,2176]{1,0:T(8,128)(2,1)S(1)}, u32[]{:S(2)}, u32[]{:S(2)}) %collective-permute-start.11) | collective-permute-done | bytes 139296 | tf_op jit(solution)/shard_map/ppermute | solution.py:306
  71.2 1.0 collective-permute-start.16
  72.9 8.1 %shard_map.110 = (bf16[128,2048]{1,0:T(8,128)(2,1)S(1)}, bf16[128,2048]{1,0:T(8,128)(2,1)S(1)}) custom-call(s32[1]{0:T(128)} %bitcast.12.mine_ref, bf16[32,2176]{1,0:T(8,128)(2,1)S(1)} %fusion.24.refs_0_, bf16[32,2176]{1,0:T(8,128)(2,1)S(1)} %collective-permute-done.6.refs_1_, bf16[32,2176]{1,0:T(8,128)(2,1)S(1)} %collective-permute-done.11.refs_2_, ...), custom_call_target="tpu_custom_call" | custom-call | flops 4429185024 | bytes 19398656 | tf_op jit(solution)/shard_map/pallas_call | solution.py:246
  82.5 8.1 %shard_map.111 = (bf16[128,2048]{1,0:T(8,128)(2,1)S(1)}, bf16[128,2048]{1,0:T(8,128)(2,1)S(1)}) custom-call(s32[1]{0:T(128)} %bitcast.12.mine_ref, bf16[32,2176]{1,0:T(8,128)(2,1)S(1)} %collective-permute-done.7.refs_0_, bf16[32,2176]{1,0:T(8,128)(2,1)S(1)} %collective-permute-done.8.refs_1_, bf16[32,2176]{1,0:T(8,128)(2,1)S(1)} %collective-permute-done.16.refs_2_, ...), custom_call_target="tpu_custom_call" | custom-call | flops 4429185024 | bytes 19398656 | tf_op jit(solution)/shard_map/pallas_call | solution.py:246
  91.0 1.5 %collective-permute-done.22 = bf16[4,32,2048]{2,1,0:T(8,128)(2,1)S(1)} collective-permute-done((bf16[4,32,2048]{2,1,0:T(8,128)(2,1)S(1)}, bf16[4,32,2048]{2,1,0:T(8,128)(2,1)S(1)}, u32[]{:S(2)}, u32[]{:S(2)}) %collective-permute-start.22) | collective-permute-done | bytes 524320 | tf_op jit(solution)/shard_map/ppermute | solution.py:309
  92.7 1.1 collective-permute-start.24
  93.8 1.0 collective-permute-start.26
  94.8 1.4 %collective-permute-start.23 = (bf16[2,32,2048]{2,1,0:T(8,128)(2,1)S(1)}, bf16[2,32,2048]{2,1,0:T(8,128)(2,1)S(1)}, u32[]{:S(2)}, u32[]{:S(2)}) collective-permute-start(bf16[2,32,2048]{2,1,0:T(8,128)(2,1)S(1)} %pad_maximum_fusion), channel_id=1, source_target_pairs={{0,4},{2,6},{4,8},{6,10},{8,12},{10,14},{12,0},{14,2},{1,5},{3,7},... | collective-permute-start | bytes 786440 | tf_op jit(solution)/shard_map/ppermute | solution.py:306
  96.2 2.9 %collective-permute-done.24 = bf16[32,2048]{1,0:T(8,128)(2,1)S(1)} collective-permute-done((bf16[32,2048]{1,0:T(8,128)(2,1)S(1)}, bf16[32,2048]{1,0:T(8,128)(2,1)S(1)}, u32[]{:S(2)}, u32[]{:S(2)}) %collective-permute-start.24) | collective-permute-done | bytes 131104 | tf_op jit(solution)/shard_map/ppermute | solution.py:300
  99.1 2.2 %collective-permute-done.26 = bf16[32,2048]{1,0:T(8,128)(2,1)S(1)} collective-permute-done((bf16[32,2048]{1,0:T(8,128)(2,1)S(1)}, bf16[32,2048]{1,0:T(8,128)(2,1)S(1)}, u32[]{:S(2)}, u32[]{:S(2)}) %collective-permute-start.26) | collective-permute-done | bytes 131104 | tf_op jit(solution)/shard_map/ppermute | solution.py:300
  101.3 3.9 %collective-permute-start.25 = (bf16[32,2048]{1,0:T(8,128)(2,1)S(1)}, bf16[32,2048]{1,0:T(8,128)(2,1)S(1)}, u32[]{:S(2)}, u32[]{:S(2)}) collective-permute-start(bf16[32,2048]{1,0:T(8,128)(2,1)S(1)} %get-tuple-element.61), channel_id=1, source_target_pairs={{0,8},{2,10},{4,12},{6,14},{8,0},{10,2},{12,4},{14,6},{1,9},{3,11}... | collective-permute-start | bytes 393224 | tf_op jit(solution)/shard_map/ppermute | solution.py:306
  105.3 1.1 collective-permute-start.28
  106.4 4.5 %collective-permute-done.25 = bf16[32,2048]{1,0:T(8,128)(2,1)S(1)} collective-permute-done((bf16[32,2048]{1,0:T(8,128)(2,1)S(1)}, bf16[32,2048]{1,0:T(8,128)(2,1)S(1)}, u32[]{:S(2)}, u32[]{:S(2)}) %collective-permute-start.25) | collective-permute-done | bytes 131104 | tf_op jit(solution)/shard_map/ppermute | solution.py:306
  110.9 1.5 %collective-permute-done.27 = bf16[32,2048]{1,0:T(8,128)(2,1)S(1)} collective-permute-done((bf16[32,2048]{1,0:T(8,128)(2,1)S(1)}, bf16[32,2048]{1,0:T(8,128)(2,1)S(1)}, u32[]{:S(2)}, u32[]{:S(2)}) %collective-permute-start.27) | collective-permute-done | bytes 131104 | tf_op jit(solution)/shard_map/ppermute | solution.py:306
  (68 shorter events, 7.8 us)
Async XLA Ops:
  1.8 18.9 %all-to-all-start = ((bf16[8,3,32,256]{3,2,1,0:T(8,128)(2,1)}), bf16[8,3,32,256]{3,2,1,0:T(8,128)(2,1)S(1)}, u32[]{:S(2)}, u32[]{:S(2)}) async-start(bf16[8,3,32,256]{3,2,1,0:T(8,128)(2,1)} %bitcast.83), calls=%async_computation | async-start | bytes 786432 | tf_op jit(solution)/shard_map/all_to_all | solution.py:318
  20.8 13.9 %collective-permute-start = (bf16[128,2048]{1,0:T(8,128)(2,1)S(1)}, bf16[128,2048]{1,0:T(8,128)(2,1)S(1)}, u32[]{:S(2)}, u32[]{:S(2)}) collective-permute-start(bf16[128,2048]{1,0:T(8,128)(2,1)S(1)} %slice_select_fusion), channel_id=1, source_target_pairs={{0,2},{2,0},{4,6},{6,4},{8,10},{10,8},{12,14},{14,12},{1,3},{3,1},... | collective-permute-start | bytes 1572872 | tf_op jit(solution)/shard_map/ppermute | solution.py:300
  34.7 2.0 %collective-permute-start.2 = (bf16[128,2048]{1,0:T(8,128)(2,1)S(1)}, bf16[128,2048]{1,0:T(8,128)(2,1)S(1)}, u32[]{:S(2)}, u32[]{:S(2)}) collective-permute-start(bf16[128,2048]{1,0:T(8,128)(2,1)S(1)} %collective-permute-done), channel_id=1, source_target_pairs={{0,1},{1,0},{2,3},{3,2},{4,5},{5,4},{6,7},{7,6},{8,9},{9,8},{10,11... | collective-permute-start | bytes 1572872 | tf_op jit(solution)/shard_map/ppermute | solution.py:309
  35.4 4.5 %collective-permute-start.1 = (bf16[4,32,256]{2,1,0:T(8,128)(2,1)S(1)}, bf16[4,32,256]{2,1,0:T(8,128)(2,1)S(1)}, u32[]{:S(2)}, u32[]{:S(2)}) collective-permute-start(bf16[4,32,256]{2,1,0:T(8,128)(2,1)S(1)} %get-tuple-element.73), channel_id=1, source_target_pairs={{0,2},{2,0},{4,6},{6,4},{8,10},{10,8},{12,14},{14,12},{1,3},{3,1},... | collective-permute-start | bytes 196616 | tf_op jit(solution)/shard_map/ppermute | solution.py:300
  40.0 16.1 %copy-start.2 = (bf16[32,2048]{1,0:T(8,128)(2,1)S(1)}, bf16[32,2048]{1,0:T(8,128)(2,1)}, u32[]{:S(2)}) copy-start(bf16[32,2048]{1,0:T(8,128)(2,1)} %param.11) | copy-start | bytes 393220
  40.0 16.3 %copy-start.3 = (f32[2048]{0:T(1024)S(1)}, f32[2048]{0:T(1024)}, u32[]{:S(2)}) copy-start(f32[2048]{0:T(1024)} %param.17) | copy-start | bytes 24580
  40.6 8.3 %collective-permute-start.3 = (bf16[32,2048]{1,0:T(8,128)(2,1)S(1)}, bf16[32,2048]{1,0:T(8,128)(2,1)S(1)}, u32[]{:S(2)}, u32[]{:S(2)}) collective-permute-start(bf16[32,2048]{1,0:T(8,128)(2,1)S(1)} %get-tuple-element.70), channel_id=1, source_target_pairs={{0,4},{2,6},{4,8},{6,10},{8,12},{10,14},{12,0},{14,2},{1,5},{3,7},... | collective-permute-start | bytes 393224 | tf_op jit(solution)/shard_map/ppermute | solution.py:306
  42.2 7.6 %collective-permute-start.5 = (bf16[32,2048]{1,0:T(8,128)(2,1)S(1)}, bf16[32,2048]{1,0:T(8,128)(2,1)S(1)}, u32[]{:S(2)}, u32[]{:S(2)}) collective-permute-start(bf16[32,2048]{1,0:T(8,128)(2,1)S(1)} %get-tuple-element.71), channel_id=1, source_target_pairs={{0,12},{2,14},{4,0},{6,2},{8,4},{10,6},{12,8},{14,10},{1,13},{3,15... | collective-permute-start | bytes 393224 | tf_op jit(solution)/shard_map/ppermute | solution.py:306
  44.5 11.5 %collective-permute-start.4 = (bf16[32,2048]{1,0:T(8,128)(2,1)S(1)}, bf16[32,2048]{1,0:T(8,128)(2,1)S(1)}, u32[]{:S(2)}, u32[]{:S(2)}) collective-permute-start(bf16[32,2048]{1,0:T(8,128)(2,1)S(1)} %get-tuple-element.72), channel_id=1, source_target_pairs={{0,8},{2,10},{4,12},{6,14},{8,0},{10,2},{12,4},{14,6},{1,9},{3,11}... | collective-permute-start | bytes 393224 | tf_op jit(solution)/shard_map/ppermute | solution.py:306
  56.4 7.7 %collective-permute-start.9 = (bf16[32,2176]{1,0:T(8,128)(2,1)S(1)}, bf16[32,2176]{1,0:T(8,128)(2,1)S(1)}, u32[]{:S(2)}, u32[]{:S(2)}) collective-permute-start(bf16[32,2176]{1,0:T(8,128)(2,1)S(1)} %fusion.24.refs_0_), channel_id=1, source_target_pairs={{0,12},{2,14},{4,0},{6,2},{8,4},{10,6},{12,8},{14,10},{1,13},{3,15... | collective-permute-start | bytes 417800 | tf_op jit(solution)/shard_map/ppermute | solution.py:306
  57.9 8.3 %collective-permute-start.6 = (bf16[32,2176]{1,0:T(8,128)(2,1)S(1)}, bf16[32,2176]{1,0:T(8,128)(2,1)S(1)}, u32[]{:S(2)}, u32[]{:S(2)}) collective-permute-start(bf16[32,2176]{1,0:T(8,128)(2,1)S(1)} %fusion.24.refs_0_), channel_id=1, source_target_pairs={{0,4},{2,6},{4,8},{6,10},{8,12},{10,14},{12,0},{14,2},{1,5},{3,7},... | collective-permute-start | bytes 417800 | tf_op jit(solution)/shard_map/ppermute | solution.py:306
  58.5 11.9 %collective-permute-start.11 = (bf16[32,2176]{1,0:T(8,128)(2,1)S(1)}, bf16[32,2176]{1,0:T(8,128)(2,1)S(1)}, u32[]{:S(2)}, u32[]{:S(2)}) collective-permute-start(bf16[32,2176]{1,0:T(8,128)(2,1)S(1)} %fusion.24.refs_0_), channel_id=1, source_target_pairs={{0,8},{2,10},{4,12},{6,14},{8,0},{10,2},{12,4},{14,6},{1,9},{3,11}... | collective-permute-start | bytes 417800 | tf_op jit(solution)/shard_map/ppermute | solution.py:306
  58.7 11.7 %collective-permute-start.7 = (bf16[32,2176]{1,0:T(8,128)(2,1)S(1)}, bf16[32,2176]{1,0:T(8,128)(2,1)S(1)}, u32[]{:S(2)}, u32[]{:S(2)}) collective-permute-start(bf16[32,2176]{1,0:T(8,128)(2,1)S(1)} %fusion.24.refs_0_), channel_id=1, source_target_pairs={{0,2},{2,0},{4,6},{6,4},{8,10},{10,8},{12,14},{14,12},{1,3},{3,1},... | collective-permute-start | bytes 417800 | tf_op jit(solution)/shard_map/ppermute | solution.py:300
  64.1 6.7 %collective-permute-start.10 = (bf16[32,2176]{1,0:T(8,128)(2,1)S(1)}, bf16[32,2176]{1,0:T(8,128)(2,1)S(1)}, u32[]{:S(2)}, u32[]{:S(2)}) collective-permute-start(bf16[32,2176]{1,0:T(8,128)(2,1)S(1)} %collective-permute-done.9.refs_3_), channel_id=1, source_target_pairs={{0,2},{2,0},{4,6},{6,4},{8,10},{10,8},{12,14},{14,12},{1,3},{3,1},... | collective-permute-start | bytes 417800 | tf_op jit(solution)/shard_map/ppermute | solution.py:300
  66.1 5.1 %collective-permute-start.8 = (bf16[32,2176]{1,0:T(8,128)(2,1)S(1)}, bf16[32,2176]{1,0:T(8,128)(2,1)S(1)}, u32[]{:S(2)}, u32[]{:S(2)}) collective-permute-start(bf16[32,2176]{1,0:T(8,128)(2,1)S(1)} %collective-permute-done.6.refs_1_), channel_id=1, source_target_pairs={{0,2},{2,0},{4,6},{6,4},{8,10},{10,8},{12,14},{14,12},{1,3},{3,1},... | collective-permute-start | bytes 417800 | tf_op jit(solution)/shard_map/ppermute | solution.py:300
  67.1 5.1 %collective-permute-start.12 = (bf16[32,2176]{1,0:T(8,128)(2,1)S(1)}, bf16[32,2176]{1,0:T(8,128)(2,1)S(1)}, u32[]{:S(2)}, u32[]{:S(2)}) collective-permute-start(bf16[32,2176]{1,0:T(8,128)(2,1)S(1)} %fusion.24.refs_0_), channel_id=1, source_target_pairs={{0,1},{1,0},{2,3},{3,2},{4,5},{5,4},{6,7},{7,6},{8,9},{9,8},{10,11... | collective-permute-start | bytes 417800 | tf_op jit(solution)/shard_map/ppermute | solution.py:309
  70.3 2.1 %collective-permute-start.15 = (bf16[32,2176]{1,0:T(8,128)(2,1)S(1)}, bf16[32,2176]{1,0:T(8,128)(2,1)S(1)}, u32[]{:S(2)}, u32[]{:S(2)}) collective-permute-start(bf16[32,2176]{1,0:T(8,128)(2,1)S(1)} %collective-permute-done.9.refs_3_), channel_id=1, source_target_pairs={{0,1},{1,0},{2,3},{3,2},{4,5},{5,4},{6,7},{7,6},{8,9},{9,8},{10,11... | collective-permute-start | bytes 417800 | tf_op jit(solution)/shard_map/ppermute | solution.py:309
  70.3 2.4 %collective-permute-start.13 = (bf16[32,2176]{1,0:T(8,128)(2,1)S(1)}, bf16[32,2176]{1,0:T(8,128)(2,1)S(1)}, u32[]{:S(2)}, u32[]{:S(2)}) collective-permute-start(bf16[32,2176]{1,0:T(8,128)(2,1)S(1)} %collective-permute-done.6.refs_1_), channel_id=1, source_target_pairs={{0,1},{1,0},{2,3},{3,2},{4,5},{5,4},{6,7},{7,6},{8,9},{9,8},{10,11... | collective-permute-start | bytes 417800 | tf_op jit(solution)/shard_map/ppermute | solution.py:309
  71.2 1.7 %collective-permute-start.14 = (bf16[32,2176]{1,0:T(8,128)(2,1)S(1)}, bf16[32,2176]{1,0:T(8,128)(2,1)S(1)}, u32[]{:S(2)}, u32[]{:S(2)}) collective-permute-start(bf16[32,2176]{1,0:T(8,128)(2,1)S(1)} %collective-permute-done.11.refs_2_), channel_id=1, source_target_pairs={{0,1},{1,0},{2,3},{3,2},{4,5},{5,4},{6,7},{7,6},{8,9},{9,8},{10,11... | collective-permute-start | bytes 417800 | tf_op jit(solution)/shard_map/ppermute | solution.py:309
  71.2 9.8 %collective-permute-start.16 = (bf16[32,2176]{1,0:T(8,128)(2,1)S(1)}, bf16[32,2176]{1,0:T(8,128)(2,1)S(1)}, u32[]{:S(2)}, u32[]{:S(2)}) collective-permute-start(bf16[32,2176]{1,0:T(8,128)(2,1)S(1)} %collective-permute-done.11.refs_2_), channel_id=1, source_target_pairs={{0,2},{2,0},{4,6},{6,4},{8,10},{10,8},{12,14},{14,12},{1,3},{3,1},... | collective-permute-start | bytes 417800 | tf_op jit(solution)/shard_map/ppermute | solution.py:300
  72.2 8.8 %collective-permute-start.17 = (bf16[32,2176]{1,0:T(8,128)(2,1)S(1)}, bf16[32,2176]{1,0:T(8,128)(2,1)S(1)}, u32[]{:S(2)}, u32[]{:S(2)}) collective-permute-start(bf16[32,2176]{1,0:T(8,128)(2,1)S(1)} %collective-permute-done.7.refs_0_), channel_id=1, source_target_pairs={{0,1},{1,0},{2,3},{3,2},{4,5},{5,4},{6,7},{7,6},{8,9},{9,8},{10,11... | collective-permute-start | bytes 417800 | tf_op jit(solution)/shard_map/ppermute | solution.py:309
  72.4 8.6 %collective-permute-start.18 = (bf16[32,2176]{1,0:T(8,128)(2,1)S(1)}, bf16[32,2176]{1,0:T(8,128)(2,1)S(1)}, u32[]{:S(2)}, u32[]{:S(2)}) collective-permute-start(bf16[32,2176]{1,0:T(8,128)(2,1)S(1)} %collective-permute-done.8.refs_1_), channel_id=1, source_target_pairs={{0,1},{1,0},{2,3},{3,2},{4,5},{5,4},{6,7},{7,6},{8,9},{9,8},{10,11... | collective-permute-start | bytes 417800 | tf_op jit(solution)/shard_map/ppermute | solution.py:309
  72.7 8.3 %collective-permute-start.19 = (bf16[32,2176]{1,0:T(8,128)(2,1)S(1)}, bf16[32,2176]{1,0:T(8,128)(2,1)S(1)}, u32[]{:S(2)}, u32[]{:S(2)}) collective-permute-start(bf16[32,2176]{1,0:T(8,128)(2,1)S(1)} %collective-permute-done.10.refs_3_), channel_id=1, source_target_pairs={{0,1},{1,0},{2,3},{3,2},{4,5},{5,4},{6,7},{7,6},{8,9},{9,8},{10,11... | collective-permute-start | bytes 417800 | tf_op jit(solution)/shard_map/ppermute | solution.py:309
  81.0 1.4 %collective-permute-start.20 = (bf16[32,2176]{1,0:T(8,128)(2,1)S(1)}, bf16[32,2176]{1,0:T(8,128)(2,1)S(1)}, u32[]{:S(2)}, u32[]{:S(2)}) collective-permute-start(bf16[32,2176]{1,0:T(8,128)(2,1)S(1)} %collective-permute-done.16.refs_2_), channel_id=1, source_target_pairs={{0,1},{1,0},{2,3},{3,2},{4,5},{5,4},{6,7},{7,6},{8,9},{9,8},{10,11... | collective-permute-start | bytes 417800 | tf_op jit(solution)/shard_map/ppermute | solution.py:309
  81.4 9.1 %collective-permute-start.21 = (bf16[4,32,2048]{2,1,0:T(8,128)(2,1)S(1)}, bf16[4,32,2048]{2,1,0:T(8,128)(2,1)S(1)}, u32[]{:S(2)}, u32[]{:S(2)}) collective-permute-start(bf16[4,32,2048]{2,1,0:T(8,128)(2,1)S(1)} %bitcast.88), channel_id=1, source_target_pairs={{0,1},{1,0},{2,3},{3,2},{4,5},{5,4},{6,7},{7,6},{8,9},{9,8},{10,11... | collective-permute-start | bytes 1572872 | tf_op jit(solution)/shard_map/ppermute | solution.py:309
  90.5 2.0 %collective-permute-start.22 = (bf16[4,32,2048]{2,1,0:T(8,128)(2,1)S(1)}, bf16[4,32,2048]{2,1,0:T(8,128)(2,1)S(1)}, u32[]{:S(2)}, u32[]{:S(2)}) collective-permute-start(bf16[4,32,2048]{2,1,0:T(8,128)(2,1)S(1)} %bitcast.89), channel_id=1, source_target_pairs={{0,1},{1,0},{2,3},{3,2},{4,5},{5,4},{6,7},{7,6},{8,9},{9,8},{10,11... | collective-permute-start | bytes 1572872 | tf_op jit(solution)/shard_map/ppermute | solution.py:309
  92.7 6.4 %collective-permute-start.24 = (bf16[32,2048]{1,0:T(8,128)(2,1)S(1)}, bf16[32,2048]{1,0:T(8,128)(2,1)S(1)}, u32[]{:S(2)}, u32[]{:S(2)}) collective-permute-start(bf16[32,2048]{1,0:T(8,128)(2,1)S(1)} %get-tuple-element.67), channel_id=1, source_target_pairs={{0,2},{2,0},{4,6},{6,4},{8,10},{10,8},{12,14},{14,12},{1,3},{3,1},... | collective-permute-start | bytes 393224 | tf_op jit(solution)/shard_map/ppermute | solution.py:300
  93.8 7.4 %collective-permute-start.26 = (bf16[32,2048]{1,0:T(8,128)(2,1)S(1)}, bf16[32,2048]{1,0:T(8,128)(2,1)S(1)}, u32[]{:S(2)}, u32[]{:S(2)}) collective-permute-start(bf16[32,2048]{1,0:T(8,128)(2,1)S(1)} %get-tuple-element.68), channel_id=1, source_target_pairs={{0,2},{2,0},{4,6},{6,4},{8,10},{10,8},{12,14},{14,12},{1,3},{3,1},... | collective-permute-start | bytes 393224 | tf_op jit(solution)/shard_map/ppermute | solution.py:300
  94.8 10.4 %collective-permute-start.23 = (bf16[2,32,2048]{2,1,0:T(8,128)(2,1)S(1)}, bf16[2,32,2048]{2,1,0:T(8,128)(2,1)S(1)}, u32[]{:S(2)}, u32[]{:S(2)}) collective-permute-start(bf16[2,32,2048]{2,1,0:T(8,128)(2,1)S(1)} %pad_maximum_fusion), channel_id=1, source_target_pairs={{0,4},{2,6},{4,8},{6,10},{8,12},{10,14},{12,0},{14,2},{1,5},{3,7},... | collective-permute-start | bytes 786440 | tf_op jit(solution)/shard_map/ppermute | solution.py:306
  101.3 9.6 %collective-permute-start.25 = (bf16[32,2048]{1,0:T(8,128)(2,1)S(1)}, bf16[32,2048]{1,0:T(8,128)(2,1)S(1)}, u32[]{:S(2)}, u32[]{:S(2)}) collective-permute-start(bf16[32,2048]{1,0:T(8,128)(2,1)S(1)} %get-tuple-element.61), channel_id=1, source_target_pairs={{0,8},{2,10},{4,12},{6,14},{8,0},{10,2},{12,4},{14,6},{1,9},{3,11}... | collective-permute-start | bytes 393224 | tf_op jit(solution)/shard_map/ppermute | solution.py:306
  105.2 7.2 %collective-permute-start.27 = (bf16[32,2048]{1,0:T(8,128)(2,1)S(1)}, bf16[32,2048]{1,0:T(8,128)(2,1)S(1)}, u32[]{:S(2)}, u32[]{:S(2)}) collective-permute-start(bf16[32,2048]{1,0:T(8,128)(2,1)S(1)} %get-tuple-element.62), channel_id=1, source_target_pairs={{0,12},{2,14},{4,0},{6,2},{8,4},{10,6},{12,8},{14,10},{1,13},{3,15... | collective-permute-start | bytes 393224 | tf_op jit(solution)/shard_map/ppermute | solution.py:306
  105.3 7.1 %collective-permute-start.28 = (bf16[32,2048]{1,0:T(8,128)(2,1)S(1)}, bf16[32,2048]{1,0:T(8,128)(2,1)S(1)}, u32[]{:S(2)}, u32[]{:S(2)}) collective-permute-start(bf16[32,2048]{1,0:T(8,128)(2,1)S(1)} %fusion.30), channel_id=1, source_target_pairs={{0,2},{2,0},{4,6},{6,4},{8,10},{10,8},{12,14},{14,12},{1,3},{3,1},... | collective-permute-start | bytes 393224 | tf_op jit(solution)/shard_map/ppermute | solution.py:300
  (4 other events, 35.1 us)
